TPU v7x, 32 devices: a whole 2x2x4 slice. The times are simulated.
32 devices in a mesh: pipe: 2 (over y), row: 4 (over z), col: 4 (over x, core).
Axes of the slice: x: 2, y: 2, z: 4, core: 2. Of those that a mesh axis runs over, the one named last changes fastest.
Arguments:
- tokens: bfloat16 [2, 128, 4096], P('pipe', 'row', 'col'), may hold values from -12 to 12
- norm_gain: float32 [2, 4096], P('pipe', 'col'), may hold values from 0.5 to 2
- gate_weight: bfloat16 [2, 4096, 14336], P('pipe', 'col', 'row'), may hold values from -0.09375 to 0.09375
- up_weight: bfloat16 [2, 4096, 14336], P('pipe', 'col', 'row'), may hold values from -0.09375 to 0.09375
- down_weight: bfloat16 [2, 14336, 4096], P('pipe', ('row', 'col')), may hold values from -0.046875 to 0.046875
Outputs:
- handed: bfloat16 [2, 128, 4096], P('pipe', 'row', 'col')
All inputs are finite; a program needn't handle non-finite values.
Results may differ from a plain program's by a relative error of at most 0.024.
Values may be sent and summed in bfloat16 or wider, within the bound.
No kernel may reach another device: no remote copies, remote signals or barrier semaphores. Data moves between devices by JAX's collectives and lax.ppermute only.
A program may use at most 64 MiB of HBM per device.

v0:
```python
import jax
import jax.numpy as jnp
from jax import lax
from jax.sharding import PartitionSpec as P

D = 4096


EPS = 1e-05


def passed_along(shard, axis, by):
    count = lax.axis_size(axis)
    return lax.ppermute(shard, axis, [(i, (i + by) % count) for i in range(count)])


def local(tokens, norm_gain, gate_weight, up_weight, down_weight):
    inputs = tokens[0]
    gain = norm_gain[0]
    gate_local = gate_weight[0]
    up_local = up_weight[0]
    down_local = down_weight[0]
    widened = inputs.astype(jnp.float32)
    squares = lax.psum(jnp.sum(widened * widened, axis=1), "col")
    inverse = lax.rsqrt(squares / D + EPS)
    normed = (widened * inverse[:, None] * gain[None, :]).astype(jnp.bfloat16)
    piece = lax.all_gather(normed, "row", axis=0, tiled=True)
    partial_sums = jnp.stack(
        [
            jnp.dot(piece, gate_local, preferred_element_type=jnp.float32),
            jnp.dot(piece, up_local, preferred_element_type=jnp.float32),
        ]
    )
    summed = lax.psum_scatter(
        partial_sums.astype(jnp.bfloat16), "col", scatter_dimension=2, tiled=True
    ).astype(jnp.float32)
    gate_value = summed[0]
    up_value = summed[1]
    hidden = (jax.nn.silu(gate_value) * up_value).astype(jnp.bfloat16)
    row_count = lax.axis_size("row")
    col_count = lax.axis_size("col")
    token_total = hidden.shape[0]
    feature_total = down_local.shape[1]
    grouped = hidden.reshape(row_count, token_total // row_count, hidden.shape[1])
    column_split = down_local.reshape(down_local.shape[0], col_count, feature_total // col_count)
    grid_terms = jnp.einsum(
        "rtf,fcd->rctd", grouped, column_split, preferred_element_type=jnp.float32
    )
    grid_terms = grid_terms.reshape(
        row_count * col_count, token_total // row_count, feature_total // col_count
    )
    branch_out = (
        lax.psum_scatter(
            grid_terms.astype(jnp.bfloat16), ("row", "col"), scatter_dimension=0, tiled=True
        )
        .astype(jnp.float32)[0]
        .astype(jnp.bfloat16)
    )
    layer_out = (widened + branch_out.astype(jnp.float32)).astype(jnp.bfloat16)
    handed = passed_along(layer_out, "pipe", 1)
    return handed[None]


def solution(mesh):
    placed = (
        P("pipe", "row", "col"),
        P("pipe", "col"),
        P("pipe", "col", "row"),
        P("pipe", "col", "row"),
        P("pipe", ("row", "col"), None),
    )
    return jax.shard_map(
        local, mesh=mesh, in_specs=placed, out_specs=P("pipe", "row", "col"), check_vma=False
    )
```

profile of v0, /device:TPU:0, one launch (start us, length us, event | category | flops | bytes accessed | tf_op | source)
XLA Modules:
  0.0 155.3 jit_solution(356246399957863881)
XLA Ops:
  6.5 0.0 reduce-scatter.7.cloned.1.call-start
  6.5 1.0 fusion.23
  7.5 8.3 %psum.7 = f32[32]{0:T(128)S(1)} all-reduce(f32[32]{0:T(128)S(1)} %fusion.23), channel_id=1, replica_groups=mesh['pipe'=2,'row'=4,'col'=4] {'col'}, use_global_device_ids=true, to_apply=%region_1.0 | all-reduce | flops 32 | bytes 256 | tf_op jit(solution)/shard_map/psum | solution.py:24
  15.8 0.0 slice-start
  15.8 1.1 fusion.25
  16.9 14.3 %all_gather.3 = bf16[128,1024]{1,0:T(8,128)(2,1)S(1)} all-gather(bf16[32,1024]{1,0:T(8,128)(2,1)S(1)} %fusion.25), channel_id=1, replica_groups=mesh['pipe'=2,'row'=4,'col'=4] {'row'}, dimensions={0}, use_global_device_ids=true | all-gather | bytes 327680 | tf_op jit(solution)/shard_map/all_gather | solution.py:27
  31.2 0.0 slice-start.1
  31.2 4.4 %fusion.13 = bf16[1,128,3584]{2,1,0:T(8,128)(2,1)S(1)} fusion(bf16[128,1024]{1,0:T(8,128)(2,1)S(1)} %all_gather.3, bf16[1,1024,3584]{2,1,0:T(8,128)(2,1)} %param.8), kind=kOutput, calls=%fused_computation.9 | convolution fusion | flops 939982848 | bytes 8519680 | tf_op jit(solution)/shard_map/dot_general | solution.py:31
  35.6 0.0 slice-done
  35.6 0.0 slice-done.1
  35.6 1.1 fusion.16
  36.7 0.2 pad_maximum_fusion
  36.9 3.6 %copy.9 = bf16[2,128,3584]{1,0,2:T(2,128)(2,1)} copy(bf16[2,128,3584]{2,1,0:T(8,128)(2,1)S(1)} %pad_maximum_fusion) | data formatting | bytes 3670016
  40.5 3.1 %copy.19 = bf16[448,8,2,128]{3,1,2,0:T(8,128)(2,1)} copy(bf16[448,8,2,128]{3,2,1,0:T(2,128)(2,1)} %bitcast.53) | data formatting | bytes 3670016
  43.5 0.0 reduce-scatter.7.cloned.1.call-update
  43.6 0.0 reduce-scatter.5.cloned.1.call-start
  43.6 13.0 %reshape_squeeze.3 = bf16[896,4,1024]{2,1,0:T(4,128)(2,1)} reshape(bf16[1,896,4096]{2,1,0:T(8,128)(2,1)} %param.9) | data formatting | bytes 14680064 | tf_op jit(solution)/shard_map/reshape;squeeze | solution.py:45
  56.6 17.5 %reduce-scatter.7.cloned.1.call-done = bf16[896,256]{1,0:T(8,128)(2,1)} async-done(((bf16[3584,256]{1,0:T(8,128)(2,1)}), bf16[896,256]{1,0:T(8,128)(2,1)}) %reduce-scatter.7.cloned.1.call-update) | async-done | bytes 458768
  74.1 1.1 reshape.17
  75.3 0.8 copy.10
  76.1 0.1 convert_element_type.44
  76.1 0.1 fusion.22
  76.3 0.0 copy-start
  76.3 8.7 %fusion.19 = bf16[4,32,4,1024]{3,1,2,0:T(8,128)(2,1)} fusion(bf16[4,32,896,1]{2,1,3,0:T(8,128)(2,1)S(1)} %bitcast.56, bf16[896,4,1024]{2,1,0:T(4,128)(2,1)} %reshape_squeeze.3), kind=kOutput, calls=%fused_computation.13 | convolution fusion | flops 940048384 | bytes 8617984 | tf_op jit(solution)/shard_map/rtf,fcd->rctd/dot_general | solution.py:46
  85.1 0.0 reduce-scatter.5.cloned.1.call-update
  85.1 57.5 %reduce-scatter.5.cloned.1.call-done = bf16[1,32,1024]{2,1,0:T(8,128)(2,1)} async-done(((bf16[16,32,1024]{2,1,0:T(8,128)(2,1)}), bf16[1,32,1024]{2,1,0:T(8,128)(2,1)}) %reduce-scatter.5.cloned.1.call-update) | async-done | bytes 65552 | tf_op jit(solution)/shard_map/reduce_scatter | solution.py:53
  142.6 0.0 copy-done
  142.6 0.9 fusion.26
  143.5 1.5 collective-permute-start
  145.0 2.8 %collective-permute-done = bf16[32,1024]{1,0:T(8,128)(2,1)S(1)} collective-permute-done((bf16[32,1024]{1,0:T(8,128)(2,1)S(1)}, bf16[32,1024]{1,0:T(8,128)(2,1)S(1)}, u32[]{:S(2)}, u32[]{:S(2)}) %collective-permute-start) | collective-permute-done | bytes 65568 | tf_op jit(solution)/shard_map/ppermute | solution.py:14
  147.8 0.6 copy.21
  (2 shorter events, 0.0 us)
Async XLA Ops:
  6.5 67.6 %reduce-scatter.7.cloned.1.call-start = ((), (), s32[]{:S(2)}) async-start(), calls=%async_computation.3 | async-start | bytes 2293760
  15.8 19.7 %slice-start = ((s8[7340032]{0:T(1024)(128)(4,1)}), s8[4194304]{0:T(1024)(128)(4,1)S(1)}, s32[]{:S(2)}) async-start(s8[7340032]{0:T(1024)(128)(4,1)} %bitcast.50), calls=%async_computation.4 | async-start | bytes 8388608
  31.2 4.4 %slice-start.1 = ((s8[7340032]{0:T(1024)(128)(4,1)}), s8[3145728]{0:T(1024)(128)(4,1)S(1)}, s32[]{:S(2)}) async-start(s8[7340032]{0:T(1024)(128)(4,1)} %bitcast.50), calls=%async_computation.5 | async-start | bytes 6291456
  43.6 99.0 %reduce-scatter.5.cloned.1.call-start = ((), (), s32[]{:S(2)}) async-start(), calls=%async_computation.2 | async-start | bytes 1114112 | tf_op jit(solution)/shard_map/reduce_scatter | solution.py:53
  76.3 66.3 %copy-start = (bf16[1,32,1024]{2,1,0:T(8,128)(2,1)S(1)}, bf16[1,32,1024]{2,1,0:T(8,128)(2,1)}, u32[]{:S(2)}) copy-start(bf16[1,32,1024]{2,1,0:T(8,128)(2,1)} %param.5) | copy-start | bytes 196612
  143.5 4.3 %collective-permute-start = (bf16[32,1024]{1,0:T(8,128)(2,1)S(1)}, bf16[32,1024]{1,0:T(8,128)(2,1)S(1)}, u32[]{:S(2)}, u32[]{:S(2)}) collective-permute-start(bf16[32,1024]{1,0:T(8,128)(2,1)S(1)} %fusion.26), channel_id=1, source_target_pairs={{0,16},{16,0},{1,17},{17,1},{2,18},{18,2},{3,19},{19,3},{4,20},{20... | collective-permute-start | bytes 196616 | tf_op jit(solution)/shard_map/ppermute | solution.py:14
Sparse Core Ops, SparseCore 0:
  43.7 30.4 reduce-scatter.6
  85.2 57.3 reduce-scatter.4
where the time goes:
time: 156 us; the launch traced here: 155 us
  waiting for transfers between devices  77.9 us (50%)
  blocking collectives  22.6 us (14%)
  local copies, waits for them, and re-layouts  22.2 us (14%)
  matrix products  14.3 us (9%)
  between operations  13.5 us (9%)
  other arithmetic  3.27 us (2%)
  starting transfers between devices  1.58 us (1%)
    reduce_scatter x1, waiting for transfers between devices, local(): lax.psum_scatter(grid_terms.astype(jnp.bfloat16), ('row', 'col'), scatter...  57.5 us
    unnamed x3, waiting for transfers between devices  17.6 us
    all_gather x1, blocking collectives, local(): piece = lax.all_gather(normed, 'row', axis=0, tiled=True)  14.3 us
    another operation x1, local copies, waits for them, and re-layouts, local(): down_local.reshape(down_local.shape[0], col_count, feature_total // col_c...  13 us
    unnamed x11, local copies, waits for them, and re-layouts  9.18 us
    dot_general x1, matrix products, local(): jnp.einsum('rtf,fcd->rctd', grouped, column_split, preferred_element_type...  8.75 us
    psum x1, blocking collectives, local(): squares = lax.psum(jnp.sum(widened * widened, axis=1), 'col')  8.34 us
    dot_general x1, matrix products, local(): jnp.dot(piece, up_local, preferred_element_type=jnp.float32)  4.37 us
  transfers between devices with their start and end apart: 3, of which 3 were waited for; matrix products, arithmetic and copies ran while one was open for 8% of the time, Pallas kernels for 0%

commit v1 on v0

v1 whole, which is shorter than its diff:
```python
import functools

import jax
import jax.numpy as jnp
from jax import lax
from jax.experimental import pallas as pl
from jax.experimental.pallas import tpu as pltpu
from jax.sharding import PartitionSpec as P

EPS = 1e-05
LANES = 128
F32 = jnp.float32
BF16 = jnp.bfloat16


def flipped(index, mask):
    bit = 1
    while bit <= mask:
        if mask & bit:
            index = index + bit - 2 * bit * ((index // bit) % 2)
        bit *= 2
    return index


def swapped(value, axis, mask):
    count = lax.axis_size(axis)
    return lax.ppermute(value, axis, [(i, i ^ mask) for i in range(count)])


def masks_of(count):
    return [1 << b for b in range(count.bit_length() - 1)]


placed_in = pltpu.with_memory_space_constraint


def call(body, name, operands, outs, scratch=(), cost=None):
    return pl.pallas_call(
        body,
        name=name,
        in_specs=[
            pl.BlockSpec(memory_space=pltpu.VMEM if held else pltpu.HBM) for _, held in operands
        ],
        out_shape=[pltpu.VMEM(shape, dtype) for shape, dtype in outs],
        out_specs=[pl.BlockSpec(memory_space=pltpu.VMEM) for _ in outs],
        scratch_shapes=list(scratch),
        cost_estimate=cost,
        compiler_params=pltpu.CompilerParams(vmem_limit_bytes=16 * 1024 * 1024),
    )(*[placed_in(a, pltpu.VMEM if held else pltpu.HBM) for a, held in operands])


def dot(a, b):
    return jnp.dot(a, b, preferred_element_type=F32)


def load_columns(gate_ref, up_ref, gate_out, up_out, sems):
    count, _, width = gate_out.shape
    mine = lax.axis_index("col")
    copies = []
    for k in reversed(range(count)):
        columns = pl.ds(pl.multiple_of(flipped(mine, k) * width, LANES), width)
        for i, (ref, out) in enumerate(((gate_ref, gate_out), (up_ref, up_out))):
            copies.append(pltpu.make_async_copy(ref.at[0, :, columns], out.at[k], sems.at[k, i]))
    for copy in copies:
        copy.start()
    for copy in copies:
        copy.wait()


def scale_and_first(k, slots, *refs):
    tokens, (gain_ref, gate_ref, up_ref, x_out, s_out, p_out) = refs[:slots], refs[slots:]
    rows = tokens[0].shape[0]
    sums = []
    for i, ref in enumerate(tokens):
        wide = ref[...].astype(F32)
        x_out[pl.ds(i * rows, rows), :] = (wide * gain_ref[...]).astype(BF16)
        sums.append(jnp.sum(wide * wide, axis=1, keepdims=True))
    p_out[0] = dot(x_out[...], gate_ref[k]).astype(p_out.dtype)
    p_out[1] = dot(x_out[...], up_ref[k]).astype(p_out.dtype)
    if slots * rows < LANES:
        sums.append(jnp.zeros((LANES - slots * rows, 1), F32))
    column = jnp.concatenate(sums, axis=0)
    s_out[...] = jnp.transpose(jnp.broadcast_to(column, (LANES, LANES)))[:1]


def product(k, x_ref, gate_ref, up_ref, p_out):
    p_out[0] = dot(x_ref[...], gate_ref[k]).astype(p_out.dtype)
    p_out[1] = dot(x_ref[...], up_ref[k]).astype(p_out.dtype)


def product_and_load(x_ref, gate_ref, up_ref, down_ref, p_out, down_out, sems):
    count, _, width = down_out.shape
    mine = lax.axis_index("col")
    copies = []
    for k in reversed(range(count)):
        columns = pl.ds(pl.multiple_of(flipped(mine, k) * width, LANES), width)
        copies.append(pltpu.make_async_copy(down_ref.at[0, :, columns], down_out.at[k], sems.at[k]))
    for copy in copies:
        copy.start()
    product(0, x_ref, gate_ref, up_ref, p_out)
    for copy in copies:
        copy.wait()


def activate(scale, own_ref, near_ref, far_ref, s_refs, h_out):
    total = sum(s[...] for s in s_refs)
    column = jnp.transpose(jnp.broadcast_to(total, (LANES, LANES)))[: h_out.shape[0], :1]
    inverse = lax.rsqrt(column * scale + EPS)
    gate, up = (
        (own_ref[i] + near_ref[i].astype(F32) + far_ref[i].astype(F32)) * inverse for i in (0, 1)
    )
    h_out[...] = (gate / (1.0 + jnp.exp(-gate)) * up).astype(BF16)


def activate_and_down(scale, blocks, own_ref, near_ref, far_ref, sa, sb, down_ref, h_out, d_out):
    activate(scale, own_ref, near_ref, far_ref, (sa, sb), h_out)
    for i, k in enumerate(blocks):
        d_out[i] = dot(h_out[...], down_ref[k]).astype(BF16)


def down(blocks, h_ref, down_ref, d_out):
    for i, k in enumerate(blocks):
        d_out[i] = dot(h_ref[...], down_ref[k]).astype(BF16)


def added(*values):
    return sum(v.astype(F32) for v in values).astype(BF16)


def fast(tokens, norm_gain, gate_weight, up_weight, down_weight):
    rows, cols, pipes = lax.axis_size("row"), lax.axis_size("col"), lax.axis_size("pipe")
    _, count, depth = tokens.shape
    width = gate_weight.shape[2] // cols
    own = tokens[0]
    forward = [(p, (p + 1) % pipes) for p in range(pipes)]
    handed_tokens = lax.ppermute(own, "pipe", forward)
    slots = [own] + [swapped(own, "row", k) for k in range(1, rows)]
    gates, ups = call(
        load_columns,
        "load_columns",
        [(gate_weight, False), (up_weight, False)],
        [((cols, depth, width), BF16)] * 2,
        [pltpu.SemaphoreType.DMA((cols, 2))],
        pl.CostEstimate(flops=0, transcendentals=0, bytes_accessed=2 * gate_weight.size * 2 * 2),
    )
    m = rows * count
    weights = [(gates, True), (ups, True)]
    x, s, p3 = call(
        functools.partial(scale_and_first, 3, rows),
        "scale_and_first",
        [(slot, True) for slot in slots] + [(norm_gain, True)] + weights,
        [((m, depth), BF16), ((1, LANES), F32), ((2, m, width), BF16)],
    )
    r3 = swapped(p3, "col", 1)
    (p2,) = call(
        functools.partial(product, 2), "product2", [(x, True)] + weights, [((2, m, width), BF16)]
    )
    q2 = added(p2, r3)
    f2 = swapped(q2, "col", 2)
    (p1,) = call(
        functools.partial(product, 1), "product1", [(x, True)] + weights, [((2, m, width), BF16)]
    )
    r1 = swapped(p1, "col", 1)
    p0, downs = call(
        product_and_load,
        "product_and_load",
        [(x, True)] + weights + [(down_weight, False)],
        [((2, m, width), F32), ((cols, width, depth), BF16)],
        [pltpu.SemaphoreType.DMA((cols,))],
    )
    s1 = s + swapped(s, "col", 1)
    s2 = swapped(s1, "col", 2)
    h, e1 = call(
        functools.partial(activate_and_down, 1.0 / (depth * cols), (1, 3)),
        "activate_and_down",
        [(p0, True), (r1, True), (f2, True), (s1, True), (s2, True), (downs, True)],
        [((m, width), BF16), ((2, m, depth), BF16)],
    )
    t1 = swapped(e1, "col", 1)
    (e0,) = call(
        functools.partial(down, (0, 2)), "down", [(h, True), (downs, True)], [((2, m, depth), BF16)]
    )
    u2 = added(e0[1], t1[1])
    v2 = swapped(u2, "col", 2)
    total = added(e0[0], t1[0], v2)
    parts = []
    for k in range(rows):
        pairs = [
            (p * rows + r, forward[p][1] * rows + (r ^ k)) for p in range(pipes) for r in range(rows)
        ]
        parts.append(lax.ppermute(total[k * count : (k + 1) * count], ("pipe", "row"), pairs))
    branch_out = added(*parts)
    return added(handed_tokens, branch_out)[None]


def plain(tokens, norm_gain, gate_weight, up_weight, down_weight):
    rows, cols, pipes = lax.axis_size("row"), lax.axis_size("col"), lax.axis_size("pipe")
    _, count, depth = tokens.shape
    wide = tokens[0].astype(F32)
    squares = lax.psum(jnp.sum(wide * wide, axis=1), "col")
    inverse = lax.rsqrt(squares / (depth * cols) + EPS)
    normed = (wide * inverse[:, None] * norm_gain).astype(BF16)
    piece = lax.all_gather(normed, "row", axis=0, tiled=True)
    sums = jnp.stack([dot(piece, gate_weight[0]), dot(piece, up_weight[0])])
    summed = lax.psum_scatter(sums.astype(BF16), "col", scatter_dimension=2, tiled=True).astype(F32)
    hidden = (jax.nn.silu(summed[0]) * summed[1]).astype(BF16)
    terms = dot(hidden, down_weight[0]).reshape(rows, count, cols, depth).transpose(0, 2, 1, 3)
    terms = terms.reshape(rows * cols, count, depth).astype(BF16)
    branch_out = lax.psum_scatter(terms, ("row", "col"), scatter_dimension=0, tiled=True)[0]
    layer_out = added(tokens[0], branch_out)
    return lax.ppermute(layer_out, "pipe", [(p, (p + 1) % pipes) for p in range(pipes)])[None]


def local(tokens, norm_gain, gate_weight, up_weight, down_weight):
    rows, cols = lax.axis_size("row"), lax.axis_size("col")
    _, count, depth = tokens.shape
    width = gate_weight.shape[2] // cols
    fits = (
        cols == 4
        and rows & (rows - 1) == 0
        and rows * count <= LANES
        and count % 16 == 0
        and depth % LANES == 0
        and width % LANES == 0
    )
    form = fast if fits else plain
    return form(tokens, norm_gain, gate_weight, up_weight, down_weight)


def solution(mesh):
    placed = (
        P("pipe", "row", "col"),
        P("pipe", "col"),
        P("pipe", "col", "row"),
        P("pipe", "col", "row"),
        P("pipe", ("row", "col"), None),
    )
    return jax.shard_map(
        local, mesh=mesh, in_specs=placed, out_specs=P("pipe", "row", "col"), check_vma=False
    )
```

time: 156 us -> 52.9 us (0.34)
  waiting for transfers between devices: 77.9 us -> 20.2 us
  blocking collectives: 22.6 us -> 0 us
  local copies, waits for them, and re-layouts: 22.2 us -> 0.03 us
  starting transfers between devices: 1.58 us -> 18.3 us
  matrix products: 14.3 us -> 0 us
  between operations: 13.5 us -> 0.13 us
  Pallas kernels: 0 us -> 13.1 us
  other arithmetic: 3.27 us -> 0.98 us
    reduce_scatter x1 -> x0, waiting for transfers between devices: 57.5 us -> none  [local(): lax.psum_scatter(grid_terms.astype(jnp.bfloat16), ('row', 'col'), scatter...]
    unnamed x3 -> x0, waiting for transfers between devices: 17.6 us -> none
    ppermute x1 -> x15, waiting for transfers between devices: 2.8 us -> 20.2 us  [the longest x10 14.1 us: swapped(): return lax.ppermute(value, axis, [(i, i ^ mask) for i in range(count)])]
    ppermute x1 -> x15, starting transfers between devices: 1.53 us -> 18.3 us  [the longest x10 9.97 us: swapped(): return lax.ppermute(value, axis, [(i, i ^ mask) for i in range(count)])]
    all_gather x1 -> x0, blocking collectives: 14.3 us -> none  [local(): piece = lax.all_gather(normed, 'row', axis=0, tiled=True)]
    dot_general x3 -> x0, matrix products: 14.3 us -> none  [the longest x1 8.75 us: local(): jnp.einsum('rtf,fcd->rctd', grouped, column_split, preferred_element_type...]
    pallas_call x0 -> x7, Pallas kernels: none -> 13.1 us  [call(): pl.pallas_call(body, name=name, in_specs=[pl.BlockSpec(memory_space=pltpu...]
    another operation x1 -> x0, local copies, waits for them, and re-layouts: 13 us -> none  [local(): down_local.reshape(down_local.shape[0], col_count, feature_total // col_c...]
  transfers between devices with their start and end apart: 3 -> 15, of which waited for: 3 -> 8; matrix products, arithmetic and copies ran while one was open for 8% -> 0% of each run, Pallas kernels for 0% -> 21%
where the time goes in v1:
time: 52.9 us; the launch traced here: 52.8 us
  waiting for transfers between devices  20.2 us (38%)
  starting transfers between devices  18.3 us (35%)
  Pallas kernels  13.1 us (25%)
  other arithmetic  0.98 us (2%)
    ppermute x10, waiting for transfers between devices, swapped(): return lax.ppermute(value, axis, [(i, i ^ mask) for i in range(count)])  14.1 us
    pallas_call x7, Pallas kernels, call(): pl.pallas_call(body, name=name, in_specs=[pl.BlockSpec(memory_space=pltpu...  13.1 us
    ppermute x10, starting transfers between devices, swapped(): return lax.ppermute(value, axis, [(i, i ^ mask) for i in range(count)])  9.97 us
    ppermute x4, starting transfers between devices, fast(): lax.ppermute(total[k * count:(k + 1) * count], ('pipe', 'row'), pairs)  6.81 us
    ppermute x4, waiting for transfers between devices, fast(): lax.ppermute(total[k * count:(k + 1) * count], ('pipe', 'row'), pairs)  6.13 us
    ppermute x1, starting transfers between devices, fast(): handed_tokens = lax.ppermute(own, 'pipe', forward)  1.52 us
  transfers between devices with their start and end apart: 15, of which 8 were waited for; matrix products, arithmetic and copies ran while one was open for 0% of the time, Pallas kernels for 21%

profile of v1, /device:TPU:0, one launch (start us, length us, event | category | flops | bytes accessed | tf_op | source)
XLA Modules:
  0.0 52.8 jit_solution(373664846710560981)
XLA Ops:
  0.0 0.0 copy-start
  0.0 0.0 copy-start.1
  0.0 3.0 %collective-permute-start.1 = (bf16[32,1024]{1,0:T(8,128)(2,1)}, bf16[32,1024]{1,0:T(8,128)(2,1)S(1)}, u32[]{:S(2)}, u32[]{:S(2)}) collective-permute-start(bf16[32,1024]{1,0:T(8,128)(2,1)} %bitcast.9), channel_id=1, source_target_pairs={{0,4},{4,0},{8,12},{12,8},{1,5},{5,1},{9,13},{13,9},{2,6},{6,2},{1... | collective-permute-start | bytes 196616 | tf_op jit(solution)/shard_map/ppermute | solution.py:27
  3.0 2.6 %collective-permute-start.2 = (bf16[32,1024]{1,0:T(8,128)(2,1)}, bf16[32,1024]{1,0:T(8,128)(2,1)S(1)}, u32[]{:S(2)}, u32[]{:S(2)}) collective-permute-start(bf16[32,1024]{1,0:T(8,128)(2,1)} %bitcast.10), channel_id=1, source_target_pairs={{0,8},{4,12},{8,0},{12,4},{1,9},{5,13},{9,1},{13,5},{2,10},{6,14},... | collective-permute-start | bytes 196616 | tf_op jit(solution)/shard_map/ppermute | solution.py:27
  5.6 0.0 collective-permute-start.3
  5.6 5.4 %load_columns.1 = (bf16[4,1024,896]{2,1,0:T(8,128)(2,1)S(1)}, bf16[4,1024,896]{2,1,0:T(8,128)(2,1)S(1)}) custom-call(bf16[1,1024,3584]{2,1,0:T(8,128)(2,1)} %gate_ref.1, bf16[1,1024,3584]{2,1,0:T(8,128)(2,1)} %up_ref.1), custom_call_target="tpu_custom_call" | custom-call | bytes 29360128 | tf_op jit(solution)/shard_map/load_columns/pallas_call | solution.py:38
  11.0 0.0 collective-permute-done.1.refs_1_
  11.0 0.0 collective-permute-done.2.refs_2_
  11.0 0.9 %collective-permute-done.3.refs_3_ = bf16[32,1024]{1,0:T(8,128)(2,1)S(1)} collective-permute-done((bf16[32,1024]{1,0:T(8,128)(2,1)}, bf16[32,1024]{1,0:T(8,128)(2,1)S(1)}, u32[]{:S(2)}, u32[]{:S(2)}) %collective-permute-start.3) | collective-permute-done | bytes 65568 | tf_op jit(solution)/shard_map/ppermute | solution.py:27
  11.9 0.0 copy-done
  11.9 0.0 copy-done.1
  11.9 0.7 %scale_and_first.1 = (bf16[128,1024]{1,0:T(8,128)(2,1)S(1)}, f32[1,128]{1,0:T(1,128)S(1)}, bf16[2,128,896]{2,1,0:T(8,128)(2,1)S(1)}) custom-call(bf16[32,1024]{1,0:T(8,128)(2,1)S(1)} %bitcast.12, bf16[32,1024]{1,0:T(8,128)(2,1)S(1)} %collective-permute-done.1.refs_1_, bf16[32,1024]{1,0:T(8,128)(2,1)S(1)} %collective-permute-done.2.refs_2_, ...), custom_call_target="tpu_custom_call" | custom-call | tf_op jit(solution)/shard_map/scale_and_first/pallas_call | solution.py:38
  12.7 0.1 collective-permute-start.5
  12.8 0.7 %product2.1 = bf16[2,128,896]{2,1,0:T(8,128)(2,1)S(1)} custom-call(bf16[128,1024]{1,0:T(8,128)(2,1)S(1)} %get-tuple-element.16.x_ref, bf16[4,1024,896]{2,1,0:T(8,128)(2,1)S(1)} %get-tuple-element.14.refs_5_.gate_ref, bf16[4,1024,896]{2,1,0:T(8,128)(2,1)S(1)} %get-tuple-element.15.refs_6_.up_ref), custom_call_target="tpu_custom_call" | custom-call | tf_op jit(solution)/shard_map/product2/pallas_call | solution.py:38
  13.5 0.7 %product1.1 = bf16[2,128,896]{2,1,0:T(8,128)(2,1)S(1)} custom-call(bf16[128,1024]{1,0:T(8,128)(2,1)S(1)} %get-tuple-element.16.x_ref, bf16[4,1024,896]{2,1,0:T(8,128)(2,1)S(1)} %get-tuple-element.14.refs_5_.gate_ref, bf16[4,1024,896]{2,1,0:T(8,128)(2,1)S(1)} %get-tuple-element.15.refs_6_.up_ref), custom_call_target="tpu_custom_call" | custom-call | tf_op jit(solution)/shard_map/product1/pallas_call | solution.py:38
  14.2 0.6 %collective-permute-start.4 = (bf16[2,128,896]{2,1,0:T(8,128)(2,1)S(1)}, bf16[2,128,896]{2,1,0:T(8,128)(2,1)S(1)}, u32[]{:S(2)}, u32[]{:S(2)}) collective-permute-start(bf16[2,128,896]{2,1,0:T(8,128)(2,1)S(1)} %product1.1), channel_id=1, source_target_pairs={{0,1},{1,0},{2,3},{3,2},{4,5},{5,4},{6,7},{7,6},{8,9},{9,8},{10,11... | collective-permute-start | bytes 1376264 | tf_op jit(solution)/shard_map/ppermute | solution.py:27
  14.8 0.0 collective-permute-done.5
  14.8 0.1 add_convert_fusion
  14.9 1.6 %collective-permute-start.6 = (bf16[2,128,896]{2,1,0:T(8,128)(2,1)S(1)}, bf16[2,128,896]{2,1,0:T(8,128)(2,1)S(1)}, u32[]{:S(2)}, u32[]{:S(2)}) collective-permute-start(bf16[2,128,896]{2,1,0:T(8,128)(2,1)S(1)} %add_convert_fusion), channel_id=1, source_target_pairs={{0,2},{1,3},{2,0},{3,1},{4,6},{5,7},{6,4},{7,5},{8,10},{9,11},{10,... | collective-permute-start | bytes 1376264 | tf_op jit(solution)/shard_map/ppermute | solution.py:27
  16.4 0.0 collective-permute-start.7
  16.4 1.1 %collective-permute-done.7 = f32[1,128]{1,0:T(1,128)S(1)} collective-permute-done((f32[1,128]{1,0:T(1,128)S(1)}, f32[1,128]{1,0:T(1,128)S(1)}, u32[]{:S(2)}, u32[]{:S(2)}) %collective-permute-start.7) | collective-permute-done | bytes 544 | tf_op jit(solution)/shard_map/ppermute | solution.py:27
  17.6 0.5 %collective-permute-start.8 = (f32[1,128]{1,0:T(1,128)S(1)}, f32[1,128]{1,0:T(1,128)S(1)}, u32[]{:S(2)}, u32[]{:S(2)}) collective-permute-start(f32[1,128]{1,0:T(1,128)S(1)} %add.32.sa), channel_id=1, source_target_pairs={{0,2},{1,3},{2,0},{3,1},{4,6},{5,7},{6,4},{7,5},{8,10},{9,11},{10,... | collective-permute-start | bytes 1544 | tf_op jit(solution)/shard_map/ppermute | solution.py:27
  18.1 3.8 %product_and_load.1 = (f32[2,128,896]{2,1,0:T(8,128)S(1)}, bf16[4,896,1024]{2,1,0:T(8,128)(2,1)S(1)}) custom-call(bf16[128,1024]{1,0:T(8,128)(2,1)S(1)} %get-tuple-element.16.x_ref, bf16[4,1024,896]{2,1,0:T(8,128)(2,1)S(1)} %get-tuple-element.14.refs_5_.gate_ref, bf16[4,1024,896]{2,1,0:T(8,128)(2,1)S(1)} %get-tuple-element.15.refs_6_.up_ref, ...), custom_call_target="tpu_custom_call" | custom-call | tf_op jit(solution)/shard_map/product_and_load/pallas_call | solution.py:38
  21.9 5.6 %collective-permute-done.8.sb = f32[1,128]{1,0:T(1,128)S(1)} collective-permute-done((f32[1,128]{1,0:T(1,128)S(1)}, f32[1,128]{1,0:T(1,128)S(1)}, u32[]{:S(2)}, u32[]{:S(2)}) %collective-permute-start.8) | collective-permute-done | bytes 544 | tf_op jit(solution)/shard_map/ppermute | solution.py:27
  27.5 0.0 collective-permute-done.4.near_ref
  27.5 0.0 collective-permute-done.6.far_ref
  27.5 1.0 %activate_and_down.1 = (bf16[128,896]{1,0:T(8,128)(2,1)S(1)}, bf16[2,128,1024]{2,1,0:T(8,128)(2,1)S(1)}) custom-call(f32[2,128,896]{2,1,0:T(8,128)S(1)} %get-tuple-element.17.own_ref, bf16[2,128,896]{2,1,0:T(8,128)(2,1)S(1)} %collective-permute-done.4.near_ref, bf16[2,128,896]{2,1,0:T(8,128)(2,1)S(1)} %collective-permute-done.6.far_ref, ...), custom_call_target="tpu_custom_call" | custom-call | tf_op jit(solution)/shard_map/activate_and_down/pallas_call | solution.py:38
  28.5 0.1 collective-permute-start.9
  28.6 0.7 %down.1 = bf16[2,128,1024]{2,1,0:T(8,128)(2,1)S(1)} custom-call(bf16[128,896]{1,0:T(8,128)(2,1)S(1)} %get-tuple-element.21.h_ref, bf16[4,896,1024]{2,1,0:T(8,128)(2,1)S(1)} %get-tuple-element.20.down_ref), custom_call_target="tpu_custom_call" | custom-call | tf_op jit(solution)/shard_map/down/pallas_call | solution.py:38
  29.3 1.2 %collective-permute-done.9 = bf16[2,128,1024]{2,1,0:T(8,128)(2,1)S(1)} collective-permute-done((bf16[2,128,1024]{2,1,0:T(8,128)(2,1)S(1)}, bf16[2,128,1024]{2,1,0:T(8,128)(2,1)S(1)}, u32[]{:S(2)}, u32[]{:S(2)}) %collective-permute-start.9) | collective-permute-done | bytes 524320 | tf_op jit(solution)/shard_map/ppermute | solution.py:27
  30.5 0.1 fusion.1
  30.6 1.6 %collective-permute-start.10 = (bf16[128,1024]{1,0:T(8,128)(2,1)S(1)}, bf16[128,1024]{1,0:T(8,128)(2,1)S(1)}, u32[]{:S(2)}, u32[]{:S(2)}) collective-permute-start(bf16[128,1024]{1,0:T(8,128)(2,1)S(1)} %fusion.1), channel_id=1, source_target_pairs={{0,2},{1,3},{2,0},{3,1},{4,6},{5,7},{6,4},{7,5},{8,10},{9,11},{10,... | collective-permute-start | bytes 786440 | tf_op jit(solution)/shard_map/ppermute | solution.py:27
  32.1 1.5 %collective-permute-start = (bf16[32,1024]{1,0:T(8,128)(2,1)S(1)}, bf16[32,1024]{1,0:T(8,128)(2,1)S(1)}, u32[]{:S(2)}, u32[]{:S(2)}) collective-permute-start(bf16[32,1024]{1,0:T(8,128)(2,1)S(1)} %bitcast.13), channel_id=1, source_target_pairs={{0,16},{16,0},{1,17},{17,1},{2,18},{18,2},{3,19},{19,3},{4,20},{20... | collective-permute-start | bytes 196616 | tf_op jit(solution)/shard_map/ppermute | solution.py:136
  33.6 5.3 %collective-permute-done.10 = bf16[128,1024]{1,0:T(8,128)(2,1)S(1)} collective-permute-done((bf16[128,1024]{1,0:T(8,128)(2,1)S(1)}, bf16[128,1024]{1,0:T(8,128)(2,1)S(1)}, u32[]{:S(2)}, u32[]{:S(2)}) %collective-permute-start.10) | collective-permute-done | bytes 262176 | tf_op jit(solution)/shard_map/ppermute | solution.py:27
  39.0 0.1 fusion
  39.1 1.6 %collective-permute-start.11 = (bf16[32,1024]{1,0:T(8,128)(2,1)S(1)}, bf16[32,1024]{1,0:T(8,128)(2,1)S(1)}, u32[]{:S(2)}, u32[]{:S(2)}) collective-permute-start(bf16[32,1024]{1,0:T(8,128)(2,1)S(1)} %get-tuple-element.23), channel_id=1, source_target_pairs={{0,16},{4,20},{8,24},{12,28},{16,0},{20,4},{24,8},{28,12},{1,17},{... | collective-permute-start | bytes 196616 | tf_op jit(solution)/shard_map/ppermute | solution.py:191
  40.7 0.0 collective-permute-start.12
  40.7 4.4 %collective-permute-start.13 = (bf16[32,1024]{1,0:T(8,128)(2,1)S(1)}, bf16[32,1024]{1,0:T(8,128)(2,1)S(1)}, u32[]{:S(2)}, u32[]{:S(2)}) collective-permute-start(bf16[32,1024]{1,0:T(8,128)(2,1)S(1)} %get-tuple-element.25), channel_id=1, source_target_pairs={{0,24},{4,28},{8,16},{12,20},{16,8},{20,12},{24,0},{28,4},{1,25},{... | collective-permute-start | bytes 196616 | tf_op jit(solution)/shard_map/ppermute | solution.py:191
  45.1 0.8 %collective-permute-start.14 = (bf16[32,1024]{1,0:T(8,128)(2,1)S(1)}, bf16[32,1024]{1,0:T(8,128)(2,1)S(1)}, u32[]{:S(2)}, u32[]{:S(2)}) collective-permute-start(bf16[32,1024]{1,0:T(8,128)(2,1)S(1)} %get-tuple-element.24), channel_id=1, source_target_pairs={{0,28},{4,24},{8,20},{12,16},{16,12},{20,8},{24,4},{28,0},{1,29},{... | collective-permute-start | bytes 196616 | tf_op jit(solution)/shard_map/ppermute | solution.py:191
  45.9 0.0 collective-permute-done
  46.0 0.0 collective-permute-done.11
  46.0 0.1 collective-permute-done.12
  46.1 2.6 %collective-permute-done.13 = bf16[32,1024]{1,0:T(8,128)(2,1)S(1)} collective-permute-done((bf16[32,1024]{1,0:T(8,128)(2,1)S(1)}, bf16[32,1024]{1,0:T(8,128)(2,1)S(1)}, u32[]{:S(2)}, u32[]{:S(2)}) %collective-permute-start.13) | collective-permute-done | bytes 65568 | tf_op jit(solution)/shard_map/ppermute | solution.py:191
  48.7 3.4 %collective-permute-done.14 = bf16[32,1024]{1,0:T(8,128)(2,1)S(1)} collective-permute-done((bf16[32,1024]{1,0:T(8,128)(2,1)S(1)}, bf16[32,1024]{1,0:T(8,128)(2,1)S(1)}, u32[]{:S(2)}, u32[]{:S(2)}) %collective-permute-start.14) | collective-permute-done | bytes 65568 | tf_op jit(solution)/shard_map/ppermute | solution.py:191
  52.1 0.7 %fusion.2 = bf16[1,32,1024]{2,1,0:T(8,128)(2,1)} fusion(bf16[32,1024]{1,0:T(8,128)(2,1)S(1)} %collective-permute-done.14, bf16[32,1024]{1,0:T(8,128)(2,1)S(1)} %collective-permute-done.13, bf16[32,1024]{1,0:T(8,128)(2,1)S(1)} %collective-permute-done.12, bf16[32,1024]{1,0:T(8,128)(2,1)S(1)} %collective-permute-done.11, ...), kind=kLoop, calls=%fused_computation.7 | loop fusion | flops 393216 | bytes 393216 | tf_op jit(solution)/shard_map/broadcast_in_dim | solution.py:193
  (2 shorter events, 0.0 us)
Async XLA Ops:
  0.0 11.9 %copy-start = (bf16[1,32,1024]{2,1,0:T(8,128)(2,1)S(1)}, bf16[1,32,1024]{2,1,0:T(8,128)(2,1)}, u32[]{:S(2)}) copy-start(bf16[1,32,1024]{2,1,0:T(8,128)(2,1)} %param.5) | copy-start | bytes 196612
  0.0 11.9 %copy-start.1 = (f32[1,1024]{1,0:T(1,128)S(1)}, f32[1,1024]{1,0:T(1,128)}, u32[]{:S(2)}) copy-start(f32[1,1024]{1,0:T(1,128)} %refs_4_.1) | copy-start | bytes 12292
  0.0 11.0 %collective-permute-start.1 = (bf16[32,1024]{1,0:T(8,128)(2,1)}, bf16[32,1024]{1,0:T(8,128)(2,1)S(1)}, u32[]{:S(2)}, u32[]{:S(2)}) collective-permute-start(bf16[32,1024]{1,0:T(8,128)(2,1)} %bitcast.9), channel_id=1, source_target_pairs={{0,4},{4,0},{8,12},{12,8},{1,5},{5,1},{9,13},{13,9},{2,6},{6,2},{1... | collective-permute-start | bytes 196616 | tf_op jit(solution)/shard_map/ppermute | solution.py:27
  3.0 8.0 %collective-permute-start.2 = (bf16[32,1024]{1,0:T(8,128)(2,1)}, bf16[32,1024]{1,0:T(8,128)(2,1)S(1)}, u32[]{:S(2)}, u32[]{:S(2)}) collective-permute-start(bf16[32,1024]{1,0:T(8,128)(2,1)} %bitcast.10), channel_id=1, source_target_pairs={{0,8},{4,12},{8,0},{12,4},{1,9},{5,13},{9,1},{13,5},{2,10},{6,14},... | collective-permute-start | bytes 196616 | tf_op jit(solution)/shard_map/ppermute | solution.py:27
  5.6 6.3 %collective-permute-start.3 = (bf16[32,1024]{1,0:T(8,128)(2,1)}, bf16[32,1024]{1,0:T(8,128)(2,1)S(1)}, u32[]{:S(2)}, u32[]{:S(2)}) collective-permute-start(bf16[32,1024]{1,0:T(8,128)(2,1)} %bitcast.11), channel_id=1, source_target_pairs={{0,12},{4,8},{8,4},{12,0},{1,13},{5,9},{9,5},{13,1},{2,14},{6,10},... | collective-permute-start | bytes 196616 | tf_op jit(solution)/shard_map/ppermute | solution.py:27
  12.7 2.1 %collective-permute-start.5 = (bf16[2,128,896]{2,1,0:T(8,128)(2,1)S(1)}, bf16[2,128,896]{2,1,0:T(8,128)(2,1)S(1)}, u32[]{:S(2)}, u32[]{:S(2)}) collective-permute-start(bf16[2,128,896]{2,1,0:T(8,128)(2,1)S(1)} %get-tuple-element.18), channel_id=1, source_target_pairs={{0,1},{1,0},{2,3},{3,2},{4,5},{5,4},{6,7},{7,6},{8,9},{9,8},{10,11... | collective-permute-start | bytes 1376264 | tf_op jit(solution)/shard_map/ppermute | solution.py:27
  14.2 13.3 %collective-permute-start.4 = (bf16[2,128,896]{2,1,0:T(8,128)(2,1)S(1)}, bf16[2,128,896]{2,1,0:T(8,128)(2,1)S(1)}, u32[]{:S(2)}, u32[]{:S(2)}) collective-permute-start(bf16[2,128,896]{2,1,0:T(8,128)(2,1)S(1)} %product1.1), channel_id=1, source_target_pairs={{0,1},{1,0},{2,3},{3,2},{4,5},{5,4},{6,7},{7,6},{8,9},{9,8},{10,11... | collective-permute-start | bytes 1376264 | tf_op jit(solution)/shard_map/ppermute | solution.py:27
  14.9 12.6 %collective-permute-start.6 = (bf16[2,128,896]{2,1,0:T(8,128)(2,1)S(1)}, bf16[2,128,896]{2,1,0:T(8,128)(2,1)S(1)}, u32[]{:S(2)}, u32[]{:S(2)}) collective-permute-start(bf16[2,128,896]{2,1,0:T(8,128)(2,1)S(1)} %add_convert_fusion), channel_id=1, source_target_pairs={{0,2},{1,3},{2,0},{3,1},{4,6},{5,7},{6,4},{7,5},{8,10},{9,11},{10,... | collective-permute-start | bytes 1376264 | tf_op jit(solution)/shard_map/ppermute | solution.py:27
  16.4 1.1 %collective-permute-start.7 = (f32[1,128]{1,0:T(1,128)S(1)}, f32[1,128]{1,0:T(1,128)S(1)}, u32[]{:S(2)}, u32[]{:S(2)}) collective-permute-start(f32[1,128]{1,0:T(1,128)S(1)} %get-tuple-element.19), channel_id=1, source_target_pairs={{0,1},{1,0},{2,3},{3,2},{4,5},{5,4},{6,7},{7,6},{8,9},{9,8},{10,11... | collective-permute-start | bytes 1544 | tf_op jit(solution)/shard_map/ppermute | solution.py:27
  17.6 9.9 %collective-permute-start.8 = (f32[1,128]{1,0:T(1,128)S(1)}, f32[1,128]{1,0:T(1,128)S(1)}, u32[]{:S(2)}, u32[]{:S(2)}) collective-permute-start(f32[1,128]{1,0:T(1,128)S(1)} %add.32.sa), channel_id=1, source_target_pairs={{0,2},{1,3},{2,0},{3,1},{4,6},{5,7},{6,4},{7,5},{8,10},{9,11},{10,... | collective-permute-start | bytes 1544 | tf_op jit(solution)/shard_map/ppermute | solution.py:27
  28.5 2.0 %collective-permute-start.9 = (bf16[2,128,1024]{2,1,0:T(8,128)(2,1)S(1)}, bf16[2,128,1024]{2,1,0:T(8,128)(2,1)S(1)}, u32[]{:S(2)}, u32[]{:S(2)}) collective-permute-start(bf16[2,128,1024]{2,1,0:T(8,128)(2,1)S(1)} %get-tuple-element.22), channel_id=1, source_target_pairs={{0,1},{1,0},{2,3},{3,2},{4,5},{5,4},{6,7},{7,6},{8,9},{9,8},{10,11... | collective-permute-start | bytes 1572872 | tf_op jit(solution)/shard_map/ppermute | solution.py:27
  30.6 8.4 %collective-permute-start.10 = (bf16[128,1024]{1,0:T(8,128)(2,1)S(1)}, bf16[128,1024]{1,0:T(8,128)(2,1)S(1)}, u32[]{:S(2)}, u32[]{:S(2)}) collective-permute-start(bf16[128,1024]{1,0:T(8,128)(2,1)S(1)} %fusion.1), channel_id=1, source_target_pairs={{0,2},{1,3},{2,0},{3,1},{4,6},{5,7},{6,4},{7,5},{8,10},{9,11},{10,... | collective-permute-start | bytes 786440 | tf_op jit(solution)/shard_map/ppermute | solution.py:27
  32.1 13.8 %collective-permute-start = (bf16[32,1024]{1,0:T(8,128)(2,1)S(1)}, bf16[32,1024]{1,0:T(8,128)(2,1)S(1)}, u32[]{:S(2)}, u32[]{:S(2)}) collective-permute-start(bf16[32,1024]{1,0:T(8,128)(2,1)S(1)} %bitcast.13), channel_id=1, source_target_pairs={{0,16},{16,0},{1,17},{17,1},{2,18},{18,2},{3,19},{19,3},{4,20},{20... | collective-permute-start | bytes 196616 | tf_op jit(solution)/shard_map/ppermute | solution.py:136
  39.1 6.8 %collective-permute-start.11 = (bf16[32,1024]{1,0:T(8,128)(2,1)S(1)}, bf16[32,1024]{1,0:T(8,128)(2,1)S(1)}, u32[]{:S(2)}, u32[]{:S(2)}) collective-permute-start(bf16[32,1024]{1,0:T(8,128)(2,1)S(1)} %get-tuple-element.23), channel_id=1, source_target_pairs={{0,16},{4,20},{8,24},{12,28},{16,0},{20,4},{24,8},{28,12},{1,17},{... | collective-permute-start | bytes 196616 | tf_op jit(solution)/shard_map/ppermute | solution.py:191
  40.7 5.4 %collective-permute-start.12 = (bf16[32,1024]{1,0:T(8,128)(2,1)S(1)}, bf16[32,1024]{1,0:T(8,128)(2,1)S(1)}, u32[]{:S(2)}, u32[]{:S(2)}) collective-permute-start(bf16[32,1024]{1,0:T(8,128)(2,1)S(1)} %get-tuple-element.26), channel_id=1, source_target_pairs={{0,20},{4,16},{8,28},{12,24},{16,4},{20,0},{24,12},{28,8},{1,21},{... | collective-permute-start | bytes 196616 | tf_op jit(solution)/shard_map/ppermute | solution.py:191
  40.7 8.0 %collective-permute-start.13 = (bf16[32,1024]{1,0:T(8,128)(2,1)S(1)}, bf16[32,1024]{1,0:T(8,128)(2,1)S(1)}, u32[]{:S(2)}, u32[]{:S(2)}) collective-permute-start(bf16[32,1024]{1,0:T(8,128)(2,1)S(1)} %get-tuple-element.25), channel_id=1, source_target_pairs={{0,24},{4,28},{8,16},{12,20},{16,8},{20,12},{24,0},{28,4},{1,25},{... | collective-permute-start | bytes 196616 | tf_op jit(solution)/shard_map/ppermute | solution.py:191
  45.1 7.0 %collective-permute-start.14 = (bf16[32,1024]{1,0:T(8,128)(2,1)S(1)}, bf16[32,1024]{1,0:T(8,128)(2,1)S(1)}, u32[]{:S(2)}, u32[]{:S(2)}) collective-permute-start(bf16[32,1024]{1,0:T(8,128)(2,1)S(1)} %get-tuple-element.24), channel_id=1, source_target_pairs={{0,28},{4,24},{8,20},{12,16},{16,12},{20,8},{24,4},{28,0},{1,29},{... | collective-permute-start | bytes 196616 | tf_op jit(solution)/shard_map/ppermute | solution.py:191

commit v2 on v1

v2 whole, which is shorter than its diff:
```python
import functools

import jax
import jax.numpy as jnp
from jax import lax
from jax.experimental import pallas as pl
from jax.experimental.pallas import tpu as pltpu
from jax.sharding import PartitionSpec as P

EPS = 1e-05
LANES = 128
F32 = jnp.float32
BF16 = jnp.bfloat16


def flipped(index, mask):
    bit = 1
    while bit <= mask:
        if mask & bit:
            index = index + bit - 2 * bit * ((index // bit) % 2)
        bit *= 2
    return index


def swapped(value, axis, mask):
    count = lax.axis_size(axis)
    return lax.ppermute(value, axis, [(i, i ^ mask) for i in range(count)])


def masks_of(count):
    return [1 << b for b in range(count.bit_length() - 1)]


placed_in = pltpu.with_memory_space_constraint


COST = {'load': 62262000000, 'first': 8762800000, 'product2': 0, 'product1': 0, 'product0': 42661000000, 'joined': 2075399999, 'activate_far': 9915800000, 'down_far': 8878100000, 'activate_near': 0, 'down_near': 0}


def call(body, name, outs, held, streamed=(), after=(), copies=0, cost=0):
    fixed = len(held) + len(streamed)

    def run(*refs):
        body(*refs[:fixed], *refs[fixed + len(after) :])

    spaces = [pltpu.VMEM] * len(held) + [pltpu.HBM] * len(streamed)
    return pl.pallas_call(
        run,
        name=name,
        in_specs=[pl.BlockSpec(memory_space=s) for s in spaces]
        + [pl.BlockSpec(memory_space=pl.ANY)] * len(after),
        out_shape=[pltpu.VMEM(shape, dtype) for shape, dtype in outs],
        out_specs=[pl.BlockSpec(memory_space=pltpu.VMEM)] * len(outs),
        scratch_shapes=[pltpu.SemaphoreType.DMA((copies,))] if copies else [],
        cost_estimate=pl.CostEstimate(flops=COST[name], transcendentals=0, bytes_accessed=0),
        compiler_params=pltpu.CompilerParams(vmem_limit_bytes=16 * 1024 * 1024),
    )(*[placed_in(a, s) for a, s in zip([*held, *streamed], spaces)], *after)


def dot(a, b):
    return jnp.dot(a, b, preferred_element_type=F32)


def copies_of(pairs, sems):
    copies = []
    for k in reversed(range(pairs[0][1].shape[0])):
        for source, held in pairs:
            width = held.shape[2]
            columns = pl.ds(pl.multiple_of(flipped(lax.axis_index("col"), k) * width, LANES), width)
            copy = pltpu.make_async_copy(
                source.at[0, :, columns], held.at[k], sems.at[len(copies)]
            )
            copy.start()
            copies.append(copy)
    return copies


def load(gate_ref, up_ref, gate_out, up_out, sems):
    for copy in copies_of([(gate_ref, gate_out), (up_ref, up_out)], sems):
        copy.wait()


def in_terms(column):
    lane = lax.broadcasted_iota(jnp.int32, (column.shape[0], LANES), 1)
    terms = jnp.zeros(lane.shape, F32)
    for i in range(3):
        part = column.astype(BF16).astype(F32)
        terms = jnp.where(lane == i, part, terms)
        column = column - part
    return terms.astype(BF16)


def from_terms(tile):
    return jnp.sum(tile.astype(F32), axis=1, keepdims=True)


def products(k, x_ref, gate_ref, up_ref, outs):
    width = gate_ref.shape[2]
    for i, ref in enumerate((gate_ref, up_ref)):
        both = dot(x_ref[...], ref[k])
        row = 0
        for out in outs:
            here = slice(row, row + out.shape[0])
            out[:, i * width : (i + 1) * width] = both[here].astype(out.dtype)
            row += out.shape[0]


def scale_and_first(k, *refs):
    *tokens, gain_ref, gate_ref, up_ref, x_out, s_out, a_out, b_out = refs
    rows = tokens[0].shape[0]
    for i, ref in enumerate(tokens):
        wide = ref[...].astype(F32)
        here = slice(i * rows, (i + 1) * rows)
        x_out[here, :] = (wide * gain_ref[...]).astype(BF16)
        s_out[here, :] = in_terms(jnp.sum(wide * wide, axis=1, keepdims=True))
    products(k, x_out, gate_ref, up_ref, (a_out, b_out))
    m, start = a_out.shape[0], a_out.shape[1] - LANES
    a_out[:, start:] = s_out[:m, :]
    b_out[:, start:] = s_out[m:, :]


def product(k, x_ref, gate_ref, up_ref, out):
    products(k, x_ref, gate_ref, up_ref, (out,))


def product_and_load(k, x_ref, gate_ref, up_ref, down_ref, out, down_out, sems):
    copies = copies_of([(down_ref, down_out)], sems)
    products(k, x_ref, gate_ref, up_ref, (out,))
    for copy in copies:
        copy.wait()


def joined(first, p_ref, s_ref, r_ref, out):
    count, width = out.shape[0], p_ref.shape[1]
    here = slice(first, first + count)
    out[:, :width] = (p_ref[here, :].astype(F32) + r_ref[:, :width].astype(F32)).astype(BF16)
    out[:, width:] = in_terms(from_terms(s_ref[here, :]) + from_terms(r_ref[:, width:]))


def joined_and_own(first, p_ref, s_ref, r_ref, own_ref, out, own_out):
    own_out[...] = own_ref[...]
    joined(first, p_ref, s_ref, r_ref, out)


def activate_and_down(first, factor, blocks, p_ref, near_ref, s_ref, far_ref, sib_ref, down_ref, h_out, d_out):
    count, width = h_out.shape
    here = slice(first, first + count)
    tail = slice(2 * width, 2 * width + LANES)
    tiles = (s_ref[here, :], sib_ref[:, tail], far_ref[:, tail])
    inverse = lax.rsqrt(sum(from_terms(tile) for tile in tiles) * factor + EPS)
    gate, up = (
        (p_ref[here, at] + near_ref[here, at].astype(F32) + far_ref[:, at].astype(F32)) * inverse
        for at in (slice(0, width), slice(width, 2 * width))
    )
    h_out[...] = (gate / (1.0 + jnp.exp(-gate)) * up).astype(BF16)
    down(blocks, h_out, down_ref, d_out)


def down(blocks, h_ref, down_ref, d_out):
    for i, k in enumerate(blocks):
        d_out[i] = dot(h_ref[...], down_ref[k]).astype(BF16)


def added(*values):
    return sum(v.astype(F32) for v in values).astype(BF16)


def fast(tokens, norm_gain, gate_weight, up_weight, down_weight):
    rows, cols, pipes = (lax.axis_size(a) for a in ("row", "col", "pipe"))
    _, count, depth = tokens.shape
    width = gate_weight.shape[2] // cols
    part = functools.partial
    own = tokens[0]
    m = rows // 2 * count
    forward = [(p, (p + 1) % pipes) for p in range(pipes)]
    slots = [own] + [swapped(own, "row", k) for k in range(1, rows)]
    order = [2, 3, 0, 1]
    weights = call(
        load, "load", [((cols, depth, width), BF16)] * 2, [], [gate_weight, up_weight],
        copies=2 * cols, cost=4 * gate_weight.size * 2,
    )
    payload, sums = ((m, 2 * width + LANES), BF16), ((2 * m, 2 * width), BF16)
    x, s, p3f, p3n = call(
        part(scale_and_first, 3), "first",
        [((2 * m, depth), BF16), ((2 * m, LANES), BF16), payload, payload],
        [slots[k] for k in order] + [norm_gain, *weights],
    )
    r3f = swapped(p3f, "col", 1)
    r3n = swapped(p3n, "col", 1)
    (p2,) = call(part(product, 2), "product2", [sums], [x, *weights])
    (q2f,) = call(part(joined, 0), "joined", [payload], [p2, s, r3f])
    f2f = swapped(q2f, "col", 2)
    q2n, own_copy = call(
        part(joined_and_own, m), "joined", [payload, (own.shape, BF16)], [p2, s, r3n, own], (), [q2f]
    )
    f2n = swapped(q2n, "col", 2)
    handed_tokens = lax.ppermute(own_copy, "pipe", forward)
    (p1,) = call(part(product, 1), "product1", [sums], [x, *weights])
    r1 = swapped(p1, "col", 1)
    p0, downs = call(
        part(product_and_load, 0), "product0",
        [((2 * m, 2 * width), F32), ((cols, width, depth), BF16)],
        [x, *weights], [down_weight], [q2n], cols,
    )

    def hidden_and_down(first, f2, r3, after, which):
        h, e1 = call(
            part(activate_and_down, first, 1.0 / (depth * cols), (1, 3)), "activate_" + which,
            [((m, width), BF16), ((2, m, depth), BF16)], [p0, r1, s, f2, r3, downs], (), after,
        )
        t1 = swapped(e1, "col", 1)
        (e0,) = call(part(down, (0, 2)), "down_" + which, [((2, m, depth), BF16)], [h, downs])
        return added(e0, t1)

    w = hidden_and_down(0, f2f, r3f, [handed_tokens], "far")
    u = hidden_and_down(m, f2n, r3n, [w], "near")
    w = added(w[0], swapped(w[1], "col", 2))
    w = added(w[:count], swapped(w[count:], "row", 1))
    n = added(u[0], swapped(u[1], "col", 2))

    def onward(value, k):
        pairs = [(p * rows + r, q * rows + (r ^ k)) for p, q in forward for r in range(rows)]
        return lax.ppermute(value, ("pipe", "row"), pairs)

    parts = [onward(n[:count], 0), onward(n[count:], 1), onward(w, 2)]
    return added(handed_tokens, added(*parts))[None]


def plain(tokens, norm_gain, gate_weight, up_weight, down_weight):
    rows, cols, pipes = lax.axis_size("row"), lax.axis_size("col"), lax.axis_size("pipe")
    _, count, depth = tokens.shape
    wide = tokens[0].astype(F32)
    squares = lax.psum(jnp.sum(wide * wide, axis=1), "col")
    inverse = lax.rsqrt(squares / (depth * cols) + EPS)
    normed = (wide * inverse[:, None] * norm_gain).astype(BF16)
    piece = lax.all_gather(normed, "row", axis=0, tiled=True)
    sums = jnp.stack([dot(piece, gate_weight[0]), dot(piece, up_weight[0])])
    summed = lax.psum_scatter(sums.astype(BF16), "col", scatter_dimension=2, tiled=True).astype(F32)
    hidden = (jax.nn.silu(summed[0]) * summed[1]).astype(BF16)
    terms = dot(hidden, down_weight[0]).reshape(rows, count, cols, depth).transpose(0, 2, 1, 3)
    terms = terms.reshape(rows * cols, count, depth).astype(BF16)
    branch_out = lax.psum_scatter(terms, ("row", "col"), scatter_dimension=0, tiled=True)[0]
    layer_out = added(tokens[0], branch_out)
    return lax.ppermute(layer_out, "pipe", [(p, (p + 1) % pipes) for p in range(pipes)])[None]


def local(tokens, norm_gain, gate_weight, up_weight, down_weight):
    rows, cols = lax.axis_size("row"), lax.axis_size("col")
    _, count, depth = tokens.shape
    width = gate_weight.shape[2] // cols
    fits = (
        cols == 4
        and rows == 4
        and count % 16 == 0
        and depth % LANES == 0
        and width % LANES == 0
    )
    form = fast if fits else plain
    return form(tokens, norm_gain, gate_weight, up_weight, down_weight)


def solution(mesh):
    placed = (
        P("pipe", "row", "col"),
        P("pipe", "col"),
        P("pipe", "col", "row"),
        P("pipe", "col", "row"),
        P("pipe", ("row", "col"), None),
    )
    return jax.shard_map(
        local, mesh=mesh, in_specs=placed, out_specs=P("pipe", "row", "col"), check_vma=False
    )
```

time: 52.9 us -> 46 us (0.87)
  waiting for transfers between devices: 20.2 us -> 8.62 us
  starting transfers between devices: 18.3 us -> 21.1 us
  Pallas kernels: 13.1 us -> 14.9 us
    ppermute x10 -> x13, waiting for transfers between devices: 14.1 us -> 5.08 us  [swapped(): return lax.ppermute(value, axis, [(i, i ^ mask) for i in range(count)])]
    ppermute x10 -> x13, starting transfers between devices: 9.97 us -> 13.5 us  [swapped(): return lax.ppermute(value, axis, [(i, i ^ mask) for i in range(count)])]
    ppermute x5 -> x4, waiting for transfers between devices: 6.13 us -> 3.54 us  [the longest x3 3.54 us: onward(): return lax.ppermute(value, ('pipe', 'row'), pairs)]
    pallas_call x7 -> x11, Pallas kernels: 13.1 us -> 14.9 us  [call(): pl.pallas_call(run, name=name, in_specs=[pl.BlockSpec(memory_space=s) for...]
    ppermute x5 -> x4, starting transfers between devices: 8.33 us -> 7.62 us  [the longest x3 6.03 us: onward(): return lax.ppermute(value, ('pipe', 'row'), pairs)]
  transfers between devices with their start and end apart: 15 -> 17, of which waited for: 8 -> 8; matrix products, arithmetic and copies ran while one was open for 0% -> 1% of each run, Pallas kernels for 21% -> 31%
where the time goes in v2:
time: 46 us; the launch traced here: 45.8 us
  starting transfers between devices  21.1 us (46%)
  Pallas kernels  14.9 us (32%)
  waiting for transfers between devices  8.62 us (19%)
  other arithmetic  0.89 us (2%)
    pallas_call x11, Pallas kernels, call(): pl.pallas_call(run, name=name, in_specs=[pl.BlockSpec(memory_space=s) for...  14.9 us
    ppermute x13, starting transfers between devices, swapped(): return lax.ppermute(value, axis, [(i, i ^ mask) for i in range(count)])  13.5 us
    ppermute x3, starting transfers between devices, onward(): return lax.ppermute(value, ('pipe', 'row'), pairs)  6.03 us
    ppermute x13, waiting for transfers between devices, swapped(): return lax.ppermute(value, axis, [(i, i ^ mask) for i in range(count)])  5.08 us
    ppermute x3, waiting for transfers between devices, onward(): return lax.ppermute(value, ('pipe', 'row'), pairs)  3.54 us
    ppermute x1, starting transfers between devices, fast(): handed_tokens = lax.ppermute(own_copy, 'pipe', forward)  1.58 us
  transfers between devices with their start and end apart: 17, of which 8 were waited for; matrix products, arithmetic and copies ran while one was open for 1% of the time, Pallas kernels for 31%

profile of v2, /device:TPU:0, one launch (start us, length us, event | category | flops | bytes accessed | tf_op | source)
XLA Modules:
  0.0 45.8 jit_solution(17423025521096056580)
XLA Ops:
  0.0 4.0 %collective-permute-start = (bf16[32,1024]{1,0:T(8,128)(2,1)}, bf16[32,1024]{1,0:T(8,128)(2,1)S(1)}, u32[]{:S(2)}, u32[]{:S(2)}) collective-permute-start(bf16[32,1024]{1,0:T(8,128)(2,1)} %bitcast.17), channel_id=1, source_target_pairs={{0,8},{4,12},{8,0},{12,4},{1,9},{5,13},{9,1},{13,5},{2,10},{6,14},... | collective-permute-start | bytes 196616 | tf_op jit(solution)/shard_map/ppermute | solution.py:27
  4.0 1.3 %collective-permute-start.1 = (bf16[32,1024]{1,0:T(8,128)(2,1)}, bf16[32,1024]{1,0:T(8,128)(2,1)S(1)}, u32[]{:S(2)}, u32[]{:S(2)}) collective-permute-start(bf16[32,1024]{1,0:T(8,128)(2,1)} %bitcast.18), channel_id=1, source_target_pairs={{0,12},{4,8},{8,4},{12,0},{1,13},{5,9},{9,5},{13,1},{2,14},{6,10},... | collective-permute-start | bytes 196616 | tf_op jit(solution)/shard_map/ppermute | solution.py:27
  5.4 0.2 collective-permute-start.2
  5.6 5.4 %load.1 = (bf16[4,1024,896]{2,1,0:T(8,128)(2,1)S(1)}, bf16[4,1024,896]{2,1,0:T(8,128)(2,1)S(1)}) custom-call(bf16[1,1024,3584]{2,1,0:T(8,128)(2,1)} %refs_0_.1, bf16[1,1024,3584]{2,1,0:T(8,128)(2,1)} %refs_1_.1), custom_call_target="tpu_custom_call" | custom-call | flops 62262001664 | tf_op jit(solution)/shard_map/load/pallas_call | solution.py:47
  11.0 0.0 collective-permute-done.refs_0_
  11.0 0.0 collective-permute-done.1.refs_1_
  11.0 0.0 collective-permute-done.2.refs_3_
  11.0 0.7 %first.1 = (bf16[128,1024]{1,0:T(8,128)(2,1)S(1)}, bf16[128,128]{1,0:T(8,128)(2,1)S(1)}, bf16[64,1920]{1,0:T(8,128)(2,1)S(1)}, bf16[64,1920]{1,0:T(8,128)(2,1)S(1)}) custom-call(bf16[32,1024]{1,0:T(8,128)(2,1)S(1)} %collective-permute-done.refs_0_, bf16[32,1024]{1,0:T(8,128)(2,1)S(1)} %collective-permute-done.1.refs_1_, bf16[32,1024]{1,0:T(8,128)(2,1)S(1)} %bitcast.20, ...), custom_call_target="tpu_custom_call" | custom-call | flops 8762800128 | tf_op jit(solution)/shard_map/first/pallas_call | solution.py:47
  11.8 0.1 collective-permute-start.4
  11.9 0.5 %collective-permute-start.3 = (bf16[64,1920]{1,0:T(8,128)(2,1)S(1)}, bf16[64,1920]{1,0:T(8,128)(2,1)S(1)}, u32[]{:S(2)}, u32[]{:S(2)}) collective-permute-start(bf16[64,1920]{1,0:T(8,128)(2,1)S(1)} %get-tuple-element.23), channel_id=1, source_target_pairs={{0,1},{1,0},{2,3},{3,2},{4,5},{5,4},{6,7},{7,6},{8,9},{9,8},{10,11... | collective-permute-start | bytes 737288 | tf_op jit(solution)/shard_map/ppermute | solution.py:27
  12.4 0.7 %product2.1.refs_0_ = bf16[128,1792]{1,0:T(8,128)(2,1)S(1)} custom-call(bf16[128,1024]{1,0:T(8,128)(2,1)S(1)} %get-tuple-element.21.refs_0_, bf16[4,1024,896]{2,1,0:T(8,128)(2,1)S(1)} %get-tuple-element.19.refs_5_.refs_1_, bf16[4,1024,896]{2,1,0:T(8,128)(2,1)S(1)} %get-tuple-element.20.refs_6_.refs_2_), custom_call_target="tpu_custom_call" | custom-call | tf_op jit(solution)/shard_map/product2/pallas_call | solution.py:47
  13.1 0.7 %product1.1 = bf16[128,1792]{1,0:T(8,128)(2,1)S(1)} custom-call(bf16[128,1024]{1,0:T(8,128)(2,1)S(1)} %get-tuple-element.21.refs_0_, bf16[4,1024,896]{2,1,0:T(8,128)(2,1)S(1)} %get-tuple-element.19.refs_5_.refs_1_, bf16[4,1024,896]{2,1,0:T(8,128)(2,1)S(1)} %get-tuple-element.20.refs_6_.refs_2_), custom_call_target="tpu_custom_call" | custom-call | tf_op jit(solution)/shard_map/product1/pallas_call | solution.py:47
  13.8 0.1 collective-permute-start.6
  14.0 0.0 collective-permute-done.4.refs_2_.refs_4_
  14.0 0.2 joined.2.refs_4_
  14.2 1.6 %collective-permute-start.8 = (bf16[64,1920]{1,0:T(8,128)(2,1)S(1)}, bf16[64,1920]{1,0:T(8,128)(2,1)S(1)}, u32[]{:S(2)}, u32[]{:S(2)}) collective-permute-start(bf16[64,1920]{1,0:T(8,128)(2,1)S(1)} %joined.2.refs_4_), channel_id=1, source_target_pairs={{0,2},{1,3},{2,0},{3,1},{4,6},{5,7},{6,4},{7,5},{8,10},{9,11},{10,... | collective-permute-start | bytes 737288 | tf_op jit(solution)/shard_map/ppermute | solution.py:27
  15.7 0.0 collective-permute-done.3.refs_2_.refs_4_
  15.7 0.2 joined.3
  15.9 1.6 %collective-permute-start.5 = (bf16[32,1024]{1,0:T(8,128)(2,1)S(1)}, bf16[32,1024]{1,0:T(8,128)(2,1)S(1)}, u32[]{:S(2)}, u32[]{:S(2)}) collective-permute-start(bf16[32,1024]{1,0:T(8,128)(2,1)S(1)} %get-tuple-element.25), channel_id=1, source_target_pairs={{0,16},{16,0},{1,17},{17,1},{2,18},{18,2},{3,19},{19,3},{4,20},{20... | collective-permute-start | bytes 196616 | tf_op jit(solution)/shard_map/ppermute | solution.py:197
  17.5 0.5 %collective-permute-start.7 = (bf16[64,1920]{1,0:T(8,128)(2,1)S(1)}, bf16[64,1920]{1,0:T(8,128)(2,1)S(1)}, u32[]{:S(2)}, u32[]{:S(2)}) collective-permute-start(bf16[64,1920]{1,0:T(8,128)(2,1)S(1)} %get-tuple-element.26.refs_4_), channel_id=1, source_target_pairs={{0,2},{1,3},{2,0},{3,1},{4,6},{5,7},{6,4},{7,5},{8,10},{9,11},{10,... | collective-permute-start | bytes 737288 | tf_op jit(solution)/shard_map/ppermute | solution.py:27
  18.0 3.8 %product0.1 = (f32[128,1792]{1,0:T(8,128)S(1)}, bf16[4,896,1024]{2,1,0:T(8,128)(2,1)S(1)}) custom-call(bf16[128,1024]{1,0:T(8,128)(2,1)S(1)} %get-tuple-element.21.refs_0_, bf16[4,1024,896]{2,1,0:T(8,128)(2,1)S(1)} %get-tuple-element.19.refs_5_.refs_1_, bf16[4,1024,896]{2,1,0:T(8,128)(2,1)S(1)} %get-tuple-element.20.refs_6_.refs_2_, ...), custom_call_target="tpu_custom_call" | custom-call | flops 42660999168 | tf_op jit(solution)/shard_map/product0/pallas_call | solution.py:47
  21.8 0.0 collective-permute-done.5.refs_6_
  21.8 0.0 collective-permute-done.6.refs_1_
  21.8 1.1 %collective-permute-done.8.refs_3_ = bf16[64,1920]{1,0:T(8,128)(2,1)S(1)} collective-permute-done((bf16[64,1920]{1,0:T(8,128)(2,1)S(1)}, bf16[64,1920]{1,0:T(8,128)(2,1)S(1)}, u32[]{:S(2)}, u32[]{:S(2)}) %collective-permute-start.8) | collective-permute-done | bytes 245792 | tf_op jit(solution)/shard_map/ppermute | solution.py:27
  23.0 0.9 %activate_far.1 = (bf16[64,896]{1,0:T(8,128)(2,1)S(1)}, bf16[2,64,1024]{2,1,0:T(8,128)(2,1)S(1)}) custom-call(f32[128,1792]{1,0:T(8,128)S(1)} %get-tuple-element.27.refs_0_, bf16[128,1792]{1,0:T(8,128)(2,1)S(1)} %collective-permute-done.6.refs_1_, bf16[128,128]{1,0:T(8,128)(2,1)S(1)} %get-tuple-element.22.refs_1_.refs_2_, ...), custom_call_target="tpu_custom_call" | custom-call | flops 9915799552 | tf_op jit(solution)/shard_map/activate_far/pallas_call | solution.py:47
  23.8 0.1 collective-permute-start.9
  23.9 0.8 %down_far.1 = bf16[2,64,1024]{2,1,0:T(8,128)(2,1)S(1)} custom-call(bf16[64,896]{1,0:T(8,128)(2,1)S(1)} %get-tuple-element.29.refs_0_, bf16[4,896,1024]{2,1,0:T(8,128)(2,1)S(1)} %get-tuple-element.28.refs_5_.refs_1_), custom_call_target="tpu_custom_call" | custom-call | flops 8878100480 | tf_op jit(solution)/shard_map/down_far/pallas_call | solution.py:47
  24.7 0.8 %collective-permute-done.9 = bf16[2,64,1024]{2,1,0:T(8,128)(2,1)S(1)} collective-permute-done((bf16[2,64,1024]{2,1,0:T(8,128)(2,1)S(1)}, bf16[2,64,1024]{2,1,0:T(8,128)(2,1)S(1)}, u32[]{:S(2)}, u32[]{:S(2)}) %collective-permute-start.9) | collective-permute-done | bytes 262176 | tf_op jit(solution)/shard_map/ppermute | solution.py:27
  25.4 0.1 add_convert_fusion.1.refs_6_
  25.5 1.6 %collective-permute-start.14 = (bf16[64,1024]{1,0:T(8,128)(2,1)S(1)}, bf16[64,1024]{1,0:T(8,128)(2,1)S(1)}, u32[]{:S(2)}, u32[]{:S(2)}) collective-permute-start(bf16[64,1024]{1,0:T(8,128)(2,1)S(1)} %slice_bitcast_fusion), channel_id=1, source_target_pairs={{0,2},{1,3},{2,0},{3,1},{4,6},{5,7},{6,4},{7,5},{8,10},{9,11},{10,... | collective-permute-start | bytes 393224 | tf_op jit(solution)/shard_map/ppermute | solution.py:27
  27.1 0.7 %collective-permute-done.7.refs_3_ = bf16[64,1920]{1,0:T(8,128)(2,1)S(1)} collective-permute-done((bf16[64,1920]{1,0:T(8,128)(2,1)S(1)}, bf16[64,1920]{1,0:T(8,128)(2,1)S(1)}, u32[]{:S(2)}, u32[]{:S(2)}) %collective-permute-start.7) | collective-permute-done | bytes 245792 | tf_op jit(solution)/shard_map/ppermute | solution.py:27
  27.8 0.9 %activate_near.1 = (bf16[64,896]{1,0:T(8,128)(2,1)S(1)}, bf16[2,64,1024]{2,1,0:T(8,128)(2,1)S(1)}) custom-call(f32[128,1792]{1,0:T(8,128)S(1)} %get-tuple-element.27.refs_0_, bf16[128,1792]{1,0:T(8,128)(2,1)S(1)} %collective-permute-done.6.refs_1_, bf16[128,128]{1,0:T(8,128)(2,1)S(1)} %get-tuple-element.22.refs_1_.refs_2_, ...), custom_call_target="tpu_custom_call" | custom-call | tf_op jit(solution)/shard_map/activate_near/pallas_call | solution.py:47
  28.7 0.1 collective-permute-start.10
  28.7 0.8 %down_near.1 = bf16[2,64,1024]{2,1,0:T(8,128)(2,1)S(1)} custom-call(bf16[64,896]{1,0:T(8,128)(2,1)S(1)} %get-tuple-element.31.refs_0_, bf16[4,896,1024]{2,1,0:T(8,128)(2,1)S(1)} %get-tuple-element.28.refs_5_.refs_1_), custom_call_target="tpu_custom_call" | custom-call | tf_op jit(solution)/shard_map/down_near/pallas_call | solution.py:47
  29.5 1.6 %collective-permute-done.14 = bf16[64,1024]{1,0:T(8,128)(2,1)S(1)} collective-permute-done((bf16[64,1024]{1,0:T(8,128)(2,1)S(1)}, bf16[64,1024]{1,0:T(8,128)(2,1)S(1)}, u32[]{:S(2)}, u32[]{:S(2)}) %collective-permute-start.14) | collective-permute-done | bytes 131104 | tf_op jit(solution)/shard_map/ppermute | solution.py:27
  31.2 1.9 %collective-permute-start.15 = (bf16[32,1024]{1,0:T(8,128)(2,1)S(1)}, bf16[32,1024]{1,0:T(8,128)(2,1)S(1)}, u32[]{:S(2)}, u32[]{:S(2)}) collective-permute-start(bf16[32,1024]{1,0:T(8,128)(2,1)S(1)} %slice.39), channel_id=1, source_target_pairs={{0,4},{4,0},{8,12},{12,8},{1,5},{5,1},{9,13},{13,9},{2,6},{6,2},{1... | collective-permute-start | bytes 196616 | tf_op jit(solution)/shard_map/ppermute | solution.py:27
  33.0 0.0 collective-permute-done.10
  33.0 0.1 add_convert_fusion
  33.1 1.5 %collective-permute-start.11 = (bf16[64,1024]{1,0:T(8,128)(2,1)S(1)}, bf16[64,1024]{1,0:T(8,128)(2,1)S(1)}, u32[]{:S(2)}, u32[]{:S(2)}) collective-permute-start(bf16[64,1024]{1,0:T(8,128)(2,1)S(1)} %slice_bitcast_fusion.2), channel_id=1, source_target_pairs={{0,2},{1,3},{2,0},{3,1},{4,6},{5,7},{6,4},{7,5},{8,10},{9,11},{10,... | collective-permute-start | bytes 393224 | tf_op jit(solution)/shard_map/ppermute | solution.py:27
  34.7 0.8 %collective-permute-done.15 = bf16[32,1024]{1,0:T(8,128)(2,1)S(1)} collective-permute-done((bf16[32,1024]{1,0:T(8,128)(2,1)S(1)}, bf16[32,1024]{1,0:T(8,128)(2,1)S(1)}, u32[]{:S(2)}, u32[]{:S(2)}) %collective-permute-start.15) | collective-permute-done | bytes 65568 | tf_op jit(solution)/shard_map/ppermute | solution.py:27
  35.5 3.8 %collective-permute-start.16 = (bf16[32,1024]{1,0:T(8,128)(2,1)S(1)}, bf16[32,1024]{1,0:T(8,128)(2,1)S(1)}, u32[]{:S(2)}, u32[]{:S(2)}) collective-permute-start(bf16[32,1024]{1,0:T(8,128)(2,1)S(1)} %add_convert_fusion.4), channel_id=1, source_target_pairs={{0,24},{4,28},{8,16},{12,20},{16,8},{20,12},{24,0},{28,4},{1,25},{... | collective-permute-start | bytes 196616 | tf_op jit(solution)/shard_map/ppermute | solution.py:223
  39.4 0.0 collective-permute-done.11
  39.4 0.6 %collective-permute-start.12 = (bf16[32,1024]{1,0:T(8,128)(2,1)S(1)}, bf16[32,1024]{1,0:T(8,128)(2,1)S(1)}, u32[]{:S(2)}, u32[]{:S(2)}) collective-permute-start(bf16[32,1024]{1,0:T(8,128)(2,1)S(1)} %get-tuple-element.33), channel_id=1, source_target_pairs={{0,16},{4,20},{8,24},{12,28},{16,0},{20,4},{24,8},{28,12},{1,17},{... | collective-permute-start | bytes 196616 | tf_op jit(solution)/shard_map/ppermute | solution.py:223
  40.0 1.6 %collective-permute-start.13 = (bf16[32,1024]{1,0:T(8,128)(2,1)S(1)}, bf16[32,1024]{1,0:T(8,128)(2,1)S(1)}, u32[]{:S(2)}, u32[]{:S(2)}) collective-permute-start(bf16[32,1024]{1,0:T(8,128)(2,1)S(1)} %get-tuple-element.34), channel_id=1, source_target_pairs={{0,20},{4,16},{8,28},{12,24},{16,4},{20,0},{24,12},{28,8},{1,21},{... | collective-permute-start | bytes 196616 | tf_op jit(solution)/shard_map/ppermute | solution.py:223
  41.6 0.1 collective-permute-done.16
  41.7 2.0 %collective-permute-done.12 = bf16[32,1024]{1,0:T(8,128)(2,1)S(1)} collective-permute-done((bf16[32,1024]{1,0:T(8,128)(2,1)S(1)}, bf16[32,1024]{1,0:T(8,128)(2,1)S(1)}, u32[]{:S(2)}, u32[]{:S(2)}) %collective-permute-start.12) | collective-permute-done | bytes 65568 | tf_op jit(solution)/shard_map/ppermute | solution.py:223
  43.8 1.4 %collective-permute-done.13 = bf16[32,1024]{1,0:T(8,128)(2,1)S(1)} collective-permute-done((bf16[32,1024]{1,0:T(8,128)(2,1)S(1)}, bf16[32,1024]{1,0:T(8,128)(2,1)S(1)}, u32[]{:S(2)}, u32[]{:S(2)}) %collective-permute-start.13) | collective-permute-done | bytes 65568 | tf_op jit(solution)/shard_map/ppermute | solution.py:223
  45.2 0.7 %fusion.2 = bf16[1,32,1024]{2,1,0:T(8,128)(2,1)} fusion(bf16[32,1024]{1,0:T(8,128)(2,1)S(1)} %collective-permute-done.16, bf16[32,1024]{1,0:T(8,128)(2,1)S(1)} %collective-permute-done.13, bf16[32,1024]{1,0:T(8,128)(2,1)S(1)} %collective-permute-done.12, bf16[32,1024]{1,0:T(8,128)(2,1)S(1)} %collective-permute-done.5.refs_6_), kind=kLoop, calls=%fused_computation.13 | loop fusion | flops 327680 | bytes 327680 | tf_op jit(solution)/shard_map/broadcast_in_dim | solution.py:226
  (11 shorter events, 0.1 us)
Async XLA Ops:
  0.0 11.0 %copy-start = (bf16[1,32,1024]{2,1,0:T(8,128)(2,1)S(1)}, bf16[1,32,1024]{2,1,0:T(8,128)(2,1)}, u32[]{:S(2)}) copy-start(bf16[1,32,1024]{2,1,0:T(8,128)(2,1)} %param.5) | copy-start | bytes 196612
  0.0 11.0 %copy-start.1 = (f32[1,1024]{1,0:T(1,128)S(1)}, f32[1,1024]{1,0:T(1,128)}, u32[]{:S(2)}) copy-start(f32[1,1024]{1,0:T(1,128)} %refs_4_.1) | copy-start | bytes 12292
  0.0 11.0 %collective-permute-start = (bf16[32,1024]{1,0:T(8,128)(2,1)}, bf16[32,1024]{1,0:T(8,128)(2,1)S(1)}, u32[]{:S(2)}, u32[]{:S(2)}) collective-permute-start(bf16[32,1024]{1,0:T(8,128)(2,1)} %bitcast.17), channel_id=1, source_target_pairs={{0,8},{4,12},{8,0},{12,4},{1,9},{5,13},{9,1},{13,5},{2,10},{6,14},... | collective-permute-start | bytes 196616 | tf_op jit(solution)/shard_map/ppermute | solution.py:27
  4.0 7.0 %collective-permute-start.1 = (bf16[32,1024]{1,0:T(8,128)(2,1)}, bf16[32,1024]{1,0:T(8,128)(2,1)S(1)}, u32[]{:S(2)}, u32[]{:S(2)}) collective-permute-start(bf16[32,1024]{1,0:T(8,128)(2,1)} %bitcast.18), channel_id=1, source_target_pairs={{0,12},{4,8},{8,4},{12,0},{1,13},{5,9},{9,5},{13,1},{2,14},{6,10},... | collective-permute-start | bytes 196616 | tf_op jit(solution)/shard_map/ppermute | solution.py:27
  5.4 5.6 %collective-permute-start.2 = (bf16[32,1024]{1,0:T(8,128)(2,1)}, bf16[32,1024]{1,0:T(8,128)(2,1)S(1)}, u32[]{:S(2)}, u32[]{:S(2)}) collective-permute-start(bf16[32,1024]{1,0:T(8,128)(2,1)} %bitcast.19), channel_id=1, source_target_pairs={{0,4},{4,0},{8,12},{12,8},{1,5},{5,1},{9,13},{13,9},{2,6},{6,2},{1... | collective-permute-start | bytes 196616 | tf_op jit(solution)/shard_map/ppermute | solution.py:27
  11.8 2.2 %collective-permute-start.4 = (bf16[64,1920]{1,0:T(8,128)(2,1)S(1)}, bf16[64,1920]{1,0:T(8,128)(2,1)S(1)}, u32[]{:S(2)}, u32[]{:S(2)}) collective-permute-start(bf16[64,1920]{1,0:T(8,128)(2,1)S(1)} %get-tuple-element.24), channel_id=1, source_target_pairs={{0,1},{1,0},{2,3},{3,2},{4,5},{5,4},{6,7},{7,6},{8,9},{9,8},{10,11... | collective-permute-start | bytes 737288 | tf_op jit(solution)/shard_map/ppermute | solution.py:27
  11.9 3.8 %collective-permute-start.3 = (bf16[64,1920]{1,0:T(8,128)(2,1)S(1)}, bf16[64,1920]{1,0:T(8,128)(2,1)S(1)}, u32[]{:S(2)}, u32[]{:S(2)}) collective-permute-start(bf16[64,1920]{1,0:T(8,128)(2,1)S(1)} %get-tuple-element.23), channel_id=1, source_target_pairs={{0,1},{1,0},{2,3},{3,2},{4,5},{5,4},{6,7},{7,6},{8,9},{9,8},{10,11... | collective-permute-start | bytes 737288 | tf_op jit(solution)/shard_map/ppermute | solution.py:27
  13.8 8.0 %collective-permute-start.6 = (bf16[128,1792]{1,0:T(8,128)(2,1)S(1)}, bf16[128,1792]{1,0:T(8,128)(2,1)S(1)}, u32[]{:S(2)}, u32[]{:S(2)}) collective-permute-start(bf16[128,1792]{1,0:T(8,128)(2,1)S(1)} %product1.1), channel_id=1, source_target_pairs={{0,1},{1,0},{2,3},{3,2},{4,5},{5,4},{6,7},{7,6},{8,9},{9,8},{10,11... | collective-permute-start | bytes 1376264 | tf_op jit(solution)/shard_map/ppermute | solution.py:27
  14.2 8.8 %collective-permute-start.8 = (bf16[64,1920]{1,0:T(8,128)(2,1)S(1)}, bf16[64,1920]{1,0:T(8,128)(2,1)S(1)}, u32[]{:S(2)}, u32[]{:S(2)}) collective-permute-start(bf16[64,1920]{1,0:T(8,128)(2,1)S(1)} %joined.2.refs_4_), channel_id=1, source_target_pairs={{0,2},{1,3},{2,0},{3,1},{4,6},{5,7},{6,4},{7,5},{8,10},{9,11},{10,... | collective-permute-start | bytes 737288 | tf_op jit(solution)/shard_map/ppermute | solution.py:27
  15.9 5.9 %collective-permute-start.5 = (bf16[32,1024]{1,0:T(8,128)(2,1)S(1)}, bf16[32,1024]{1,0:T(8,128)(2,1)S(1)}, u32[]{:S(2)}, u32[]{:S(2)}) collective-permute-start(bf16[32,1024]{1,0:T(8,128)(2,1)S(1)} %get-tuple-element.25), channel_id=1, source_target_pairs={{0,16},{16,0},{1,17},{17,1},{2,18},{18,2},{3,19},{19,3},{4,20},{20... | collective-permute-start | bytes 196616 | tf_op jit(solution)/shard_map/ppermute | solution.py:197
  17.5 10.3 %collective-permute-start.7 = (bf16[64,1920]{1,0:T(8,128)(2,1)S(1)}, bf16[64,1920]{1,0:T(8,128)(2,1)S(1)}, u32[]{:S(2)}, u32[]{:S(2)}) collective-permute-start(bf16[64,1920]{1,0:T(8,128)(2,1)S(1)} %get-tuple-element.26.refs_4_), channel_id=1, source_target_pairs={{0,2},{1,3},{2,0},{3,1},{4,6},{5,7},{6,4},{7,5},{8,10},{9,11},{10,... | collective-permute-start | bytes 737288 | tf_op jit(solution)/shard_map/ppermute | solution.py:27
  23.8 1.6 %collective-permute-start.9 = (bf16[2,64,1024]{2,1,0:T(8,128)(2,1)S(1)}, bf16[2,64,1024]{2,1,0:T(8,128)(2,1)S(1)}, u32[]{:S(2)}, u32[]{:S(2)}) collective-permute-start(bf16[2,64,1024]{2,1,0:T(8,128)(2,1)S(1)} %get-tuple-element.30), channel_id=1, source_target_pairs={{0,1},{1,0},{2,3},{3,2},{4,5},{5,4},{6,7},{7,6},{8,9},{9,8},{10,11... | collective-permute-start | bytes 786440 | tf_op jit(solution)/shard_map/ppermute | solution.py:27
  25.5 5.6 %collective-permute-start.14 = (bf16[64,1024]{1,0:T(8,128)(2,1)S(1)}, bf16[64,1024]{1,0:T(8,128)(2,1)S(1)}, u32[]{:S(2)}, u32[]{:S(2)}) collective-permute-start(bf16[64,1024]{1,0:T(8,128)(2,1)S(1)} %slice_bitcast_fusion), channel_id=1, source_target_pairs={{0,2},{1,3},{2,0},{3,1},{4,6},{5,7},{6,4},{7,5},{8,10},{9,11},{10,... | collective-permute-start | bytes 393224 | tf_op jit(solution)/shard_map/ppermute | solution.py:27
  28.7 4.4 %collective-permute-start.10 = (bf16[2,64,1024]{2,1,0:T(8,128)(2,1)S(1)}, bf16[2,64,1024]{2,1,0:T(8,128)(2,1)S(1)}, u32[]{:S(2)}, u32[]{:S(2)}) collective-permute-start(bf16[2,64,1024]{2,1,0:T(8,128)(2,1)S(1)} %get-tuple-element.32), channel_id=1, source_target_pairs={{0,1},{1,0},{2,3},{3,2},{4,5},{5,4},{6,7},{7,6},{8,9},{9,8},{10,11... | collective-permute-start | bytes 786440 | tf_op jit(solution)/shard_map/ppermute | solution.py:27
  31.2 4.3 %collective-permute-start.15 = (bf16[32,1024]{1,0:T(8,128)(2,1)S(1)}, bf16[32,1024]{1,0:T(8,128)(2,1)S(1)}, u32[]{:S(2)}, u32[]{:S(2)}) collective-permute-start(bf16[32,1024]{1,0:T(8,128)(2,1)S(1)} %slice.39), channel_id=1, source_target_pairs={{0,4},{4,0},{8,12},{12,8},{1,5},{5,1},{9,13},{13,9},{2,6},{6,2},{1... | collective-permute-start | bytes 196616 | tf_op jit(solution)/shard_map/ppermute | solution.py:27
  33.1 6.2 %collective-permute-start.11 = (bf16[64,1024]{1,0:T(8,128)(2,1)S(1)}, bf16[64,1024]{1,0:T(8,128)(2,1)S(1)}, u32[]{:S(2)}, u32[]{:S(2)}) collective-permute-start(bf16[64,1024]{1,0:T(8,128)(2,1)S(1)} %slice_bitcast_fusion.2), channel_id=1, source_target_pairs={{0,2},{1,3},{2,0},{3,1},{4,6},{5,7},{6,4},{7,5},{8,10},{9,11},{10,... | collective-permute-start | bytes 393224 | tf_op jit(solution)/shard_map/ppermute | solution.py:27
  35.5 6.2 %collective-permute-start.16 = (bf16[32,1024]{1,0:T(8,128)(2,1)S(1)}, bf16[32,1024]{1,0:T(8,128)(2,1)S(1)}, u32[]{:S(2)}, u32[]{:S(2)}) collective-permute-start(bf16[32,1024]{1,0:T(8,128)(2,1)S(1)} %add_convert_fusion.4), channel_id=1, source_target_pairs={{0,24},{4,28},{8,16},{12,20},{16,8},{20,12},{24,0},{28,4},{1,25},{... | collective-permute-start | bytes 196616 | tf_op jit(solution)/shard_map/ppermute | solution.py:223
  39.4 4.3 %collective-permute-start.12 = (bf16[32,1024]{1,0:T(8,128)(2,1)S(1)}, bf16[32,1024]{1,0:T(8,128)(2,1)S(1)}, u32[]{:S(2)}, u32[]{:S(2)}) collective-permute-start(bf16[32,1024]{1,0:T(8,128)(2,1)S(1)} %get-tuple-element.33), channel_id=1, source_target_pairs={{0,16},{4,20},{8,24},{12,28},{16,0},{20,4},{24,8},{28,12},{1,17},{... | collective-permute-start | bytes 196616 | tf_op jit(solution)/shard_map/ppermute | solution.py:223
  40.0 5.2 %collective-permute-start.13 = (bf16[32,1024]{1,0:T(8,128)(2,1)S(1)}, bf16[32,1024]{1,0:T(8,128)(2,1)S(1)}, u32[]{:S(2)}, u32[]{:S(2)}) collective-permute-start(bf16[32,1024]{1,0:T(8,128)(2,1)S(1)} %get-tuple-element.34), channel_id=1, source_target_pairs={{0,20},{4,16},{8,28},{12,24},{16,4},{20,0},{24,12},{28,8},{1,21},{... | collective-permute-start | bytes 196616 | tf_op jit(solution)/shard_map/ppermute | solution.py:223

commit v3 on v2

v3 whole, which is shorter than its diff:
```python
import functools

import jax
import jax.numpy as jnp
from jax import lax
from jax.experimental import pallas as pl
from jax.experimental.pallas import tpu as pltpu
from jax.sharding import PartitionSpec as P

EPS = 1e-05
LANES = 128
F32 = jnp.float32
BF16 = jnp.bfloat16


def flipped(index, mask):
    bit = 1
    while bit <= mask:
        if mask & bit:
            index = index + bit - 2 * bit * ((index // bit) % 2)
        bit *= 2
    return index


def swapped(value, axis, mask):
    count = lax.axis_size(axis)
    return lax.ppermute(value, axis, [(i, i ^ mask) for i in range(count)])


def masks_of(count):
    return [1 << b for b in range(count.bit_length() - 1)]


placed_in = pltpu.with_memory_space_constraint

COST = dict(
    pause=1000, first_near=100, next_near=100, first_far=100, next_far=100, joined_near=100, joined_far=100, product1=15, product0=1, activate_near=100, down_near=100, activate_far=100, down_far=1
)


def call(body, name, outs, held, streamed=(), after=(), copies=0):
    fixed = len(held) + len(streamed)

    def run(*refs):
        body(*refs[:fixed], *refs[fixed + len(after) :])

    spaces = [pltpu.VMEM] * len(held) + [pltpu.HBM] * len(streamed)
    return pl.pallas_call(
        run,
        name=name,
        in_specs=[pl.BlockSpec(memory_space=s) for s in spaces]
        + [pl.BlockSpec(memory_space=pl.ANY)] * len(after),
        out_shape=[pltpu.VMEM(shape, dtype) for shape, dtype in outs],
        out_specs=[pl.BlockSpec(memory_space=pltpu.VMEM)] * len(outs),
        scratch_shapes=[pltpu.SemaphoreType.DMA((copies,))] if copies else [],
        cost_estimate=pl.CostEstimate(
            flops=COST.get(name, 0) * 10**8, transcendentals=0, bytes_accessed=0
        ),
        compiler_params=pltpu.CompilerParams(vmem_limit_bytes=16 * 1024 * 1024),
    )(*[placed_in(a, s) for a, s in zip([*held, *streamed], spaces)], *after)


def dot(a, b):
    return jnp.dot(a, b, preferred_element_type=F32)


def block(k, width):
    return pl.ds(pl.multiple_of(flipped(lax.axis_index("col"), k) * width, LANES), width)


def in_terms(column):
    lane = lax.broadcasted_iota(jnp.int32, (column.shape[0], LANES), 1)
    terms = jnp.zeros(lane.shape, F32)
    for i in range(3):
        part = column.astype(BF16).astype(F32)
        terms = jnp.where(lane == i, part, terms)
        column = column - part
    return terms.astype(BF16)


def from_terms(tile):
    return jnp.sum(tile.astype(F32), axis=1, keepdims=True)


def products(k, xs, weights, outs):
    width = weights[0].shape[2] // lax.axis_size("col")
    for i, ref in enumerate(weights):
        x = xs[0][...] if len(xs) == 1 else jnp.concatenate([x[...] for x in xs], axis=0)
        both = dot(x, ref[0, :, block(k, width)])
        row = 0
        for out in outs:
            here = slice(row, row + out.shape[0])
            out[:, i * width : (i + 1) * width] = both[here].astype(out.dtype)
            row += out.shape[0]


def first(k, a_ref, b_ref, gain_ref, gate, up, x_out, s_out, out):
    rows = a_ref.shape[0]
    for i, ref in enumerate((a_ref, b_ref)):
        wide = ref[...].astype(F32)
        here = slice(i * rows, (i + 1) * rows)
        x_out[here, :] = (wide * gain_ref[...]).astype(BF16)
        s_out[here, :] = in_terms(jnp.sum(wide * wide, axis=1, keepdims=True))
    out[:, out.shape[1] - LANES :] = s_out[...]
    products(k, [x_out], (gate, up), (out,))


def two_products(ks, x, gate, up, a_out, b_out):
    products(ks[0], [x], (gate, up), (a_out,))
    products(ks[1], [x], (gate, up), (b_out,))


def product_of_both(k, xa, xb, gate, up, a_out, b_out):
    products(k, [xa, xb], (gate, up), (a_out, b_out))


def pause(value_ref, out):
    out[...] = value_ref[...]


def joined(p_ref, s_ref, r_ref, out):
    width = p_ref.shape[1]
    out[:, :width] = (p_ref[...].astype(F32) + r_ref[:, :width].astype(F32)).astype(BF16)
    out[:, width:] = in_terms(from_terms(s_ref[...]) + from_terms(r_ref[:, width:]))


def activate(factor, p_ref, near_ref, s_ref, far_ref, sib_ref, h_out):
    width = h_out.shape[1]
    tail = slice(2 * width, 2 * width + LANES)
    tiles = (s_ref[...], sib_ref[:, tail], far_ref[:, tail])
    inverse = lax.rsqrt(sum(from_terms(tile) for tile in tiles) * factor + EPS)
    gate, up = (
        (p_ref[:, at] + near_ref[:, at].astype(F32) + far_ref[:, at].astype(F32)) * inverse
        for at in (slice(0, width), slice(width, 2 * width))
    )
    h_out[...] = (gate / (1.0 + jnp.exp(-gate)) * up).astype(BF16)


def down(blocks, h, weight, out):
    for i, k in enumerate(blocks):
        out[i] = dot(h[...], weight[0, :, block(k, out.shape[2])]).astype(BF16)


def activate_and_down(factor, blocks, p, near, s, far, sib, weight, h_out, out):
    activate(factor, p, near, s, far, sib, h_out)
    down(blocks, h_out, weight, out)


def added(*values):
    return sum(v.astype(F32) for v in values).astype(BF16)


def sum_of_two(a_ref, b_ref, out):
    out[...] = added(a_ref[...], b_ref[...])


def fast(tokens, norm_gain, gate_weight, up_weight, down_weight):
    rows, cols, pipes = (lax.axis_size(a) for a in ("row", "col", "pipe"))
    _, count, depth = tokens.shape
    width = gate_weight.shape[2] // cols
    part = functools.partial
    own = tokens[0]
    m = rows // 2 * count
    forward = [(p, (p + 1) % pipes) for p in range(pipes)]
    slots = [own] + [swapped(own, "row", k) for k in range(1, rows)]
    payload, sums, wide = (((m, 2 * width + LANES), BF16), ((m, 2 * width), BF16), ((m, 2 * width), F32))
    x_shape, s_shape = ((m, depth), BF16), ((m, LANES), BF16)
    h_shape, e_shape = ((m, width), BF16), ((2, m, depth), BF16)
    weights = [gate_weight, up_weight]
    (gain,) = call(pause, "pause", [(norm_gain.shape, F32)], [norm_gain])

    xn, sn, p3n = call(
        part(first, 3), "first_near", [x_shape, s_shape, payload], [*slots[:2], gain, *weights]
    )
    r3n = swapped(p3n, "col", 1)
    p2n, p1n = call(part(two_products, (2, 1)), "next_near", [sums, sums], [xn, *weights])
    r1n = swapped(p1n, "col", 1)
    (q2n,) = call(joined, "joined_near", [payload], [p2n, sn, r3n])
    f2n = swapped(q2n, "col", 2)

    xf, sf, p3f = call(
        part(first, 3), "first_far", [x_shape, s_shape, payload], [*slots[2:], gain, *weights], (), [q2n]
    )
    r3f = swapped(p3f, "col", 1)
    p2f, p1f = call(
        part(two_products, (2, 1)), "next_far", [sums, sums], [xf, *weights], (), [p3f]
    )
    r1f = swapped(p1f, "col", 1)
    (q2f,) = call(joined, "joined_far", [payload], [p2f, sf, r3f])
    f2f = swapped(q2f, "col", 2)

    p0n, p0f = call(
        part(product_of_both, 0), "product0", [wide, wide], [xn, xf, *weights], (), [q2f]
    )

    def hidden_and_down(which, p0, r1, s, f2, r3, after):
        h, e1 = call(
            part(activate_and_down, 1.0 / (depth * cols), (1, 3)), "activate_" + which,
            [h_shape, e_shape], [p0, r1, s, f2, r3, down_weight], (), after,
        )
        t1 = swapped(e1, "col", 1)
        (e0,) = call(part(down, (0, 2)), "down_" + which, [e_shape], [h, down_weight], (), [e1])
        return e0, t1

    u = added(*hidden_and_down("near", p0n, r1n, sn, f2n, r3n, ()))
    n = added(u[0], swapped(u[1], "col", 2))
    e0f, t1f = hidden_and_down("far", p0f, r1f, sf, f2f, r3f, [u])
    (w,) = call(sum_of_two, "sum_far", [e_shape], [e0f, t1f], (), [])

    def onward(value, k):
        pairs = [(p * rows + r, q * rows + (r ^ k)) for p, q in forward for r in range(rows)]
        return lax.ppermute(value, ("pipe", "row"), pairs)

    own_part = onward(added(own, n[:count]), 0)
    near_part = onward(n[count:], 1)
    w = added(w[:, :count], swapped(w[:, count:], "row", 1))
    (w,) = call(sum_of_two, "sum_over_x", [(own.shape, BF16)], [w[0], swapped(w[1], "col", 2)], (), [own_part])
    return added(own_part, near_part, onward(w, 2))[None]


def plain(tokens, norm_gain, gate_weight, up_weight, down_weight):
    rows, cols, pipes = lax.axis_size("row"), lax.axis_size("col"), lax.axis_size("pipe")
    _, count, depth = tokens.shape
    wide = tokens[0].astype(F32)
    squares = lax.psum(jnp.sum(wide * wide, axis=1), "col")
    inverse = lax.rsqrt(squares / (depth * cols) + EPS)
    normed = (wide * inverse[:, None] * norm_gain).astype(BF16)
    piece = lax.all_gather(normed, "row", axis=0, tiled=True)
    sums = jnp.stack([dot(piece, gate_weight[0]), dot(piece, up_weight[0])])
    summed = lax.psum_scatter(sums.astype(BF16), "col", scatter_dimension=2, tiled=True).astype(F32)
    hidden = (jax.nn.silu(summed[0]) * summed[1]).astype(BF16)
    terms = dot(hidden, down_weight[0]).reshape(rows, count, cols, depth).transpose(0, 2, 1, 3)
    terms = terms.reshape(rows * cols, count, depth).astype(BF16)
    branch_out = lax.psum_scatter(terms, ("row", "col"), scatter_dimension=0, tiled=True)[0]
    layer_out = added(tokens[0], branch_out)
    return lax.ppermute(layer_out, "pipe", [(p, (p + 1) % pipes) for p in range(pipes)])[None]


def local(tokens, norm_gain, gate_weight, up_weight, down_weight):
    rows, cols = lax.axis_size("row"), lax.axis_size("col")
    _, count, depth = tokens.shape
    width = gate_weight.shape[2] // cols
    fits = (
        cols == 4
        and rows == 4
        and count % 16 == 0
        and depth % LANES == 0
        and width % LANES == 0
    )
    form = fast if fits else plain
    return form(tokens, norm_gain, gate_weight, up_weight, down_weight)


def solution(mesh):
    placed = (
        P("pipe", "row", "col"),
        P("pipe", "col"),
        P("pipe", "col", "row"),
        P("pipe", "col", "row"),
        P("pipe", ("row", "col"), None),
    )
    return jax.shard_map(
        local, mesh=mesh, in_specs=placed, out_specs=P("pipe", "row", "col"), check_vma=False
    )
```

time: 46 us -> 43.1 us (0.937)
  Pallas kernels: 14.9 us -> 8.68 us
  starting transfers between devices: 21.1 us -> 24.5 us
  waiting for transfers between devices: 8.62 us -> 7.89 us
  local copies, waits for them, and re-layouts: 0.05 us -> 0.75 us
    pallas_call x11 -> x14, Pallas kernels: 14.9 us -> 8.68 us  [call(): pl.pallas_call(run, name=name, in_specs=[pl.BlockSpec(memory_space=s) for...]
    ppermute x13 -> x14, starting transfers between devices: 13.5 us -> 16.4 us  [swapped(): return lax.ppermute(value, axis, [(i, i ^ mask) for i in range(count)])]
    ppermute x3, starting transfers between devices: 6.03 us -> 8.12 us  [onward(): return lax.ppermute(value, ('pipe', 'row'), pairs)]
    ppermute x1 -> x0, starting transfers between devices: 1.58 us -> none  [fast(): handed_tokens = lax.ppermute(own_copy, 'pipe', forward)]
    ppermute x3, waiting for transfers between devices: 3.54 us -> 2.53 us  [onward(): return lax.ppermute(value, ('pipe', 'row'), pairs)]
    unnamed x4 -> x16, local copies, waits for them, and re-layouts: 0.01 us -> 0.72 us
    ppermute x13 -> x14, waiting for transfers between devices: 5.08 us -> 5.36 us  [swapped(): return lax.ppermute(value, axis, [(i, i ^ mask) for i in range(count)])]
  transfers between devices with their start and end apart: 17 -> 17, of which waited for: 8 -> 7; matrix products, arithmetic and copies ran while one was open for 1% -> 0% of each run, Pallas kernels for 31% -> 20%
where the time goes in v3:
time: 43.1 us; the launch traced here: 42.9 us
  starting transfers between devices  24.5 us (57%)
  Pallas kernels  8.68 us (20%)
  waiting for transfers between devices  7.89 us (18%)
  other arithmetic  0.81 us (2%)
  local copies, waits for them, and re-layouts  0.75 us (2%)
    ppermute x14, starting transfers between devices, swapped(): return lax.ppermute(value, axis, [(i, i ^ mask) for i in range(count)])  16.4 us
    pallas_call x14, Pallas kernels, call(): pl.pallas_call(run, name=name, in_specs=[pl.BlockSpec(memory_space=s) for...  8.68 us
    ppermute x3, starting transfers between devices, onward(): return lax.ppermute(value, ('pipe', 'row'), pairs)  8.12 us
    ppermute x14, waiting for transfers between devices, swapped(): return lax.ppermute(value, axis, [(i, i ^ mask) for i in range(count)])  5.36 us
    ppermute x3, waiting for transfers between devices, onward(): return lax.ppermute(value, ('pipe', 'row'), pairs)  2.53 us
  transfers between devices with their start and end apart: 17, of which 7 were waited for; matrix products, arithmetic and copies ran while one was open for 0% of the time, Pallas kernels for 20%

profile of v3, /device:TPU:0, one launch (start us, length us, event | category | flops | bytes accessed | tf_op | source)
XLA Modules:
  0.0 42.9 jit_solution(3577828455940616659)
XLA Ops:
  0.0 3.1 %collective-permute-start = (bf16[32,1024]{1,0:T(8,128)(2,1)}, bf16[32,1024]{1,0:T(8,128)(2,1)S(1)}, u32[]{:S(2)}, u32[]{:S(2)}) collective-permute-start(bf16[32,1024]{1,0:T(8,128)(2,1)} %bitcast.21), channel_id=1, source_target_pairs={{0,4},{4,0},{8,12},{12,8},{1,5},{5,1},{9,13},{13,9},{2,6},{6,2},{1... | collective-permute-start | bytes 196616 | tf_op jit(solution)/shard_map/ppermute | solution.py:27
  3.1 2.6 %collective-permute-start.1 = (bf16[32,1024]{1,0:T(8,128)(2,1)}, bf16[32,1024]{1,0:T(8,128)(2,1)S(1)}, u32[]{:S(2)}, u32[]{:S(2)}) collective-permute-start(bf16[32,1024]{1,0:T(8,128)(2,1)} %bitcast.22), channel_id=1, source_target_pairs={{0,8},{4,12},{8,0},{12,4},{1,9},{5,13},{9,1},{13,5},{2,10},{6,14},... | collective-permute-start | bytes 196616 | tf_op jit(solution)/shard_map/ppermute | solution.py:27
  5.7 0.0 collective-permute-start.2
  5.7 0.7 %copy-done.1 = f32[1,1024]{1,0:T(1,128)S(1)} copy-done((f32[1,1024]{1,0:T(1,128)S(1)}, f32[1,1024]{1,0:T(1,128)}, u32[]{:S(2)}) %copy-start.1) | copy-done | bytes 4120
  6.4 0.0 collective-permute-done.refs_1_
  6.5 0.8 %first_near.1 = (bf16[64,1024]{1,0:T(8,128)(2,1)S(1)}, bf16[64,128]{1,0:T(8,128)(2,1)S(1)}, bf16[64,1920]{1,0:T(8,128)(2,1)S(1)}) custom-call(bf16[32,1024]{1,0:T(8,128)(2,1)S(1)} %bitcast.24, bf16[32,1024]{1,0:T(8,128)(2,1)S(1)} %collective-permute-done.refs_1_, f32[1,1024]{1,0:T(1,128)S(1)} %pause.1.refs_2_, bf16[1,1024,3584]{2,1,0:T(8,128)(2,1)S(1)} %bitcast.16, ...), custom_call_target="tpu_custom_call" | custom-call | flops 10000000000 | tf_op jit(solution)/shard_map/first_near/pallas_call | solution.py:48
  7.2 0.1 collective-permute-start.3
  7.3 1.4 %next_near.1 = (bf16[64,1792]{1,0:T(8,128)(2,1)S(1)}, bf16[64,1792]{1,0:T(8,128)(2,1)S(1)}) custom-call(bf16[64,1024]{1,0:T(8,128)(2,1)S(1)} %get-tuple-element.21.refs_0_, bf16[1,1024,3584]{2,1,0:T(8,128)(2,1)S(1)} %bitcast.16, bf16[1,1024,3584]{2,1,0:T(8,128)(2,1)S(1)} %bitcast.18), custom_call_target="tpu_custom_call" | custom-call | flops 10000000000 | tf_op jit(solution)/shard_map/next_near/pallas_call | solution.py:48
  8.7 0.5 %collective-permute-start.5 = (bf16[64,1792]{1,0:T(8,128)(2,1)S(1)}, bf16[64,1792]{1,0:T(8,128)(2,1)S(1)}, u32[]{:S(2)}, u32[]{:S(2)}) collective-permute-start(bf16[64,1792]{1,0:T(8,128)(2,1)S(1)} %get-tuple-element.30), channel_id=1, source_target_pairs={{0,1},{1,0},{2,3},{3,2},{4,5},{5,4},{6,7},{7,6},{8,9},{9,8},{10,11... | collective-permute-start | bytes 688136 | tf_op jit(solution)/shard_map/ppermute | solution.py:27
  9.2 0.0 collective-permute-done.3.refs_2_.refs_4_
  9.2 0.2 joined_near.1.refs_5_
  9.4 1.8 %collective-permute-start.6 = (bf16[64,1920]{1,0:T(8,128)(2,1)S(1)}, bf16[64,1920]{1,0:T(8,128)(2,1)S(1)}, u32[]{:S(2)}, u32[]{:S(2)}) collective-permute-start(bf16[64,1920]{1,0:T(8,128)(2,1)S(1)} %joined_near.1.refs_5_), channel_id=1, source_target_pairs={{0,2},{1,3},{2,0},{3,1},{4,6},{5,7},{6,4},{7,5},{8,10},{9,11},{10,... | collective-permute-start | bytes 737288 | tf_op jit(solution)/shard_map/ppermute | solution.py:27
  11.2 0.0 collective-permute-done.1.refs_0_
  11.2 0.8 %collective-permute-done.2.refs_1_ = bf16[32,1024]{1,0:T(8,128)(2,1)S(1)} collective-permute-done((bf16[32,1024]{1,0:T(8,128)(2,1)}, bf16[32,1024]{1,0:T(8,128)(2,1)S(1)}, u32[]{:S(2)}, u32[]{:S(2)}) %collective-permute-start.2) | collective-permute-done | bytes 65568 | tf_op jit(solution)/shard_map/ppermute | solution.py:27
  12.0 0.8 %first_far.1 = (bf16[64,1024]{1,0:T(8,128)(2,1)S(1)}, bf16[64,128]{1,0:T(8,128)(2,1)S(1)}, bf16[64,1920]{1,0:T(8,128)(2,1)S(1)}) custom-call(bf16[32,1024]{1,0:T(8,128)(2,1)S(1)} %collective-permute-done.1.refs_0_, bf16[32,1024]{1,0:T(8,128)(2,1)S(1)} %collective-permute-done.2.refs_1_, f32[1,1024]{1,0:T(1,128)S(1)} %pause.1.refs_2_, ...), custom_call_target="tpu_custom_call" | custom-call | flops 10000000000 | tf_op jit(solution)/shard_map/first_far/pallas_call | solution.py:48
  12.8 0.1 collective-permute-start.4
  12.9 0.0 slice-start.4
  12.9 1.4 %next_far.1 = (bf16[64,1792]{1,0:T(8,128)(2,1)S(1)}, bf16[64,1792]{1,0:T(8,128)(2,1)S(1)}) custom-call(bf16[64,1024]{1,0:T(8,128)(2,1)S(1)} %get-tuple-element.25.refs_0_.refs_1_, bf16[1,1024,3584]{2,1,0:T(8,128)(2,1)S(1)} %bitcast.16, bf16[1,1024,3584]{2,1,0:T(8,128)(2,1)S(1)} %bitcast.18, bf16[64,1920]{1,0:T(8,128)(2,1)S(1)} %get-tuple-element.26.refs_3_), custom_call_target="tpu_custom_call" | custom-call | flops 10000000000 | tf_op jit(solution)/shard_map/next_far/pallas_call | solution.py:48
  14.3 0.5 %collective-permute-start.11 = (bf16[64,1792]{1,0:T(8,128)(2,1)S(1)}, bf16[64,1792]{1,0:T(8,128)(2,1)S(1)}, u32[]{:S(2)}, u32[]{:S(2)}) collective-permute-start(bf16[64,1792]{1,0:T(8,128)(2,1)S(1)} %get-tuple-element.34), channel_id=1, source_target_pairs={{0,1},{1,0},{2,3},{3,2},{4,5},{5,4},{6,7},{7,6},{8,9},{9,8},{10,11... | collective-permute-start | bytes 688136 | tf_op jit(solution)/shard_map/ppermute | solution.py:27
  14.8 0.2 joined_far.1.refs_4_
  15.0 1.6 %collective-permute-start.12 = (bf16[64,1920]{1,0:T(8,128)(2,1)S(1)}, bf16[64,1920]{1,0:T(8,128)(2,1)S(1)}, u32[]{:S(2)}, u32[]{:S(2)}) collective-permute-start(bf16[64,1920]{1,0:T(8,128)(2,1)S(1)} %joined_far.1.refs_4_), channel_id=1, source_target_pairs={{0,2},{1,3},{2,0},{3,1},{4,6},{5,7},{6,4},{7,5},{8,10},{9,11},{10,... | collective-permute-start | bytes 737288 | tf_op jit(solution)/shard_map/ppermute | solution.py:27
  16.5 0.7 %product0.1 = (f32[64,1792]{1,0:T(8,128)S(1)}, f32[64,1792]{1,0:T(8,128)S(1)}) custom-call(bf16[64,1024]{1,0:T(8,128)(2,1)S(1)} %get-tuple-element.21.refs_0_, bf16[64,1024]{1,0:T(8,128)(2,1)S(1)} %get-tuple-element.25.refs_0_.refs_1_, bf16[1,1024,3584]{2,1,0:T(8,128)(2,1)S(1)} %bitcast.16, bf16[1,1024,3584]{2,1,0:T(8,128)(2,1)S(1)} %bitcast.18, ...), custom_call_target="tpu_custom_call" | custom-call | flops 100000000 | tf_op jit(solution)/shard_map/product0/pallas_call | solution.py:48
  17.3 0.1 collective-permute-done.6.refs_3_
  17.4 0.9 %activate_near.1 = (bf16[64,896]{1,0:T(8,128)(2,1)S(1)}, bf16[2,64,1024]{2,1,0:T(8,128)(2,1)S(1)}) custom-call(f32[64,1792]{1,0:T(8,128)S(1)} %get-tuple-element.29.refs_0_, bf16[64,1792]{1,0:T(8,128)(2,1)S(1)} %collective-permute-done.5.refs_1_, bf16[64,128]{1,0:T(8,128)(2,1)S(1)} %get-tuple-element.23.refs_1_.refs_2_, ...), custom_call_target="tpu_custom_call" | custom-call | flops 10000000000 | tf_op jit(solution)/shard_map/activate_near/pallas_call | solution.py:48
  18.3 0.1 collective-permute-start.7
  18.3 0.8 %down_near.1 = bf16[2,64,1024]{2,1,0:T(8,128)(2,1)S(1)} custom-call(bf16[64,896]{1,0:T(8,128)(2,1)S(1)} %get-tuple-element.31.refs_0_, bf16[1,896,4096]{2,1,0:T(8,128)(2,1)S(1)} %bitcast.20, bf16[2,64,1024]{2,1,0:T(8,128)(2,1)S(1)} %get-tuple-element.32.refs_2_), custom_call_target="tpu_custom_call" | custom-call | flops 10000000000 | tf_op jit(solution)/shard_map/down_near/pallas_call | solution.py:48
  19.1 0.7 %collective-permute-done.7 = bf16[2,64,1024]{2,1,0:T(8,128)(2,1)S(1)} collective-permute-done((bf16[2,64,1024]{2,1,0:T(8,128)(2,1)S(1)}, bf16[2,64,1024]{2,1,0:T(8,128)(2,1)S(1)}, u32[]{:S(2)}, u32[]{:S(2)}) %collective-permute-start.7) | collective-permute-done | bytes 262176 | tf_op jit(solution)/shard_map/ppermute | solution.py:27
  19.9 0.1 add_convert_fusion.refs_6_
  20.0 1.8 %collective-permute-start.8 = (bf16[64,1024]{1,0:T(8,128)(2,1)S(1)}, bf16[64,1024]{1,0:T(8,128)(2,1)S(1)}, u32[]{:S(2)}, u32[]{:S(2)}) collective-permute-start(bf16[64,1024]{1,0:T(8,128)(2,1)S(1)} %slice_bitcast_fusion), channel_id=1, source_target_pairs={{0,2},{1,3},{2,0},{3,1},{4,6},{5,7},{6,4},{7,5},{8,10},{9,11},{10,... | collective-permute-start | bytes 393224 | tf_op jit(solution)/shard_map/ppermute | solution.py:27
  21.8 0.0 collective-permute-done.11.refs_1_
  21.8 1.3 %collective-permute-done.12.refs_3_ = bf16[64,1920]{1,0:T(8,128)(2,1)S(1)} collective-permute-done((bf16[64,1920]{1,0:T(8,128)(2,1)S(1)}, bf16[64,1920]{1,0:T(8,128)(2,1)S(1)}, u32[]{:S(2)}, u32[]{:S(2)}) %collective-permute-start.12) | collective-permute-done | bytes 245792 | tf_op jit(solution)/shard_map/ppermute | solution.py:27
  23.1 0.9 %activate_far.1 = (bf16[64,896]{1,0:T(8,128)(2,1)S(1)}, bf16[2,64,1024]{2,1,0:T(8,128)(2,1)S(1)}) custom-call(f32[64,1792]{1,0:T(8,128)S(1)} %get-tuple-element.33.refs_0_, bf16[64,1792]{1,0:T(8,128)(2,1)S(1)} %collective-permute-done.11.refs_1_, bf16[64,128]{1,0:T(8,128)(2,1)S(1)} %get-tuple-element.28.refs_1_.refs_2_, ...), custom_call_target="tpu_custom_call" | custom-call | flops 10000000000 | tf_op jit(solution)/shard_map/activate_far/pallas_call | solution.py:48
  23.9 0.1 collective-permute-start.13
  24.0 0.8 %down_far.1.refs_0_ = bf16[2,64,1024]{2,1,0:T(8,128)(2,1)S(1)} custom-call(bf16[64,896]{1,0:T(8,128)(2,1)S(1)} %get-tuple-element.35.refs_0_, bf16[1,896,4096]{2,1,0:T(8,128)(2,1)S(1)} %bitcast.20, bf16[2,64,1024]{2,1,0:T(8,128)(2,1)S(1)} %get-tuple-element.36.refs_2_), custom_call_target="tpu_custom_call" | custom-call | flops 100000000 | tf_op jit(solution)/shard_map/down_far/pallas_call | solution.py:48
  24.8 1.0 %collective-permute-done.8 = bf16[64,1024]{1,0:T(8,128)(2,1)S(1)} collective-permute-done((bf16[64,1024]{1,0:T(8,128)(2,1)S(1)}, bf16[64,1024]{1,0:T(8,128)(2,1)S(1)}, u32[]{:S(2)}, u32[]{:S(2)}) %collective-permute-start.8) | collective-permute-done | bytes 131104 | tf_op jit(solution)/shard_map/ppermute | solution.py:27
  25.8 0.0 collective-permute-done.13.refs_1_
  25.8 0.1 sum_far.1
  25.9 2.4 %collective-permute-start.14 = (bf16[2,32,1024]{2,1,0:T(8,128)(2,1)S(1)}, bf16[2,32,1024]{2,1,0:T(8,128)(2,1)S(1)}, u32[]{:S(2)}, u32[]{:S(2)}) collective-permute-start(bf16[2,32,1024]{2,1,0:T(8,128)(2,1)S(1)} %slice.37), channel_id=1, source_target_pairs={{0,4},{4,0},{8,12},{12,8},{1,5},{5,1},{9,13},{13,9},{2,6},{6,2},{1... | collective-permute-start | bytes 393224 | tf_op jit(solution)/shard_map/ppermute | solution.py:27
  28.3 1.6 %collective-permute-start.9 = (bf16[32,1024]{1,0:T(8,128)(2,1)S(1)}, bf16[32,1024]{1,0:T(8,128)(2,1)S(1)}, u32[]{:S(2)}, u32[]{:S(2)}) collective-permute-start(bf16[32,1024]{1,0:T(8,128)(2,1)S(1)} %add_convert_fusion.3), channel_id=1, source_target_pairs={{0,16},{4,20},{8,24},{12,28},{16,0},{20,4},{24,8},{28,12},{1,17},{... | collective-permute-start | bytes 196616 | tf_op jit(solution)/shard_map/ppermute | solution.py:212
  29.9 1.4 %collective-permute-done.14 = bf16[2,32,1024]{2,1,0:T(8,128)(2,1)S(1)} collective-permute-done((bf16[2,32,1024]{2,1,0:T(8,128)(2,1)S(1)}, bf16[2,32,1024]{2,1,0:T(8,128)(2,1)S(1)}, u32[]{:S(2)}, u32[]{:S(2)}) %collective-permute-start.14) | collective-permute-done | bytes 131104 | tf_op jit(solution)/shard_map/ppermute | solution.py:27
  31.3 1.8 %collective-permute-start.15 = (bf16[32,1024]{1,0:T(8,128)(2,1)S(1)}, bf16[32,1024]{1,0:T(8,128)(2,1)S(1)}, u32[]{:S(2)}, u32[]{:S(2)}) collective-permute-start(bf16[32,1024]{1,0:T(8,128)(2,1)S(1)} %get-tuple-element.37), channel_id=1, source_target_pairs={{0,2},{1,3},{2,0},{3,1},{4,6},{5,7},{6,4},{7,5},{8,10},{9,11},{10,... | collective-permute-start | bytes 196616 | tf_op jit(solution)/shard_map/ppermute | solution.py:27
  33.1 2.9 %collective-permute-start.10 = (bf16[32,1024]{1,0:T(8,128)(2,1)S(1)}, bf16[32,1024]{1,0:T(8,128)(2,1)S(1)}, u32[]{:S(2)}, u32[]{:S(2)}) collective-permute-start(bf16[32,1024]{1,0:T(8,128)(2,1)S(1)} %slice.35), channel_id=1, source_target_pairs={{0,20},{4,16},{8,28},{12,24},{16,4},{20,0},{24,12},{28,8},{1,21},{... | collective-permute-start | bytes 196616 | tf_op jit(solution)/shard_map/ppermute | solution.py:212
  36.1 0.0 collective-permute-done.9.refs_2_
  36.1 0.0 collective-permute-done.15.refs_1_
  36.1 3.6 %collective-permute-start.16 = (bf16[32,1024]{1,0:T(8,128)(2,1)S(1)}, bf16[32,1024]{1,0:T(8,128)(2,1)S(1)}, u32[]{:S(2)}, u32[]{:S(2)}) collective-permute-start(bf16[32,1024]{1,0:T(8,128)(2,1)S(1)} %sum_over_x.1), channel_id=1, source_target_pairs={{0,24},{4,28},{8,16},{12,20},{16,8},{20,12},{24,0},{28,4},{1,25},{... | collective-permute-start | bytes 196616 | tf_op jit(solution)/shard_map/ppermute | solution.py:212
  39.7 0.0 collective-permute-done.10
  39.7 2.5 %collective-permute-done.16 = bf16[32,1024]{1,0:T(8,128)(2,1)S(1)} collective-permute-done((bf16[32,1024]{1,0:T(8,128)(2,1)S(1)}, bf16[32,1024]{1,0:T(8,128)(2,1)S(1)}, u32[]{:S(2)}, u32[]{:S(2)}) %collective-permute-start.16) | collective-permute-done | bytes 65568 | tf_op jit(solution)/shard_map/ppermute | solution.py:212
  42.2 0.7 %fusion.1 = bf16[1,32,1024]{2,1,0:T(8,128)(2,1)} fusion(bf16[32,1024]{1,0:T(8,128)(2,1)S(1)} %collective-permute-done.16, bf16[32,1024]{1,0:T(8,128)(2,1)S(1)} %collective-permute-done.10, bf16[32,1024]{1,0:T(8,128)(2,1)S(1)} %collective-permute-done.9.refs_2_), kind=kLoop, calls=%fused_computation.8 | loop fusion | flops 196608 | bytes 262144 | tf_op jit(solution)/shard_map/broadcast_in_dim | solution.py:218
  (28 shorter events, 0.2 us)
Async XLA Ops:
  0.0 6.4 %slice-start = ((s8[7340032]{0:T(1024)(128)(4,1)}), s8[4194304]{0:T(1024)(128)(4,1)S(1)}, s32[]{:S(2)}) async-start(s8[7340032]{0:T(1024)(128)(4,1)} %bitcast.15), calls=%async_computation | async-start | bytes 8388608
  0.0 6.4 %slice-start.2 = ((s8[7340032]{0:T(1024)(128)(4,1)}), s8[4194304]{0:T(1024)(128)(4,1)S(1)}, s32[]{:S(2)}) async-start(s8[7340032]{0:T(1024)(128)(4,1)} %bitcast.17), calls=%async_computation.2 | async-start | bytes 8388608
  0.0 6.4 %slice-start.1 = ((s8[7340032]{0:T(1024)(128)(4,1)}), s8[3145728]{0:T(1024)(128)(4,1)S(1)}, s32[]{:S(2)}) async-start(s8[7340032]{0:T(1024)(128)(4,1)} %bitcast.15), calls=%async_computation.1 | async-start | bytes 6291456
  0.0 6.4 %slice-start.3 = ((s8[7340032]{0:T(1024)(128)(4,1)}), s8[3145728]{0:T(1024)(128)(4,1)S(1)}, s32[]{:S(2)}) async-start(s8[7340032]{0:T(1024)(128)(4,1)} %bitcast.17), calls=%async_computation.3 | async-start | bytes 6291456
  0.0 6.4 %copy-start = (bf16[1,32,1024]{2,1,0:T(8,128)(2,1)S(1)}, bf16[1,32,1024]{2,1,0:T(8,128)(2,1)}, u32[]{:S(2)}) copy-start(bf16[1,32,1024]{2,1,0:T(8,128)(2,1)} %param.5) | copy-start | bytes 196612
  0.0 6.4 %collective-permute-start = (bf16[32,1024]{1,0:T(8,128)(2,1)}, bf16[32,1024]{1,0:T(8,128)(2,1)S(1)}, u32[]{:S(2)}, u32[]{:S(2)}) collective-permute-start(bf16[32,1024]{1,0:T(8,128)(2,1)} %bitcast.21), channel_id=1, source_target_pairs={{0,4},{4,0},{8,12},{12,8},{1,5},{5,1},{9,13},{13,9},{2,6},{6,2},{1... | collective-permute-start | bytes 196616 | tf_op jit(solution)/shard_map/ppermute | solution.py:27
  3.1 8.1 %collective-permute-start.1 = (bf16[32,1024]{1,0:T(8,128)(2,1)}, bf16[32,1024]{1,0:T(8,128)(2,1)S(1)}, u32[]{:S(2)}, u32[]{:S(2)}) collective-permute-start(bf16[32,1024]{1,0:T(8,128)(2,1)} %bitcast.22), channel_id=1, source_target_pairs={{0,8},{4,12},{8,0},{12,4},{1,9},{5,13},{9,1},{13,5},{2,10},{6,14},... | collective-permute-start | bytes 196616 | tf_op jit(solution)/shard_map/ppermute | solution.py:27
  5.7 6.3 %collective-permute-start.2 = (bf16[32,1024]{1,0:T(8,128)(2,1)}, bf16[32,1024]{1,0:T(8,128)(2,1)S(1)}, u32[]{:S(2)}, u32[]{:S(2)}) collective-permute-start(bf16[32,1024]{1,0:T(8,128)(2,1)} %bitcast.23), channel_id=1, source_target_pairs={{0,12},{4,8},{8,4},{12,0},{1,13},{5,9},{9,5},{13,1},{2,14},{6,10},... | collective-permute-start | bytes 196616 | tf_op jit(solution)/shard_map/ppermute | solution.py:27
  5.7 0.7 %copy-start.1 = (f32[1,1024]{1,0:T(1,128)S(1)}, f32[1,1024]{1,0:T(1,128)}, u32[]{:S(2)}) copy-start(f32[1,1024]{1,0:T(1,128)} %refs_0_.1) | copy-start | bytes 12292
  7.2 2.0 %collective-permute-start.3 = (bf16[64,1920]{1,0:T(8,128)(2,1)S(1)}, bf16[64,1920]{1,0:T(8,128)(2,1)S(1)}, u32[]{:S(2)}, u32[]{:S(2)}) collective-permute-start(bf16[64,1920]{1,0:T(8,128)(2,1)S(1)} %get-tuple-element.24), channel_id=1, source_target_pairs={{0,1},{1,0},{2,3},{3,2},{4,5},{5,4},{6,7},{7,6},{8,9},{9,8},{10,11... | collective-permute-start | bytes 737288 | tf_op jit(solution)/shard_map/ppermute | solution.py:27
  8.7 8.6 %collective-permute-start.5 = (bf16[64,1792]{1,0:T(8,128)(2,1)S(1)}, bf16[64,1792]{1,0:T(8,128)(2,1)S(1)}, u32[]{:S(2)}, u32[]{:S(2)}) collective-permute-start(bf16[64,1792]{1,0:T(8,128)(2,1)S(1)} %get-tuple-element.30), channel_id=1, source_target_pairs={{0,1},{1,0},{2,3},{3,2},{4,5},{5,4},{6,7},{7,6},{8,9},{9,8},{10,11... | collective-permute-start | bytes 688136 | tf_op jit(solution)/shard_map/ppermute | solution.py:27
  9.4 8.0 %collective-permute-start.6 = (bf16[64,1920]{1,0:T(8,128)(2,1)S(1)}, bf16[64,1920]{1,0:T(8,128)(2,1)S(1)}, u32[]{:S(2)}, u32[]{:S(2)}) collective-permute-start(bf16[64,1920]{1,0:T(8,128)(2,1)S(1)} %joined_near.1.refs_5_), channel_id=1, source_target_pairs={{0,2},{1,3},{2,0},{3,1},{4,6},{5,7},{6,4},{7,5},{8,10},{9,11},{10,... | collective-permute-start | bytes 737288 | tf_op jit(solution)/shard_map/ppermute | solution.py:27
  12.8 2.0 %collective-permute-start.4 = (bf16[64,1920]{1,0:T(8,128)(2,1)S(1)}, bf16[64,1920]{1,0:T(8,128)(2,1)S(1)}, u32[]{:S(2)}, u32[]{:S(2)}) collective-permute-start(bf16[64,1920]{1,0:T(8,128)(2,1)S(1)} %get-tuple-element.26.refs_3_), channel_id=1, source_target_pairs={{0,1},{1,0},{2,3},{3,2},{4,5},{5,4},{6,7},{7,6},{8,9},{9,8},{10,11... | collective-permute-start | bytes 737288 | tf_op jit(solution)/shard_map/ppermute | solution.py:27
  12.9 4.5 %slice-start.4 = ((s8[7340032]{0:T(1024)(128)(4,1)}), s8[4194304]{0:T(1024)(128)(4,1)S(1)}, s32[]{:S(2)}) async-start(s8[7340032]{0:T(1024)(128)(4,1)} %bitcast.19), calls=%async_computation.4 | async-start | bytes 8388608
  14.3 7.5 %collective-permute-start.11 = (bf16[64,1792]{1,0:T(8,128)(2,1)S(1)}, bf16[64,1792]{1,0:T(8,128)(2,1)S(1)}, u32[]{:S(2)}, u32[]{:S(2)}) collective-permute-start(bf16[64,1792]{1,0:T(8,128)(2,1)S(1)} %get-tuple-element.34), channel_id=1, source_target_pairs={{0,1},{1,0},{2,3},{3,2},{4,5},{5,4},{6,7},{7,6},{8,9},{9,8},{10,11... | collective-permute-start | bytes 688136 | tf_op jit(solution)/shard_map/ppermute | solution.py:27
  14.8 2.6 %slice-start.5 = ((s8[7340032]{0:T(1024)(128)(4,1)}), s8[3145728]{0:T(1024)(128)(4,1)S(1)}, s32[]{:S(2)}) async-start(s8[7340032]{0:T(1024)(128)(4,1)} %bitcast.19), calls=%async_computation.5 | async-start | bytes 6291456
  15.0 8.1 %collective-permute-start.12 = (bf16[64,1920]{1,0:T(8,128)(2,1)S(1)}, bf16[64,1920]{1,0:T(8,128)(2,1)S(1)}, u32[]{:S(2)}, u32[]{:S(2)}) collective-permute-start(bf16[64,1920]{1,0:T(8,128)(2,1)S(1)} %joined_far.1.refs_4_), channel_id=1, source_target_pairs={{0,2},{1,3},{2,0},{3,1},{4,6},{5,7},{6,4},{7,5},{8,10},{9,11},{10,... | collective-permute-start | bytes 737288 | tf_op jit(solution)/shard_map/ppermute | solution.py:27
  18.3 1.6 %collective-permute-start.7 = (bf16[2,64,1024]{2,1,0:T(8,128)(2,1)S(1)}, bf16[2,64,1024]{2,1,0:T(8,128)(2,1)S(1)}, u32[]{:S(2)}, u32[]{:S(2)}) collective-permute-start(bf16[2,64,1024]{2,1,0:T(8,128)(2,1)S(1)} %get-tuple-element.32.refs_2_), channel_id=1, source_target_pairs={{0,1},{1,0},{2,3},{3,2},{4,5},{5,4},{6,7},{7,6},{8,9},{9,8},{10,11... | collective-permute-start | bytes 786440 | tf_op jit(solution)/shard_map/ppermute | solution.py:27
  20.0 5.8 %collective-permute-start.8 = (bf16[64,1024]{1,0:T(8,128)(2,1)S(1)}, bf16[64,1024]{1,0:T(8,128)(2,1)S(1)}, u32[]{:S(2)}, u32[]{:S(2)}) collective-permute-start(bf16[64,1024]{1,0:T(8,128)(2,1)S(1)} %slice_bitcast_fusion), channel_id=1, source_target_pairs={{0,2},{1,3},{2,0},{3,1},{4,6},{5,7},{6,4},{7,5},{8,10},{9,11},{10,... | collective-permute-start | bytes 393224 | tf_op jit(solution)/shard_map/ppermute | solution.py:27
  23.9 1.9 %collective-permute-start.13 = (bf16[2,64,1024]{2,1,0:T(8,128)(2,1)S(1)}, bf16[2,64,1024]{2,1,0:T(8,128)(2,1)S(1)}, u32[]{:S(2)}, u32[]{:S(2)}) collective-permute-start(bf16[2,64,1024]{2,1,0:T(8,128)(2,1)S(1)} %get-tuple-element.36.refs_2_), channel_id=1, source_target_pairs={{0,1},{1,0},{2,3},{3,2},{4,5},{5,4},{6,7},{7,6},{8,9},{9,8},{10,11... | collective-permute-start | bytes 786440 | tf_op jit(solution)/shard_map/ppermute | solution.py:27
  25.9 5.4 %collective-permute-start.14 = (bf16[2,32,1024]{2,1,0:T(8,128)(2,1)S(1)}, bf16[2,32,1024]{2,1,0:T(8,128)(2,1)S(1)}, u32[]{:S(2)}, u32[]{:S(2)}) collective-permute-start(bf16[2,32,1024]{2,1,0:T(8,128)(2,1)S(1)} %slice.37), channel_id=1, source_target_pairs={{0,4},{4,0},{8,12},{12,8},{1,5},{5,1},{9,13},{13,9},{2,6},{6,2},{1... | collective-permute-start | bytes 393224 | tf_op jit(solution)/shard_map/ppermute | solution.py:27
  28.3 7.8 %collective-permute-start.9 = (bf16[32,1024]{1,0:T(8,128)(2,1)S(1)}, bf16[32,1024]{1,0:T(8,128)(2,1)S(1)}, u32[]{:S(2)}, u32[]{:S(2)}) collective-permute-start(bf16[32,1024]{1,0:T(8,128)(2,1)S(1)} %add_convert_fusion.3), channel_id=1, source_target_pairs={{0,16},{4,20},{8,24},{12,28},{16,0},{20,4},{24,8},{28,12},{1,17},{... | collective-permute-start | bytes 196616 | tf_op jit(solution)/shard_map/ppermute | solution.py:212
  31.3 4.7 %collective-permute-start.15 = (bf16[32,1024]{1,0:T(8,128)(2,1)S(1)}, bf16[32,1024]{1,0:T(8,128)(2,1)S(1)}, u32[]{:S(2)}, u32[]{:S(2)}) collective-permute-start(bf16[32,1024]{1,0:T(8,128)(2,1)S(1)} %get-tuple-element.37), channel_id=1, source_target_pairs={{0,2},{1,3},{2,0},{3,1},{4,6},{5,7},{6,4},{7,5},{8,10},{9,11},{10,... | collective-permute-start | bytes 196616 | tf_op jit(solution)/shard_map/ppermute | solution.py:27
  33.1 6.6 %collective-permute-start.10 = (bf16[32,1024]{1,0:T(8,128)(2,1)S(1)}, bf16[32,1024]{1,0:T(8,128)(2,1)S(1)}, u32[]{:S(2)}, u32[]{:S(2)}) collective-permute-start(bf16[32,1024]{1,0:T(8,128)(2,1)S(1)} %slice.35), channel_id=1, source_target_pairs={{0,20},{4,16},{8,28},{12,24},{16,4},{20,0},{24,12},{28,8},{1,21},{... | collective-permute-start | bytes 196616 | tf_op jit(solution)/shard_map/ppermute | solution.py:212
  36.1 6.1 %collective-permute-start.16 = (bf16[32,1024]{1,0:T(8,128)(2,1)S(1)}, bf16[32,1024]{1,0:T(8,128)(2,1)S(1)}, u32[]{:S(2)}, u32[]{:S(2)}) collective-permute-start(bf16[32,1024]{1,0:T(8,128)(2,1)S(1)} %sum_over_x.1), channel_id=1, source_target_pairs={{0,24},{4,28},{8,16},{12,20},{16,8},{20,12},{24,0},{28,4},{1,25},{... | collective-permute-start | bytes 196616 | tf_op jit(solution)/shard_map/ppermute | solution.py:212

commit v4 on v3

--- a/solution.py
+++ b/solution.py
@@ -154,6 +154,16 @@
     out[...] = added(a_ref[...], b_ref[...])
 
 
+def sum_over_rows(both_ref, other_ref, out):
+    out[...] = added(both_ref[:, : out.shape[1]], other_ref[...])
+
+
+def near_sums(u_ref, other_ref, own_ref, a_out, b_out):
+    count = a_out.shape[0]
+    a_out[...] = added(own_ref[...], u_ref[0, :count], other_ref[:count])
+    b_out[...] = added(u_ref[0, count:], other_ref[count:])
+
+
 def fast(tokens, norm_gain, gate_weight, up_weight, down_weight):
     rows, cols, pipes = (lax.axis_size(a) for a in ("row", "col", "pipe"))
     _, count, depth = tokens.shape
@@ -203,18 +213,22 @@
         return e0, t1
 
     u = added(*hidden_and_down("near", p0n, r1n, sn, f2n, r3n, ()))
-    n = added(u[0], swapped(u[1], "col", 2))
+    un = swapped(u[1], "col", 2)
     e0f, t1f = hidden_and_down("far", p0f, r1f, sf, f2f, r3f, [u])
     (w,) = call(sum_of_two, "sum_far", [e_shape], [e0f, t1f], (), [])
+    n0, n1 = call(near_sums, "sum_near", [(own.shape, BF16)] * 2, [u, un, own], (), [w])
 
     def onward(value, k):
         pairs = [(p * rows + r, q * rows + (r ^ k)) for p, q in forward for r in range(rows)]
         return lax.ppermute(value, ("pipe", "row"), pairs)
 
-    own_part = onward(added(own, n[:count]), 0)
-    near_part = onward(n[count:], 1)
-    w = added(w[:, :count], swapped(w[:, count:], "row", 1))
-    (w,) = call(sum_of_two, "sum_over_x", [(own.shape, BF16)], [w[0], swapped(w[1], "col", 2)], (), [own_part])
+    own_part = onward(n0, 0)
+    near_part = onward(n1, 1)
+    (w,) = call(
+        sum_over_rows, "sum_over_rows", [((2, *own.shape), BF16)],
+        [w, swapped(w[:, count:], "row", 1)], (), [],
+    )
+    (w,) = call(sum_of_two, "sum_over_x", [(own.shape, BF16)], [w[0], swapped(w[1], "col", 2)], (), [])
     return added(own_part, near_part, onward(w, 2))[None]
 
 

time: 43.1 us -> 42.8 us (level)
  starting transfers between devices: 24.5 us -> 21.8 us
  waiting for transfers between devices: 7.89 us -> 10.4 us
    ppermute x14, waiting for transfers between devices: 5.36 us -> 7.84 us  [swapped(): return lax.ppermute(value, axis, [(i, i ^ mask) for i in range(count)])]
    ppermute x3, starting transfers between devices: 8.12 us -> 6.66 us  [onward(): return lax.ppermute(value, ('pipe', 'row'), pairs)]
    ppermute x14, starting transfers between devices: 16.4 us -> 15.1 us  [swapped(): return lax.ppermute(value, axis, [(i, i ^ mask) for i in range(count)])]
    pallas_call x14 -> x16, Pallas kernels: 8.68 us -> 8.76 us  [call(): pl.pallas_call(run, name=name, in_specs=[pl.BlockSpec(memory_space=s) for...]
  transfers between devices with their start and end apart: 17 -> 17, of which waited for: 7 -> 8; matrix products, arithmetic and copies ran while one was open for 0% -> 0% of each run, Pallas kernels for 20% -> 18%
where the time goes in v4:
time: 42.8 us; the launch traced here: 42.6 us
  starting transfers between devices  21.8 us (51%)
  waiting for transfers between devices  10.4 us (24%)
  Pallas kernels  8.76 us (20%)
  local copies, waits for them, and re-layouts  0.75 us (2%)
  other arithmetic  0.72 us (2%)
    ppermute x14, starting transfers between devices, swapped(): return lax.ppermute(value, axis, [(i, i ^ mask) for i in range(count)])  15.1 us
    pallas_call x16, Pallas kernels, call(): pl.pallas_call(run, name=name, in_specs=[pl.BlockSpec(memory_space=s) for...  8.76 us
    ppermute x14, waiting for transfers between devices, swapped(): return lax.ppermute(value, axis, [(i, i ^ mask) for i in range(count)])  7.84 us
    ppermute x3, starting transfers between devices, onward(): return lax.ppermute(value, ('pipe', 'row'), pairs)  6.66 us
    ppermute x3, waiting for transfers between devices, onward(): return lax.ppermute(value, ('pipe', 'row'), pairs)  2.53 us
  transfers between devices with their start and end apart: 17, of which 8 were waited for; matrix products, arithmetic and copies ran while one was open for 0% of the time, Pallas kernels for 18%

profile of v4, /device:TPU:0, one launch (start us, length us, event | category | flops | bytes accessed | tf_op | source)
XLA Modules:
  0.0 42.6 jit_solution(8403597902434152754)
XLA Ops:
  0.0 3.1 %collective-permute-start = (bf16[32,1024]{1,0:T(8,128)(2,1)}, bf16[32,1024]{1,0:T(8,128)(2,1)S(1)}, u32[]{:S(2)}, u32[]{:S(2)}) collective-permute-start(bf16[32,1024]{1,0:T(8,128)(2,1)} %bitcast.15), channel_id=1, source_target_pairs={{0,4},{4,0},{8,12},{12,8},{1,5},{5,1},{9,13},{13,9},{2,6},{6,2},{1... | collective-permute-start | bytes 196616 | tf_op jit(solution)/shard_map/ppermute | solution.py:27
  3.1 2.6 %collective-permute-start.1 = (bf16[32,1024]{1,0:T(8,128)(2,1)}, bf16[32,1024]{1,0:T(8,128)(2,1)S(1)}, u32[]{:S(2)}, u32[]{:S(2)}) collective-permute-start(bf16[32,1024]{1,0:T(8,128)(2,1)} %bitcast.16), channel_id=1, source_target_pairs={{0,8},{4,12},{8,0},{12,4},{1,9},{5,13},{9,1},{13,5},{2,10},{6,14},... | collective-permute-start | bytes 196616 | tf_op jit(solution)/shard_map/ppermute | solution.py:27
  5.7 0.0 collective-permute-start.2
  5.7 0.7 %copy-done.1 = f32[1,1024]{1,0:T(1,128)S(1)} copy-done((f32[1,1024]{1,0:T(1,128)S(1)}, f32[1,1024]{1,0:T(1,128)}, u32[]{:S(2)}) %copy-start.1) | copy-done | bytes 4120
  6.4 0.0 collective-permute-done.refs_1_
  6.5 0.8 %first_near.1 = (bf16[64,1024]{1,0:T(8,128)(2,1)S(1)}, bf16[64,128]{1,0:T(8,128)(2,1)S(1)}, bf16[64,1920]{1,0:T(8,128)(2,1)S(1)}) custom-call(bf16[32,1024]{1,0:T(8,128)(2,1)S(1)} %bitcast.18, bf16[32,1024]{1,0:T(8,128)(2,1)S(1)} %collective-permute-done.refs_1_, f32[1,1024]{1,0:T(1,128)S(1)} %pause.1.refs_2_, bf16[1,1024,3584]{2,1,0:T(8,128)(2,1)S(1)} %bitcast.10, ...), custom_call_target="tpu_custom_call" | custom-call | flops 10000000000 | tf_op jit(solution)/shard_map/first_near/pallas_call | solution.py:48
  7.2 0.1 collective-permute-start.3
  7.3 1.4 %next_near.1 = (bf16[64,1792]{1,0:T(8,128)(2,1)S(1)}, bf16[64,1792]{1,0:T(8,128)(2,1)S(1)}) custom-call(bf16[64,1024]{1,0:T(8,128)(2,1)S(1)} %get-tuple-element.23.refs_0_, bf16[1,1024,3584]{2,1,0:T(8,128)(2,1)S(1)} %bitcast.10, bf16[1,1024,3584]{2,1,0:T(8,128)(2,1)S(1)} %bitcast.12), custom_call_target="tpu_custom_call" | custom-call | flops 10000000000 | tf_op jit(solution)/shard_map/next_near/pallas_call | solution.py:48
  8.7 0.5 %collective-permute-start.5 = (bf16[64,1792]{1,0:T(8,128)(2,1)S(1)}, bf16[64,1792]{1,0:T(8,128)(2,1)S(1)}, u32[]{:S(2)}, u32[]{:S(2)}) collective-permute-start(bf16[64,1792]{1,0:T(8,128)(2,1)S(1)} %get-tuple-element.32), channel_id=1, source_target_pairs={{0,1},{1,0},{2,3},{3,2},{4,5},{5,4},{6,7},{7,6},{8,9},{9,8},{10,11... | collective-permute-start | bytes 688136 | tf_op jit(solution)/shard_map/ppermute | solution.py:27
  9.2 0.0 collective-permute-done.3.refs_2_.refs_4_
  9.2 0.2 joined_near.1.refs_5_
  9.4 1.8 %collective-permute-start.6 = (bf16[64,1920]{1,0:T(8,128)(2,1)S(1)}, bf16[64,1920]{1,0:T(8,128)(2,1)S(1)}, u32[]{:S(2)}, u32[]{:S(2)}) collective-permute-start(bf16[64,1920]{1,0:T(8,128)(2,1)S(1)} %joined_near.1.refs_5_), channel_id=1, source_target_pairs={{0,2},{1,3},{2,0},{3,1},{4,6},{5,7},{6,4},{7,5},{8,10},{9,11},{10,... | collective-permute-start | bytes 737288 | tf_op jit(solution)/shard_map/ppermute | solution.py:27
  11.2 0.0 collective-permute-done.1.refs_0_
  11.2 0.8 %collective-permute-done.2.refs_1_ = bf16[32,1024]{1,0:T(8,128)(2,1)S(1)} collective-permute-done((bf16[32,1024]{1,0:T(8,128)(2,1)}, bf16[32,1024]{1,0:T(8,128)(2,1)S(1)}, u32[]{:S(2)}, u32[]{:S(2)}) %collective-permute-start.2) | collective-permute-done | bytes 65568 | tf_op jit(solution)/shard_map/ppermute | solution.py:27
  12.0 0.8 %first_far.1 = (bf16[64,1024]{1,0:T(8,128)(2,1)S(1)}, bf16[64,128]{1,0:T(8,128)(2,1)S(1)}, bf16[64,1920]{1,0:T(8,128)(2,1)S(1)}) custom-call(bf16[32,1024]{1,0:T(8,128)(2,1)S(1)} %collective-permute-done.1.refs_0_, bf16[32,1024]{1,0:T(8,128)(2,1)S(1)} %collective-permute-done.2.refs_1_, f32[1,1024]{1,0:T(1,128)S(1)} %pause.1.refs_2_, ...), custom_call_target="tpu_custom_call" | custom-call | flops 10000000000 | tf_op jit(solution)/shard_map/first_far/pallas_call | solution.py:48
  12.8 0.1 collective-permute-start.4
  12.9 0.0 slice-start.4
  12.9 1.4 %next_far.1 = (bf16[64,1792]{1,0:T(8,128)(2,1)S(1)}, bf16[64,1792]{1,0:T(8,128)(2,1)S(1)}) custom-call(bf16[64,1024]{1,0:T(8,128)(2,1)S(1)} %get-tuple-element.27.refs_0_.refs_1_, bf16[1,1024,3584]{2,1,0:T(8,128)(2,1)S(1)} %bitcast.10, bf16[1,1024,3584]{2,1,0:T(8,128)(2,1)S(1)} %bitcast.12, bf16[64,1920]{1,0:T(8,128)(2,1)S(1)} %get-tuple-element.28.refs_3_), custom_call_target="tpu_custom_call" | custom-call | flops 10000000000 | tf_op jit(solution)/shard_map/next_far/pallas_call | solution.py:48
  14.3 0.5 %collective-permute-start.9 = (bf16[64,1792]{1,0:T(8,128)(2,1)S(1)}, bf16[64,1792]{1,0:T(8,128)(2,1)S(1)}, u32[]{:S(2)}, u32[]{:S(2)}) collective-permute-start(bf16[64,1792]{1,0:T(8,128)(2,1)S(1)} %get-tuple-element.36), channel_id=1, source_target_pairs={{0,1},{1,0},{2,3},{3,2},{4,5},{5,4},{6,7},{7,6},{8,9},{9,8},{10,11... | collective-permute-start | bytes 688136 | tf_op jit(solution)/shard_map/ppermute | solution.py:27
  14.8 0.0 collective-permute-done.4.refs_2_.refs_4_
  14.8 0.2 joined_far.1.refs_4_
  15.0 1.6 %collective-permute-start.10 = (bf16[64,1920]{1,0:T(8,128)(2,1)S(1)}, bf16[64,1920]{1,0:T(8,128)(2,1)S(1)}, u32[]{:S(2)}, u32[]{:S(2)}) collective-permute-start(bf16[64,1920]{1,0:T(8,128)(2,1)S(1)} %joined_far.1.refs_4_), channel_id=1, source_target_pairs={{0,2},{1,3},{2,0},{3,1},{4,6},{5,7},{6,4},{7,5},{8,10},{9,11},{10,... | collective-permute-start | bytes 737288 | tf_op jit(solution)/shard_map/ppermute | solution.py:27
  16.5 0.7 %product0.1 = (f32[64,1792]{1,0:T(8,128)S(1)}, f32[64,1792]{1,0:T(8,128)S(1)}) custom-call(bf16[64,1024]{1,0:T(8,128)(2,1)S(1)} %get-tuple-element.23.refs_0_, bf16[64,1024]{1,0:T(8,128)(2,1)S(1)} %get-tuple-element.27.refs_0_.refs_1_, bf16[1,1024,3584]{2,1,0:T(8,128)(2,1)S(1)} %bitcast.10, bf16[1,1024,3584]{2,1,0:T(8,128)(2,1)S(1)} %bitcast.12, ...), custom_call_target="tpu_custom_call" | custom-call | flops 100000000 | tf_op jit(solution)/shard_map/product0/pallas_call | solution.py:48
  17.3 0.1 collective-permute-done.6.refs_3_
  17.4 0.9 %activate_near.1 = (bf16[64,896]{1,0:T(8,128)(2,1)S(1)}, bf16[2,64,1024]{2,1,0:T(8,128)(2,1)S(1)}) custom-call(f32[64,1792]{1,0:T(8,128)S(1)} %get-tuple-element.31.refs_0_, bf16[64,1792]{1,0:T(8,128)(2,1)S(1)} %collective-permute-done.5.refs_1_, bf16[64,128]{1,0:T(8,128)(2,1)S(1)} %get-tuple-element.25.refs_1_.refs_2_, ...), custom_call_target="tpu_custom_call" | custom-call | flops 10000000000 | tf_op jit(solution)/shard_map/activate_near/pallas_call | solution.py:48
  18.3 0.1 collective-permute-start.7
  18.3 0.8 %down_near.1 = bf16[2,64,1024]{2,1,0:T(8,128)(2,1)S(1)} custom-call(bf16[64,896]{1,0:T(8,128)(2,1)S(1)} %get-tuple-element.33.refs_0_, bf16[1,896,4096]{2,1,0:T(8,128)(2,1)S(1)} %bitcast.14, bf16[2,64,1024]{2,1,0:T(8,128)(2,1)S(1)} %get-tuple-element.34.refs_2_), custom_call_target="tpu_custom_call" | custom-call | flops 10000000000 | tf_op jit(solution)/shard_map/down_near/pallas_call | solution.py:48
  19.1 0.7 %collective-permute-done.7 = bf16[2,64,1024]{2,1,0:T(8,128)(2,1)S(1)} collective-permute-done((bf16[2,64,1024]{2,1,0:T(8,128)(2,1)S(1)}, bf16[2,64,1024]{2,1,0:T(8,128)(2,1)S(1)}, u32[]{:S(2)}, u32[]{:S(2)}) %collective-permute-start.7) | collective-permute-done | bytes 262176 | tf_op jit(solution)/shard_map/ppermute | solution.py:27
  19.9 0.1 add_convert_fusion.refs_6_.refs_0_
  19.9 0.0 collective-permute-done.9.refs_1_
  19.9 3.0 %collective-permute-done.10.refs_3_ = bf16[64,1920]{1,0:T(8,128)(2,1)S(1)} collective-permute-done((bf16[64,1920]{1,0:T(8,128)(2,1)S(1)}, bf16[64,1920]{1,0:T(8,128)(2,1)S(1)}, u32[]{:S(2)}, u32[]{:S(2)}) %collective-permute-start.10) | collective-permute-done | bytes 245792 | tf_op jit(solution)/shard_map/ppermute | solution.py:27
  23.0 0.9 %activate_far.1 = (bf16[64,896]{1,0:T(8,128)(2,1)S(1)}, bf16[2,64,1024]{2,1,0:T(8,128)(2,1)S(1)}) custom-call(f32[64,1792]{1,0:T(8,128)S(1)} %get-tuple-element.35.refs_0_, bf16[64,1792]{1,0:T(8,128)(2,1)S(1)} %collective-permute-done.9.refs_1_, bf16[64,128]{1,0:T(8,128)(2,1)S(1)} %get-tuple-element.30.refs_1_.refs_2_, ...), custom_call_target="tpu_custom_call" | custom-call | flops 10000000000 | tf_op jit(solution)/shard_map/activate_far/pallas_call | solution.py:48
  23.8 0.1 collective-permute-start.11
  23.9 0.8 %down_far.1.refs_0_ = bf16[2,64,1024]{2,1,0:T(8,128)(2,1)S(1)} custom-call(bf16[64,896]{1,0:T(8,128)(2,1)S(1)} %get-tuple-element.37.refs_0_, bf16[1,896,4096]{2,1,0:T(8,128)(2,1)S(1)} %bitcast.14, bf16[2,64,1024]{2,1,0:T(8,128)(2,1)S(1)} %get-tuple-element.38.refs_2_), custom_call_target="tpu_custom_call" | custom-call | flops 100000000 | tf_op jit(solution)/shard_map/down_far/pallas_call | solution.py:48
  24.7 0.7 %collective-permute-done.11.refs_1_ = bf16[2,64,1024]{2,1,0:T(8,128)(2,1)S(1)} collective-permute-done((bf16[2,64,1024]{2,1,0:T(8,128)(2,1)S(1)}, bf16[2,64,1024]{2,1,0:T(8,128)(2,1)S(1)}, u32[]{:S(2)}, u32[]{:S(2)}) %collective-permute-start.11) | collective-permute-done | bytes 262176 | tf_op jit(solution)/shard_map/ppermute | solution.py:27
  25.4 0.1 sum_far.1.refs_3_.refs_0_
  25.5 1.6 %collective-permute-start.14 = (bf16[2,32,1024]{2,1,0:T(8,128)(2,1)S(1)}, bf16[2,32,1024]{2,1,0:T(8,128)(2,1)S(1)}, u32[]{:S(2)}, u32[]{:S(2)}) collective-permute-start(bf16[2,32,1024]{2,1,0:T(8,128)(2,1)S(1)} %slice.17), channel_id=1, source_target_pairs={{0,4},{4,0},{8,12},{12,8},{1,5},{5,1},{9,13},{13,9},{2,6},{6,2},{1... | collective-permute-start | bytes 393224 | tf_op jit(solution)/shard_map/ppermute | solution.py:27
  27.1 1.6 %collective-permute-start.8 = (bf16[64,1024]{1,0:T(8,128)(2,1)S(1)}, bf16[64,1024]{1,0:T(8,128)(2,1)S(1)}, u32[]{:S(2)}, u32[]{:S(2)}) collective-permute-start(bf16[64,1024]{1,0:T(8,128)(2,1)S(1)} %slice_bitcast_fusion), channel_id=1, source_target_pairs={{0,2},{1,3},{2,0},{3,1},{4,6},{5,7},{6,4},{7,5},{8,10},{9,11},{10,... | collective-permute-start | bytes 393224 | tf_op jit(solution)/shard_map/ppermute | solution.py:27
  28.7 2.4 %collective-permute-done.14.refs_1_ = bf16[2,32,1024]{2,1,0:T(8,128)(2,1)S(1)} collective-permute-done((bf16[2,32,1024]{2,1,0:T(8,128)(2,1)S(1)}, bf16[2,32,1024]{2,1,0:T(8,128)(2,1)S(1)}, u32[]{:S(2)}, u32[]{:S(2)}) %collective-permute-start.14) | collective-permute-done | bytes 131104 | tf_op jit(solution)/shard_map/ppermute | solution.py:27
  31.2 1.6 %collective-permute-start.15 = (bf16[32,1024]{1,0:T(8,128)(2,1)S(1)}, bf16[32,1024]{1,0:T(8,128)(2,1)S(1)}, u32[]{:S(2)}, u32[]{:S(2)}) collective-permute-start(bf16[32,1024]{1,0:T(8,128)(2,1)S(1)} %get-tuple-element.41), channel_id=1, source_target_pairs={{0,2},{1,3},{2,0},{3,1},{4,6},{5,7},{6,4},{7,5},{8,10},{9,11},{10,... | collective-permute-start | bytes 196616 | tf_op jit(solution)/shard_map/ppermute | solution.py:27
  32.7 0.0 collective-permute-done.8.refs_1_
  32.8 2.5 %collective-permute-start.13 = (bf16[32,1024]{1,0:T(8,128)(2,1)S(1)}, bf16[32,1024]{1,0:T(8,128)(2,1)S(1)}, u32[]{:S(2)}, u32[]{:S(2)}) collective-permute-start(bf16[32,1024]{1,0:T(8,128)(2,1)S(1)} %get-tuple-element.40), channel_id=1, source_target_pairs={{0,20},{4,16},{8,28},{12,24},{16,4},{20,0},{24,12},{28,8},{1,21},{... | collective-permute-start | bytes 196616 | tf_op jit(solution)/shard_map/ppermute | solution.py:223
  35.3 0.5 %collective-permute-start.12 = (bf16[32,1024]{1,0:T(8,128)(2,1)S(1)}, bf16[32,1024]{1,0:T(8,128)(2,1)S(1)}, u32[]{:S(2)}, u32[]{:S(2)}) collective-permute-start(bf16[32,1024]{1,0:T(8,128)(2,1)S(1)} %get-tuple-element.39), channel_id=1, source_target_pairs={{0,16},{4,20},{8,24},{12,28},{16,0},{20,4},{24,8},{28,12},{1,17},{... | collective-permute-start | bytes 196616 | tf_op jit(solution)/shard_map/ppermute | solution.py:223
  35.8 3.6 %collective-permute-start.16 = (bf16[32,1024]{1,0:T(8,128)(2,1)S(1)}, bf16[32,1024]{1,0:T(8,128)(2,1)S(1)}, u32[]{:S(2)}, u32[]{:S(2)}) collective-permute-start(bf16[32,1024]{1,0:T(8,128)(2,1)S(1)} %sum_over_x.1), channel_id=1, source_target_pairs={{0,24},{4,28},{8,16},{12,20},{16,8},{20,12},{24,0},{28,4},{1,25},{... | collective-permute-start | bytes 196616 | tf_op jit(solution)/shard_map/ppermute | solution.py:223
  39.5 0.0 collective-permute-done.13
  39.5 0.7 %collective-permute-done.12 = bf16[32,1024]{1,0:T(8,128)(2,1)S(1)} collective-permute-done((bf16[32,1024]{1,0:T(8,128)(2,1)S(1)}, bf16[32,1024]{1,0:T(8,128)(2,1)S(1)}, u32[]{:S(2)}, u32[]{:S(2)}) %collective-permute-start.12) | collective-permute-done | bytes 65568 | tf_op jit(solution)/shard_map/ppermute | solution.py:223
  40.2 1.8 %collective-permute-done.16 = bf16[32,1024]{1,0:T(8,128)(2,1)S(1)} collective-permute-done((bf16[32,1024]{1,0:T(8,128)(2,1)S(1)}, bf16[32,1024]{1,0:T(8,128)(2,1)S(1)}, u32[]{:S(2)}, u32[]{:S(2)}) %collective-permute-start.16) | collective-permute-done | bytes 65568 | tf_op jit(solution)/shard_map/ppermute | solution.py:223
  42.0 0.7 %fusion = bf16[1,32,1024]{2,1,0:T(8,128)(2,1)} fusion(bf16[32,1024]{1,0:T(8,128)(2,1)S(1)} %collective-permute-done.16, bf16[32,1024]{1,0:T(8,128)(2,1)S(1)} %collective-permute-done.13, bf16[32,1024]{1,0:T(8,128)(2,1)S(1)} %collective-permute-done.12), kind=kLoop, calls=%fused_computation.3 | loop fusion | flops 196608 | bytes 262144 | tf_op jit(solution)/shard_map/broadcast_in_dim | solution.py:232
  (26 shorter events, 0.2 us)
Async XLA Ops:
  0.0 6.4 %slice-start = ((s8[7340032]{0:T(1024)(128)(4,1)}), s8[4194304]{0:T(1024)(128)(4,1)S(1)}, s32[]{:S(2)}) async-start(s8[7340032]{0:T(1024)(128)(4,1)} %bitcast.9), calls=%async_computation | async-start | bytes 8388608
  0.0 6.4 %slice-start.2 = ((s8[7340032]{0:T(1024)(128)(4,1)}), s8[4194304]{0:T(1024)(128)(4,1)S(1)}, s32[]{:S(2)}) async-start(s8[7340032]{0:T(1024)(128)(4,1)} %bitcast.11), calls=%async_computation.2 | async-start | bytes 8388608
  0.0 6.4 %slice-start.1 = ((s8[7340032]{0:T(1024)(128)(4,1)}), s8[3145728]{0:T(1024)(128)(4,1)S(1)}, s32[]{:S(2)}) async-start(s8[7340032]{0:T(1024)(128)(4,1)} %bitcast.9), calls=%async_computation.1 | async-start | bytes 6291456
  0.0 6.4 %slice-start.3 = ((s8[7340032]{0:T(1024)(128)(4,1)}), s8[3145728]{0:T(1024)(128)(4,1)S(1)}, s32[]{:S(2)}) async-start(s8[7340032]{0:T(1024)(128)(4,1)} %bitcast.11), calls=%async_computation.3 | async-start | bytes 6291456
  0.0 6.4 %copy-start = (bf16[1,32,1024]{2,1,0:T(8,128)(2,1)S(1)}, bf16[1,32,1024]{2,1,0:T(8,128)(2,1)}, u32[]{:S(2)}) copy-start(bf16[1,32,1024]{2,1,0:T(8,128)(2,1)} %param.5) | copy-start | bytes 196612
  0.0 6.4 %collective-permute-start = (bf16[32,1024]{1,0:T(8,128)(2,1)}, bf16[32,1024]{1,0:T(8,128)(2,1)S(1)}, u32[]{:S(2)}, u32[]{:S(2)}) collective-permute-start(bf16[32,1024]{1,0:T(8,128)(2,1)} %bitcast.15), channel_id=1, source_target_pairs={{0,4},{4,0},{8,12},{12,8},{1,5},{5,1},{9,13},{13,9},{2,6},{6,2},{1... | collective-permute-start | bytes 196616 | tf_op jit(solution)/shard_map/ppermute | solution.py:27
  3.1 8.1 %collective-permute-start.1 = (bf16[32,1024]{1,0:T(8,128)(2,1)}, bf16[32,1024]{1,0:T(8,128)(2,1)S(1)}, u32[]{:S(2)}, u32[]{:S(2)}) collective-permute-start(bf16[32,1024]{1,0:T(8,128)(2,1)} %bitcast.16), channel_id=1, source_target_pairs={{0,8},{4,12},{8,0},{12,4},{1,9},{5,13},{9,1},{13,5},{2,10},{6,14},... | collective-permute-start | bytes 196616 | tf_op jit(solution)/shard_map/ppermute | solution.py:27
  5.7 6.3 %collective-permute-start.2 = (bf16[32,1024]{1,0:T(8,128)(2,1)}, bf16[32,1024]{1,0:T(8,128)(2,1)S(1)}, u32[]{:S(2)}, u32[]{:S(2)}) collective-permute-start(bf16[32,1024]{1,0:T(8,128)(2,1)} %bitcast.17), channel_id=1, source_target_pairs={{0,12},{4,8},{8,4},{12,0},{1,13},{5,9},{9,5},{13,1},{2,14},{6,10},... | collective-permute-start | bytes 196616 | tf_op jit(solution)/shard_map/ppermute | solution.py:27
  5.7 0.7 %copy-start.1 = (f32[1,1024]{1,0:T(1,128)S(1)}, f32[1,1024]{1,0:T(1,128)}, u32[]{:S(2)}) copy-start(f32[1,1024]{1,0:T(1,128)} %refs_0_.1) | copy-start | bytes 12292
  7.2 2.0 %collective-permute-start.3 = (bf16[64,1920]{1,0:T(8,128)(2,1)S(1)}, bf16[64,1920]{1,0:T(8,128)(2,1)S(1)}, u32[]{:S(2)}, u32[]{:S(2)}) collective-permute-start(bf16[64,1920]{1,0:T(8,128)(2,1)S(1)} %get-tuple-element.26), channel_id=1, source_target_pairs={{0,1},{1,0},{2,3},{3,2},{4,5},{5,4},{6,7},{7,6},{8,9},{9,8},{10,11... | collective-permute-start | bytes 737288 | tf_op jit(solution)/shard_map/ppermute | solution.py:27
  8.7 8.6 %collective-permute-start.5 = (bf16[64,1792]{1,0:T(8,128)(2,1)S(1)}, bf16[64,1792]{1,0:T(8,128)(2,1)S(1)}, u32[]{:S(2)}, u32[]{:S(2)}) collective-permute-start(bf16[64,1792]{1,0:T(8,128)(2,1)S(1)} %get-tuple-element.32), channel_id=1, source_target_pairs={{0,1},{1,0},{2,3},{3,2},{4,5},{5,4},{6,7},{7,6},{8,9},{9,8},{10,11... | collective-permute-start | bytes 688136 | tf_op jit(solution)/shard_map/ppermute | solution.py:27
  9.4 8.0 %collective-permute-start.6 = (bf16[64,1920]{1,0:T(8,128)(2,1)S(1)}, bf16[64,1920]{1,0:T(8,128)(2,1)S(1)}, u32[]{:S(2)}, u32[]{:S(2)}) collective-permute-start(bf16[64,1920]{1,0:T(8,128)(2,1)S(1)} %joined_near.1.refs_5_), channel_id=1, source_target_pairs={{0,2},{1,3},{2,0},{3,1},{4,6},{5,7},{6,4},{7,5},{8,10},{9,11},{10,... | collective-permute-start | bytes 737288 | tf_op jit(solution)/shard_map/ppermute | solution.py:27
  12.8 2.0 %collective-permute-start.4 = (bf16[64,1920]{1,0:T(8,128)(2,1)S(1)}, bf16[64,1920]{1,0:T(8,128)(2,1)S(1)}, u32[]{:S(2)}, u32[]{:S(2)}) collective-permute-start(bf16[64,1920]{1,0:T(8,128)(2,1)S(1)} %get-tuple-element.28.refs_3_), channel_id=1, source_target_pairs={{0,1},{1,0},{2,3},{3,2},{4,5},{5,4},{6,7},{7,6},{8,9},{9,8},{10,11... | collective-permute-start | bytes 737288 | tf_op jit(solution)/shard_map/ppermute | solution.py:27
  12.9 4.5 %slice-start.4 = ((s8[7340032]{0:T(1024)(128)(4,1)}), s8[4194304]{0:T(1024)(128)(4,1)S(1)}, s32[]{:S(2)}) async-start(s8[7340032]{0:T(1024)(128)(4,1)} %bitcast.13), calls=%async_computation.4 | async-start | bytes 8388608
  14.3 5.7 %collective-permute-start.9 = (bf16[64,1792]{1,0:T(8,128)(2,1)S(1)}, bf16[64,1792]{1,0:T(8,128)(2,1)S(1)}, u32[]{:S(2)}, u32[]{:S(2)}) collective-permute-start(bf16[64,1792]{1,0:T(8,128)(2,1)S(1)} %get-tuple-element.36), channel_id=1, source_target_pairs={{0,1},{1,0},{2,3},{3,2},{4,5},{5,4},{6,7},{7,6},{8,9},{9,8},{10,11... | collective-permute-start | bytes 688136 | tf_op jit(solution)/shard_map/ppermute | solution.py:27
  14.8 2.6 %slice-start.5 = ((s8[7340032]{0:T(1024)(128)(4,1)}), s8[3145728]{0:T(1024)(128)(4,1)S(1)}, s32[]{:S(2)}) async-start(s8[7340032]{0:T(1024)(128)(4,1)} %bitcast.13), calls=%async_computation.5 | async-start | bytes 6291456
  15.0 8.0 %collective-permute-start.10 = (bf16[64,1920]{1,0:T(8,128)(2,1)S(1)}, bf16[64,1920]{1,0:T(8,128)(2,1)S(1)}, u32[]{:S(2)}, u32[]{:S(2)}) collective-permute-start(bf16[64,1920]{1,0:T(8,128)(2,1)S(1)} %joined_far.1.refs_4_), channel_id=1, source_target_pairs={{0,2},{1,3},{2,0},{3,1},{4,6},{5,7},{6,4},{7,5},{8,10},{9,11},{10,... | collective-permute-start | bytes 737288 | tf_op jit(solution)/shard_map/ppermute | solution.py:27
  18.3 1.6 %collective-permute-start.7 = (bf16[2,64,1024]{2,1,0:T(8,128)(2,1)S(1)}, bf16[2,64,1024]{2,1,0:T(8,128)(2,1)S(1)}, u32[]{:S(2)}, u32[]{:S(2)}) collective-permute-start(bf16[2,64,1024]{2,1,0:T(8,128)(2,1)S(1)} %get-tuple-element.34.refs_2_), channel_id=1, source_target_pairs={{0,1},{1,0},{2,3},{3,2},{4,5},{5,4},{6,7},{7,6},{8,9},{9,8},{10,11... | collective-permute-start | bytes 786440 | tf_op jit(solution)/shard_map/ppermute | solution.py:27
  23.8 1.6 %collective-permute-start.11 = (bf16[2,64,1024]{2,1,0:T(8,128)(2,1)S(1)}, bf16[2,64,1024]{2,1,0:T(8,128)(2,1)S(1)}, u32[]{:S(2)}, u32[]{:S(2)}) collective-permute-start(bf16[2,64,1024]{2,1,0:T(8,128)(2,1)S(1)} %get-tuple-element.38.refs_2_), channel_id=1, source_target_pairs={{0,1},{1,0},{2,3},{3,2},{4,5},{5,4},{6,7},{7,6},{8,9},{9,8},{10,11... | collective-permute-start | bytes 786440 | tf_op jit(solution)/shard_map/ppermute | solution.py:27
  25.5 5.6 %collective-permute-start.14 = (bf16[2,32,1024]{2,1,0:T(8,128)(2,1)S(1)}, bf16[2,32,1024]{2,1,0:T(8,128)(2,1)S(1)}, u32[]{:S(2)}, u32[]{:S(2)}) collective-permute-start(bf16[2,32,1024]{2,1,0:T(8,128)(2,1)S(1)} %slice.17), channel_id=1, source_target_pairs={{0,4},{4,0},{8,12},{12,8},{1,5},{5,1},{9,13},{13,9},{2,6},{6,2},{1... | collective-permute-start | bytes 393224 | tf_op jit(solution)/shard_map/ppermute | solution.py:27
  27.1 5.6 %collective-permute-start.8 = (bf16[64,1024]{1,0:T(8,128)(2,1)S(1)}, bf16[64,1024]{1,0:T(8,128)(2,1)S(1)}, u32[]{:S(2)}, u32[]{:S(2)}) collective-permute-start(bf16[64,1024]{1,0:T(8,128)(2,1)S(1)} %slice_bitcast_fusion), channel_id=1, source_target_pairs={{0,2},{1,3},{2,0},{3,1},{4,6},{5,7},{6,4},{7,5},{8,10},{9,11},{10,... | collective-permute-start | bytes 393224 | tf_op jit(solution)/shard_map/ppermute | solution.py:27
  31.2 4.7 %collective-permute-start.15 = (bf16[32,1024]{1,0:T(8,128)(2,1)S(1)}, bf16[32,1024]{1,0:T(8,128)(2,1)S(1)}, u32[]{:S(2)}, u32[]{:S(2)}) collective-permute-start(bf16[32,1024]{1,0:T(8,128)(2,1)S(1)} %get-tuple-element.41), channel_id=1, source_target_pairs={{0,2},{1,3},{2,0},{3,1},{4,6},{5,7},{6,4},{7,5},{8,10},{9,11},{10,... | collective-permute-start | bytes 196616 | tf_op jit(solution)/shard_map/ppermute | solution.py:27
  32.8 6.7 %collective-permute-start.13 = (bf16[32,1024]{1,0:T(8,128)(2,1)S(1)}, bf16[32,1024]{1,0:T(8,128)(2,1)S(1)}, u32[]{:S(2)}, u32[]{:S(2)}) collective-permute-start(bf16[32,1024]{1,0:T(8,128)(2,1)S(1)} %get-tuple-element.40), channel_id=1, source_target_pairs={{0,20},{4,16},{8,28},{12,24},{16,4},{20,0},{24,12},{28,8},{1,21},{... | collective-permute-start | bytes 196616 | tf_op jit(solution)/shard_map/ppermute | solution.py:223
  35.3 4.9 %collective-permute-start.12 = (bf16[32,1024]{1,0:T(8,128)(2,1)S(1)}, bf16[32,1024]{1,0:T(8,128)(2,1)S(1)}, u32[]{:S(2)}, u32[]{:S(2)}) collective-permute-start(bf16[32,1024]{1,0:T(8,128)(2,1)S(1)} %get-tuple-element.39), channel_id=1, source_target_pairs={{0,16},{4,20},{8,24},{12,28},{16,0},{20,4},{24,8},{28,12},{1,17},{... | collective-permute-start | bytes 196616 | tf_op jit(solution)/shard_map/ppermute | solution.py:223
  35.8 6.1 %collective-permute-start.16 = (bf16[32,1024]{1,0:T(8,128)(2,1)S(1)}, bf16[32,1024]{1,0:T(8,128)(2,1)S(1)}, u32[]{:S(2)}, u32[]{:S(2)}) collective-permute-start(bf16[32,1024]{1,0:T(8,128)(2,1)S(1)} %sum_over_x.1), channel_id=1, source_target_pairs={{0,24},{4,28},{8,16},{12,20},{16,8},{20,12},{24,0},{28,4},{1,25},{... | collective-permute-start | bytes 196616 | tf_op jit(solution)/shard_map/ppermute | solution.py:223

commit v5 on v4

--- a/solution.py
+++ b/solution.py
@@ -38,26 +38,27 @@
 )
 
 
-def call(body, name, outs, held, streamed=(), after=(), copies=0):
-    fixed = len(held) + len(streamed)
+def call(body, name, outs, held, after=(), passed=()):
+    own, last = len(held), len(held) + len(passed) + len(after)
 
     def run(*refs):
-        body(*refs[:fixed], *refs[fixed + len(after) :])
-
-    spaces = [pltpu.VMEM] * len(held) + [pltpu.HBM] * len(streamed)
+        body(*refs[:own], *refs[last : last + count])
+
+    outs = [*outs, *((a.shape, a.dtype) for a in passed)]
+    count = len(outs) - len(passed)
+    vmem = pl.BlockSpec(memory_space=pltpu.VMEM)
     return pl.pallas_call(
         run,
         name=name,
-        in_specs=[pl.BlockSpec(memory_space=s) for s in spaces]
-        + [pl.BlockSpec(memory_space=pl.ANY)] * len(after),
+        in_specs=[vmem] * (own + len(passed)) + [pl.BlockSpec(memory_space=pl.ANY)] * len(after),
         out_shape=[pltpu.VMEM(shape, dtype) for shape, dtype in outs],
-        out_specs=[pl.BlockSpec(memory_space=pltpu.VMEM)] * len(outs),
-        scratch_shapes=[pltpu.SemaphoreType.DMA((copies,))] if copies else [],
+        out_specs=[vmem] * len(outs),
+        input_output_aliases={own + i: count + i for i in range(len(passed))},
         cost_estimate=pl.CostEstimate(
             flops=COST.get(name, 0) * 10**8, transcendentals=0, bytes_accessed=0
         ),
         compiler_params=pltpu.CompilerParams(vmem_limit_bytes=16 * 1024 * 1024),
-    )(*[placed_in(a, s) for a, s in zip([*held, *streamed], spaces)], *after)
+    )(*[placed_in(a, pltpu.VMEM) for a in [*held, *passed]], *after)
 
 
 def dot(a, b):
@@ -105,13 +106,18 @@
     products(k, [x_out], (gate, up), (out,))
 
 
+def one_product(k, x, gate, up, out):
+    products(k, [x], (gate, up), (out,))
+
+
 def two_products(ks, x, gate, up, a_out, b_out):
     products(ks[0], [x], (gate, up), (a_out,))
     products(ks[1], [x], (gate, up), (b_out,))
 
 
-def product_of_both(k, xa, xb, gate, up, a_out, b_out):
-    products(k, [xa, xb], (gate, up), (a_out, b_out))
+def last_products(xn, xf, gate, up, a_out, b_out, c_out):
+    products(0, [xn, xf], (gate, up), (a_out, b_out))
+    products(1, [xf], (gate, up), (c_out,))
 
 
 def pause(value_ref, out):
@@ -177,7 +183,7 @@
     x_shape, s_shape = ((m, depth), BF16), ((m, LANES), BF16)
     h_shape, e_shape = ((m, width), BF16), ((2, m, depth), BF16)
     weights = [gate_weight, up_weight]
-    (gain,) = call(pause, "pause", [(norm_gain.shape, F32)], [norm_gain])
+    (gain,) = call(pause, "pause", [(norm_gain.shape, F32)], [norm_gain], [slots[1]])
 
     xn, sn, p3n = call(
         part(first, 3), "first_near", [x_shape, s_shape, payload], [*slots[:2], gain, *weights]
@@ -189,34 +195,33 @@
     f2n = swapped(q2n, "col", 2)
 
     xf, sf, p3f = call(
-        part(first, 3), "first_far", [x_shape, s_shape, payload], [*slots[2:], gain, *weights], (), [q2n]
+        part(first, 3), "first_far", [x_shape, s_shape, payload], [*slots[2:], gain, *weights], [q2n]
     )
     r3f = swapped(p3f, "col", 1)
-    p2f, p1f = call(
-        part(two_products, (2, 1)), "next_far", [sums, sums], [xf, *weights], (), [p3f]
-    )
-    r1f = swapped(p1f, "col", 1)
+    (p2f,) = call(part(one_product, 2), "next_far", [sums], [xf, *weights], [p3f])
     (q2f,) = call(joined, "joined_far", [payload], [p2f, sf, r3f])
     f2f = swapped(q2f, "col", 2)
 
-    p0n, p0f = call(
-        part(product_of_both, 0), "product0", [wide, wide], [xn, xf, *weights], (), [q2f]
-    )
-
-    def hidden_and_down(which, p0, r1, s, f2, r3, after):
-        h, e1 = call(
+    p0n, p0f, p1f = call(
+        last_products, "product0", [wide, wide, sums], [xn, xf, *weights], [q2f]
+    )
+
+    def hidden_and_down(which, p0, r1, s, f2, r3, after, passed=()):
+        h, e1, *passed = call(
             part(activate_and_down, 1.0 / (depth * cols), (1, 3)), "activate_" + which,
-            [h_shape, e_shape], [p0, r1, s, f2, r3, down_weight], (), after,
+            [h_shape, e_shape], [p0, r1, s, f2, r3, down_weight], after, passed,
         )
         t1 = swapped(e1, "col", 1)
-        (e0,) = call(part(down, (0, 2)), "down_" + which, [e_shape], [h, down_weight], (), [e1])
-        return e0, t1
-
-    u = added(*hidden_and_down("near", p0n, r1n, sn, f2n, r3n, ()))
+        (e0,) = call(part(down, (0, 2)), "down_" + which, [e_shape], [h, down_weight], [e1])
+        return e0, t1, *passed
+
+    e0n, t1n, p1f = hidden_and_down("near", p0n, r1n, sn, f2n, r3n, (), [p1f])
+    r1f = swapped(p1f, "col", 1)
+    u = added(e0n, t1n)
     un = swapped(u[1], "col", 2)
     e0f, t1f = hidden_and_down("far", p0f, r1f, sf, f2f, r3f, [u])
-    (w,) = call(sum_of_two, "sum_far", [e_shape], [e0f, t1f], (), [])
-    n0, n1 = call(near_sums, "sum_near", [(own.shape, BF16)] * 2, [u, un, own], (), [w])
+    (w,) = call(sum_of_two, "sum_far", [e_shape], [e0f, t1f], [])
+    n0, n1 = call(near_sums, "sum_near", [(own.shape, BF16)] * 2, [u, un, own], [w])
 
     def onward(value, k):
         pairs = [(p * rows + r, q * rows + (r ^ k)) for p, q in forward for r in range(rows)]
@@ -226,9 +231,9 @@
     near_part = onward(n1, 1)
     (w,) = call(
         sum_over_rows, "sum_over_rows", [((2, *own.shape), BF16)],
-        [w, swapped(w[:, count:], "row", 1)], (), [],
-    )
-    (w,) = call(sum_of_two, "sum_over_x", [(own.shape, BF16)], [w[0], swapped(w[1], "col", 2)], (), [])
+        [w, swapped(w[:, count:], "row", 1)], [],
+    )
+    (w,) = call(sum_of_two, "sum_over_x", [(own.shape, BF16)], [w[0], swapped(w[1], "col", 2)], [])
     return added(own_part, near_part, onward(w, 2))[None]
 
 

time: 42.8 us -> 42.9 us (level)
  starting transfers between devices: 21.8 us -> 22.4 us
  waiting for transfers between devices: 10.4 us -> 9.84 us
  transfers between devices with their start and end apart: 17 -> 17, of which waited for: 8 -> 9; matrix products, arithmetic and copies ran while one was open for 0% -> 0% of each run, Pallas kernels for 18% -> 18%
where the time goes in v5:
time: 42.9 us; the launch traced here: 42.7 us
  starting transfers between devices  22.4 us (52%)
  waiting for transfers between devices  9.84 us (23%)
  Pallas kernels  8.73 us (20%)
  local copies, waits for them, and re-layouts  0.75 us (2%)
  other arithmetic  0.72 us (2%)
    ppermute x14, starting transfers between devices, swapped(): return lax.ppermute(value, axis, [(i, i ^ mask) for i in range(count)])  15.4 us
    pallas_call x16, Pallas kernels, call(): pl.pallas_call(run, name=name, in_specs=[vmem] * (own + len(passed)) + [p...  8.73 us
    ppermute x14, waiting for transfers between devices, swapped(): return lax.ppermute(value, axis, [(i, i ^ mask) for i in range(count)])  7.58 us
    ppermute x3, starting transfers between devices, onward(): return lax.ppermute(value, ('pipe', 'row'), pairs)  6.97 us
    ppermute x3, waiting for transfers between devices, onward(): return lax.ppermute(value, ('pipe', 'row'), pairs)  2.27 us
  transfers between devices with their start and end apart: 17, of which 9 were waited for; matrix products, arithmetic and copies ran while one was open for 0% of the time, Pallas kernels for 18%

profile of v5, /device:TPU:0, one launch (start us, length us, event | category | flops | bytes accessed | tf_op | source)
XLA Modules:
  0.0 42.7 jit_solution(5565317884317314978)
XLA Ops:
  0.0 3.1 %collective-permute-start = (bf16[32,1024]{1,0:T(8,128)(2,1)}, bf16[32,1024]{1,0:T(8,128)(2,1)S(1)}, u32[]{:S(2)}, u32[]{:S(2)}) collective-permute-start(bf16[32,1024]{1,0:T(8,128)(2,1)} %bitcast.15), channel_id=1, source_target_pairs={{0,4},{4,0},{8,12},{12,8},{1,5},{5,1},{9,13},{13,9},{2,6},{6,2},{1... | collective-permute-start | bytes 196616 | tf_op jit(solution)/shard_map/ppermute | solution.py:27
  3.1 2.5 %collective-permute-start.2 = (bf16[32,1024]{1,0:T(8,128)(2,1)}, bf16[32,1024]{1,0:T(8,128)(2,1)S(1)}, u32[]{:S(2)}, u32[]{:S(2)}) collective-permute-start(bf16[32,1024]{1,0:T(8,128)(2,1)} %bitcast.16), channel_id=1, source_target_pairs={{0,12},{4,8},{8,4},{12,0},{1,13},{5,9},{9,5},{13,1},{2,14},{6,10},... | collective-permute-start | bytes 196616 | tf_op jit(solution)/shard_map/ppermute | solution.py:27
  5.6 0.1 collective-permute-start.1
  5.7 0.0 collective-permute-done.refs_1_
  5.7 0.7 %copy-done.1 = f32[1,1024]{1,0:T(1,128)S(1)} copy-done((f32[1,1024]{1,0:T(1,128)S(1)}, f32[1,1024]{1,0:T(1,128)}, u32[]{:S(2)}) %copy-start.1) | copy-done | bytes 4120
  6.5 0.8 %first_near.1 = (bf16[64,1024]{1,0:T(8,128)(2,1)S(1)}, bf16[64,128]{1,0:T(8,128)(2,1)S(1)}, bf16[64,1920]{1,0:T(8,128)(2,1)S(1)}) custom-call(bf16[32,1024]{1,0:T(8,128)(2,1)S(1)} %bitcast.18, bf16[32,1024]{1,0:T(8,128)(2,1)S(1)} %collective-permute-done.refs_1_, f32[1,1024]{1,0:T(1,128)S(1)} %pause.1.refs_2_, bf16[1,1024,3584]{2,1,0:T(8,128)(2,1)S(1)} %bitcast.10, ...), custom_call_target="tpu_custom_call" | custom-call | flops 10000000000 | tf_op jit(solution)/shard_map/first_near/pallas_call | solution.py:50
  7.2 0.1 collective-permute-start.3
  7.3 1.4 %next_near.1 = (bf16[64,1792]{1,0:T(8,128)(2,1)S(1)}, bf16[64,1792]{1,0:T(8,128)(2,1)S(1)}) custom-call(bf16[64,1024]{1,0:T(8,128)(2,1)S(1)} %get-tuple-element.23.refs_0_, bf16[1,1024,3584]{2,1,0:T(8,128)(2,1)S(1)} %bitcast.10, bf16[1,1024,3584]{2,1,0:T(8,128)(2,1)S(1)} %bitcast.12), custom_call_target="tpu_custom_call" | custom-call | flops 10000000000 | tf_op jit(solution)/shard_map/next_near/pallas_call | solution.py:50
  8.7 0.5 %collective-permute-start.5 = (bf16[64,1792]{1,0:T(8,128)(2,1)S(1)}, bf16[64,1792]{1,0:T(8,128)(2,1)S(1)}, u32[]{:S(2)}, u32[]{:S(2)}) collective-permute-start(bf16[64,1792]{1,0:T(8,128)(2,1)S(1)} %get-tuple-element.31), channel_id=1, source_target_pairs={{0,1},{1,0},{2,3},{3,2},{4,5},{5,4},{6,7},{7,6},{8,9},{9,8},{10,11... | collective-permute-start | bytes 688136 | tf_op jit(solution)/shard_map/ppermute | solution.py:27
  9.2 0.0 collective-permute-done.3.refs_2_.refs_4_
  9.2 0.2 joined_near.1.refs_5_
  9.4 1.9 %collective-permute-start.6 = (bf16[64,1920]{1,0:T(8,128)(2,1)S(1)}, bf16[64,1920]{1,0:T(8,128)(2,1)S(1)}, u32[]{:S(2)}, u32[]{:S(2)}) collective-permute-start(bf16[64,1920]{1,0:T(8,128)(2,1)S(1)} %joined_near.1.refs_5_), channel_id=1, source_target_pairs={{0,2},{1,3},{2,0},{3,1},{4,6},{5,7},{6,4},{7,5},{8,10},{9,11},{10,... | collective-permute-start | bytes 737288 | tf_op jit(solution)/shard_map/ppermute | solution.py:27
  11.3 0.0 collective-permute-done.2.refs_1_
  11.3 1.0 %collective-permute-done.1.refs_0_ = bf16[32,1024]{1,0:T(8,128)(2,1)S(1)} collective-permute-done((bf16[32,1024]{1,0:T(8,128)(2,1)}, bf16[32,1024]{1,0:T(8,128)(2,1)S(1)}, u32[]{:S(2)}, u32[]{:S(2)}) %collective-permute-start.1) | collective-permute-done | bytes 65568 | tf_op jit(solution)/shard_map/ppermute | solution.py:27
  12.3 0.8 %first_far.1 = (bf16[64,1024]{1,0:T(8,128)(2,1)S(1)}, bf16[64,128]{1,0:T(8,128)(2,1)S(1)}, bf16[64,1920]{1,0:T(8,128)(2,1)S(1)}) custom-call(bf16[32,1024]{1,0:T(8,128)(2,1)S(1)} %collective-permute-done.1.refs_0_, bf16[32,1024]{1,0:T(8,128)(2,1)S(1)} %collective-permute-done.2.refs_1_, f32[1,1024]{1,0:T(1,128)S(1)} %pause.1.refs_2_, ...), custom_call_target="tpu_custom_call" | custom-call | flops 10000000000 | tf_op jit(solution)/shard_map/first_far/pallas_call | solution.py:50
  13.0 0.1 collective-permute-start.4
  13.1 0.0 slice-start.4
  13.1 0.8 %next_far.1.refs_0_ = bf16[64,1792]{1,0:T(8,128)(2,1)S(1)} custom-call(bf16[64,1024]{1,0:T(8,128)(2,1)S(1)} %get-tuple-element.27.refs_0_.refs_1_, bf16[1,1024,3584]{2,1,0:T(8,128)(2,1)S(1)} %bitcast.10, bf16[1,1024,3584]{2,1,0:T(8,128)(2,1)S(1)} %bitcast.12, bf16[64,1920]{1,0:T(8,128)(2,1)S(1)} %get-tuple-element.28.refs_3_), custom_call_target="tpu_custom_call" | custom-call | flops 10000000000 | tf_op jit(solution)/shard_map/next_far/pallas_call | solution.py:50
  13.9 0.7 %collective-permute-done.4.refs_2_.refs_4_ = bf16[64,1920]{1,0:T(8,128)(2,1)S(1)} collective-permute-done((bf16[64,1920]{1,0:T(8,128)(2,1)S(1)}, bf16[64,1920]{1,0:T(8,128)(2,1)S(1)}, u32[]{:S(2)}, u32[]{:S(2)}) %collective-permute-start.4) | collective-permute-done | bytes 245792 | tf_op jit(solution)/shard_map/ppermute | solution.py:27
  14.6 0.2 joined_far.1.refs_4_
  14.8 1.6 %collective-permute-start.10 = (bf16[64,1920]{1,0:T(8,128)(2,1)S(1)}, bf16[64,1920]{1,0:T(8,128)(2,1)S(1)}, u32[]{:S(2)}, u32[]{:S(2)}) collective-permute-start(bf16[64,1920]{1,0:T(8,128)(2,1)S(1)} %joined_far.1.refs_4_), channel_id=1, source_target_pairs={{0,2},{1,3},{2,0},{3,1},{4,6},{5,7},{6,4},{7,5},{8,10},{9,11},{10,... | collective-permute-start | bytes 737288 | tf_op jit(solution)/shard_map/ppermute | solution.py:27
  16.4 1.3 %product0.1 = (f32[64,1792]{1,0:T(8,128)S(1)}, f32[64,1792]{1,0:T(8,128)S(1)}, bf16[64,1792]{1,0:T(8,128)(2,1)S(1)}) custom-call(bf16[64,1024]{1,0:T(8,128)(2,1)S(1)} %get-tuple-element.23.refs_0_, bf16[64,1024]{1,0:T(8,128)(2,1)S(1)} %get-tuple-element.27.refs_0_.refs_1_, bf16[1,1024,3584]{2,1,0:T(8,128)(2,1)S(1)} %bitcast.10, ...), custom_call_target="tpu_custom_call" | custom-call | flops 100000000 | tf_op jit(solution)/shard_map/product0/pallas_call | solution.py:50
  17.7 0.0 collective-permute-done.5.refs_1_
  17.7 0.0 collective-permute-done.6.refs_3_
  17.7 0.9 %activate_near.1 = (bf16[64,896]{1,0:T(8,128)(2,1)S(1)}, bf16[2,64,1024]{2,1,0:T(8,128)(2,1)S(1)}, bf16[64,1792]{1,0:T(8,128)(2,1)S(1)}) custom-call(f32[64,1792]{1,0:T(8,128)S(1)} %get-tuple-element.30.refs_0_, bf16[64,1792]{1,0:T(8,128)(2,1)S(1)} %collective-permute-done.5.refs_1_, ...), custom_call_target="tpu_custom_call", output_to_operand_aliasing={{2}: (6, {})} | custom-call | flops 10000000000 | tf_op jit(solution)/shard_map/activate_near/pallas_call | solution.py:50
  18.6 0.1 collective-permute-start.7
  18.7 0.8 %down_near.1 = bf16[2,64,1024]{2,1,0:T(8,128)(2,1)S(1)} custom-call(bf16[64,896]{1,0:T(8,128)(2,1)S(1)} %get-tuple-element.33.refs_0_, bf16[1,896,4096]{2,1,0:T(8,128)(2,1)S(1)} %bitcast.14, bf16[2,64,1024]{2,1,0:T(8,128)(2,1)S(1)} %get-tuple-element.34.refs_2_), custom_call_target="tpu_custom_call" | custom-call | flops 10000000000 | tf_op jit(solution)/shard_map/down_near/pallas_call | solution.py:50
  19.4 0.6 %collective-permute-start.9 = (bf16[64,1792]{1,0:T(8,128)(2,1)S(1)}, bf16[64,1792]{1,0:T(8,128)(2,1)S(1)}, u32[]{:S(2)}, u32[]{:S(2)}) collective-permute-start(bf16[64,1792]{1,0:T(8,128)(2,1)S(1)} %get-tuple-element.36), channel_id=1, source_target_pairs={{0,1},{1,0},{2,3},{3,2},{4,5},{5,4},{6,7},{7,6},{8,9},{9,8},{10,11... | collective-permute-start | bytes 688136 | tf_op jit(solution)/shard_map/ppermute | solution.py:27
  20.0 0.2 collective-permute-done.7
  20.2 0.1 add_convert_fusion.refs_6_.refs_0_
  20.3 0.8 %collective-permute-done.9.refs_1_ = bf16[64,1792]{1,0:T(8,128)(2,1)S(1)} collective-permute-done((bf16[64,1792]{1,0:T(8,128)(2,1)S(1)}, bf16[64,1792]{1,0:T(8,128)(2,1)S(1)}, u32[]{:S(2)}, u32[]{:S(2)}) %collective-permute-start.9) | collective-permute-done | bytes 229408 | tf_op jit(solution)/shard_map/ppermute | solution.py:27
  21.1 1.8 %collective-permute-done.10.refs_3_ = bf16[64,1920]{1,0:T(8,128)(2,1)S(1)} collective-permute-done((bf16[64,1920]{1,0:T(8,128)(2,1)S(1)}, bf16[64,1920]{1,0:T(8,128)(2,1)S(1)}, u32[]{:S(2)}, u32[]{:S(2)}) %collective-permute-start.10) | collective-permute-done | bytes 245792 | tf_op jit(solution)/shard_map/ppermute | solution.py:27
  22.9 0.9 %activate_far.1 = (bf16[64,896]{1,0:T(8,128)(2,1)S(1)}, bf16[2,64,1024]{2,1,0:T(8,128)(2,1)S(1)}) custom-call(f32[64,1792]{1,0:T(8,128)S(1)} %get-tuple-element.35.refs_0_, bf16[64,1792]{1,0:T(8,128)(2,1)S(1)} %collective-permute-done.9.refs_1_, bf16[64,128]{1,0:T(8,128)(2,1)S(1)} %get-tuple-element.29.refs_1_.refs_2_, ...), custom_call_target="tpu_custom_call" | custom-call | flops 10000000000 | tf_op jit(solution)/shard_map/activate_far/pallas_call | solution.py:50
  23.7 0.1 collective-permute-start.11
  23.8 0.8 %down_far.1.refs_0_ = bf16[2,64,1024]{2,1,0:T(8,128)(2,1)S(1)} custom-call(bf16[64,896]{1,0:T(8,128)(2,1)S(1)} %get-tuple-element.37.refs_0_, bf16[1,896,4096]{2,1,0:T(8,128)(2,1)S(1)} %bitcast.14, bf16[2,64,1024]{2,1,0:T(8,128)(2,1)S(1)} %get-tuple-element.38.refs_2_), custom_call_target="tpu_custom_call" | custom-call | flops 100000000 | tf_op jit(solution)/shard_map/down_far/pallas_call | solution.py:50
  24.6 0.7 %collective-permute-done.11.refs_1_ = bf16[2,64,1024]{2,1,0:T(8,128)(2,1)S(1)} collective-permute-done((bf16[2,64,1024]{2,1,0:T(8,128)(2,1)S(1)}, bf16[2,64,1024]{2,1,0:T(8,128)(2,1)S(1)}, u32[]{:S(2)}, u32[]{:S(2)}) %collective-permute-start.11) | collective-permute-done | bytes 262176 | tf_op jit(solution)/shard_map/ppermute | solution.py:27
  25.3 0.1 sum_far.1.refs_3_.refs_0_
  25.4 1.7 %collective-permute-start.14 = (bf16[2,32,1024]{2,1,0:T(8,128)(2,1)S(1)}, bf16[2,32,1024]{2,1,0:T(8,128)(2,1)S(1)}, u32[]{:S(2)}, u32[]{:S(2)}) collective-permute-start(bf16[2,32,1024]{2,1,0:T(8,128)(2,1)S(1)} %slice.17), channel_id=1, source_target_pairs={{0,4},{4,0},{8,12},{12,8},{1,5},{5,1},{9,13},{13,9},{2,6},{6,2},{1... | collective-permute-start | bytes 393224 | tf_op jit(solution)/shard_map/ppermute | solution.py:27
  27.2 1.6 %collective-permute-start.8 = (bf16[64,1024]{1,0:T(8,128)(2,1)S(1)}, bf16[64,1024]{1,0:T(8,128)(2,1)S(1)}, u32[]{:S(2)}, u32[]{:S(2)}) collective-permute-start(bf16[64,1024]{1,0:T(8,128)(2,1)S(1)} %slice_bitcast_fusion), channel_id=1, source_target_pairs={{0,2},{1,3},{2,0},{3,1},{4,6},{5,7},{6,4},{7,5},{8,10},{9,11},{10,... | collective-permute-start | bytes 393224 | tf_op jit(solution)/shard_map/ppermute | solution.py:27
  28.7 2.3 %collective-permute-done.14.refs_1_ = bf16[2,32,1024]{2,1,0:T(8,128)(2,1)S(1)} collective-permute-done((bf16[2,32,1024]{2,1,0:T(8,128)(2,1)S(1)}, bf16[2,32,1024]{2,1,0:T(8,128)(2,1)S(1)}, u32[]{:S(2)}, u32[]{:S(2)}) %collective-permute-start.14) | collective-permute-done | bytes 131104 | tf_op jit(solution)/shard_map/ppermute | solution.py:27
  31.1 1.6 %collective-permute-start.15 = (bf16[32,1024]{1,0:T(8,128)(2,1)S(1)}, bf16[32,1024]{1,0:T(8,128)(2,1)S(1)}, u32[]{:S(2)}, u32[]{:S(2)}) collective-permute-start(bf16[32,1024]{1,0:T(8,128)(2,1)S(1)} %get-tuple-element.41), channel_id=1, source_target_pairs={{0,2},{1,3},{2,0},{3,1},{4,6},{5,7},{6,4},{7,5},{8,10},{9,11},{10,... | collective-permute-start | bytes 196616 | tf_op jit(solution)/shard_map/ppermute | solution.py:27
  32.8 1.6 %collective-permute-start.12 = (bf16[32,1024]{1,0:T(8,128)(2,1)S(1)}, bf16[32,1024]{1,0:T(8,128)(2,1)S(1)}, u32[]{:S(2)}, u32[]{:S(2)}) collective-permute-start(bf16[32,1024]{1,0:T(8,128)(2,1)S(1)} %get-tuple-element.39), channel_id=1, source_target_pairs={{0,16},{4,20},{8,24},{12,28},{16,0},{20,4},{24,8},{28,12},{1,17},{... | collective-permute-start | bytes 196616 | tf_op jit(solution)/shard_map/ppermute | solution.py:228
  34.3 1.5 %collective-permute-start.13 = (bf16[32,1024]{1,0:T(8,128)(2,1)S(1)}, bf16[32,1024]{1,0:T(8,128)(2,1)S(1)}, u32[]{:S(2)}, u32[]{:S(2)}) collective-permute-start(bf16[32,1024]{1,0:T(8,128)(2,1)S(1)} %get-tuple-element.40), channel_id=1, source_target_pairs={{0,20},{4,16},{8,28},{12,24},{16,4},{20,0},{24,12},{28,8},{1,21},{... | collective-permute-start | bytes 196616 | tf_op jit(solution)/shard_map/ppermute | solution.py:228
  35.9 3.9 %collective-permute-start.16 = (bf16[32,1024]{1,0:T(8,128)(2,1)S(1)}, bf16[32,1024]{1,0:T(8,128)(2,1)S(1)}, u32[]{:S(2)}, u32[]{:S(2)}) collective-permute-start(bf16[32,1024]{1,0:T(8,128)(2,1)S(1)} %sum_over_x.1), channel_id=1, source_target_pairs={{0,24},{4,28},{8,16},{12,20},{16,8},{20,12},{24,0},{28,4},{1,25},{... | collective-permute-start | bytes 196616 | tf_op jit(solution)/shard_map/ppermute | solution.py:228
  39.8 0.0 collective-permute-done.12
  39.8 0.5 %collective-permute-done.13 = bf16[32,1024]{1,0:T(8,128)(2,1)S(1)} collective-permute-done((bf16[32,1024]{1,0:T(8,128)(2,1)S(1)}, bf16[32,1024]{1,0:T(8,128)(2,1)S(1)}, u32[]{:S(2)}, u32[]{:S(2)}) %collective-permute-start.13) | collective-permute-done | bytes 65568 | tf_op jit(solution)/shard_map/ppermute | solution.py:228
  40.2 1.8 %collective-permute-done.16 = bf16[32,1024]{1,0:T(8,128)(2,1)S(1)} collective-permute-done((bf16[32,1024]{1,0:T(8,128)(2,1)S(1)}, bf16[32,1024]{1,0:T(8,128)(2,1)S(1)}, u32[]{:S(2)}, u32[]{:S(2)}) %collective-permute-start.16) | collective-permute-done | bytes 65568 | tf_op jit(solution)/shard_map/ppermute | solution.py:228
  42.0 0.7 %fusion = bf16[1,32,1024]{2,1,0:T(8,128)(2,1)} fusion(bf16[32,1024]{1,0:T(8,128)(2,1)S(1)} %collective-permute-done.16, bf16[32,1024]{1,0:T(8,128)(2,1)S(1)} %collective-permute-done.13, bf16[32,1024]{1,0:T(8,128)(2,1)S(1)} %collective-permute-done.12), kind=kLoop, calls=%fused_computation.3 | loop fusion | flops 196608 | bytes 262144 | tf_op jit(solution)/shard_map/broadcast_in_dim | solution.py:237
  (26 shorter events, 0.2 us)
Async XLA Ops:
  0.0 6.4 %slice-start = ((s8[7340032]{0:T(1024)(128)(4,1)}), s8[4194304]{0:T(1024)(128)(4,1)S(1)}, s32[]{:S(2)}) async-start(s8[7340032]{0:T(1024)(128)(4,1)} %bitcast.9), calls=%async_computation | async-start | bytes 8388608
  0.0 6.4 %slice-start.2 = ((s8[7340032]{0:T(1024)(128)(4,1)}), s8[4194304]{0:T(1024)(128)(4,1)S(1)}, s32[]{:S(2)}) async-start(s8[7340032]{0:T(1024)(128)(4,1)} %bitcast.11), calls=%async_computation.2 | async-start | bytes 8388608
  0.0 6.4 %slice-start.1 = ((s8[7340032]{0:T(1024)(128)(4,1)}), s8[3145728]{0:T(1024)(128)(4,1)S(1)}, s32[]{:S(2)}) async-start(s8[7340032]{0:T(1024)(128)(4,1)} %bitcast.9), calls=%async_computation.1 | async-start | bytes 6291456
  0.0 6.4 %slice-start.3 = ((s8[7340032]{0:T(1024)(128)(4,1)}), s8[3145728]{0:T(1024)(128)(4,1)S(1)}, s32[]{:S(2)}) async-start(s8[7340032]{0:T(1024)(128)(4,1)} %bitcast.11), calls=%async_computation.3 | async-start | bytes 6291456
  0.0 6.4 %copy-start = (bf16[1,32,1024]{2,1,0:T(8,128)(2,1)S(1)}, bf16[1,32,1024]{2,1,0:T(8,128)(2,1)}, u32[]{:S(2)}) copy-start(bf16[1,32,1024]{2,1,0:T(8,128)(2,1)} %param.5) | copy-start | bytes 196612
  0.0 5.7 %collective-permute-start = (bf16[32,1024]{1,0:T(8,128)(2,1)}, bf16[32,1024]{1,0:T(8,128)(2,1)S(1)}, u32[]{:S(2)}, u32[]{:S(2)}) collective-permute-start(bf16[32,1024]{1,0:T(8,128)(2,1)} %bitcast.15), channel_id=1, source_target_pairs={{0,4},{4,0},{8,12},{12,8},{1,5},{5,1},{9,13},{13,9},{2,6},{6,2},{1... | collective-permute-start | bytes 196616 | tf_op jit(solution)/shard_map/ppermute | solution.py:27
  3.1 8.2 %collective-permute-start.2 = (bf16[32,1024]{1,0:T(8,128)(2,1)}, bf16[32,1024]{1,0:T(8,128)(2,1)S(1)}, u32[]{:S(2)}, u32[]{:S(2)}) collective-permute-start(bf16[32,1024]{1,0:T(8,128)(2,1)} %bitcast.16), channel_id=1, source_target_pairs={{0,12},{4,8},{8,4},{12,0},{1,13},{5,9},{9,5},{13,1},{2,14},{6,10},... | collective-permute-start | bytes 196616 | tf_op jit(solution)/shard_map/ppermute | solution.py:27
  5.6 6.7 %collective-permute-start.1 = (bf16[32,1024]{1,0:T(8,128)(2,1)}, bf16[32,1024]{1,0:T(8,128)(2,1)S(1)}, u32[]{:S(2)}, u32[]{:S(2)}) collective-permute-start(bf16[32,1024]{1,0:T(8,128)(2,1)} %bitcast.17), channel_id=1, source_target_pairs={{0,8},{4,12},{8,0},{12,4},{1,9},{5,13},{9,1},{13,5},{2,10},{6,14},... | collective-permute-start | bytes 196616 | tf_op jit(solution)/shard_map/ppermute | solution.py:27
  5.7 0.7 %copy-start.1 = (f32[1,1024]{1,0:T(1,128)S(1)}, f32[1,1024]{1,0:T(1,128)}, u32[]{:S(2)}) copy-start(f32[1,1024]{1,0:T(1,128)} %refs_0_.1) | copy-start | bytes 12292
  7.2 2.0 %collective-permute-start.3 = (bf16[64,1920]{1,0:T(8,128)(2,1)S(1)}, bf16[64,1920]{1,0:T(8,128)(2,1)S(1)}, u32[]{:S(2)}, u32[]{:S(2)}) collective-permute-start(bf16[64,1920]{1,0:T(8,128)(2,1)S(1)} %get-tuple-element.26), channel_id=1, source_target_pairs={{0,1},{1,0},{2,3},{3,2},{4,5},{5,4},{6,7},{7,6},{8,9},{9,8},{10,11... | collective-permute-start | bytes 737288 | tf_op jit(solution)/shard_map/ppermute | solution.py:27
  8.7 9.0 %collective-permute-start.5 = (bf16[64,1792]{1,0:T(8,128)(2,1)S(1)}, bf16[64,1792]{1,0:T(8,128)(2,1)S(1)}, u32[]{:S(2)}, u32[]{:S(2)}) collective-permute-start(bf16[64,1792]{1,0:T(8,128)(2,1)S(1)} %get-tuple-element.31), channel_id=1, source_target_pairs={{0,1},{1,0},{2,3},{3,2},{4,5},{5,4},{6,7},{7,6},{8,9},{9,8},{10,11... | collective-permute-start | bytes 688136 | tf_op jit(solution)/shard_map/ppermute | solution.py:27
  9.4 8.3 %collective-permute-start.6 = (bf16[64,1920]{1,0:T(8,128)(2,1)S(1)}, bf16[64,1920]{1,0:T(8,128)(2,1)S(1)}, u32[]{:S(2)}, u32[]{:S(2)}) collective-permute-start(bf16[64,1920]{1,0:T(8,128)(2,1)S(1)} %joined_near.1.refs_5_), channel_id=1, source_target_pairs={{0,2},{1,3},{2,0},{3,1},{4,6},{5,7},{6,4},{7,5},{8,10},{9,11},{10,... | collective-permute-start | bytes 737288 | tf_op jit(solution)/shard_map/ppermute | solution.py:27
  13.0 1.6 %collective-permute-start.4 = (bf16[64,1920]{1,0:T(8,128)(2,1)S(1)}, bf16[64,1920]{1,0:T(8,128)(2,1)S(1)}, u32[]{:S(2)}, u32[]{:S(2)}) collective-permute-start(bf16[64,1920]{1,0:T(8,128)(2,1)S(1)} %get-tuple-element.28.refs_3_), channel_id=1, source_target_pairs={{0,1},{1,0},{2,3},{3,2},{4,5},{5,4},{6,7},{7,6},{8,9},{9,8},{10,11... | collective-permute-start | bytes 737288 | tf_op jit(solution)/shard_map/ppermute | solution.py:27
  13.1 4.6 %slice-start.4 = ((s8[7340032]{0:T(1024)(128)(4,1)}), s8[4194304]{0:T(1024)(128)(4,1)S(1)}, s32[]{:S(2)}) async-start(s8[7340032]{0:T(1024)(128)(4,1)} %bitcast.13), calls=%async_computation.4 | async-start | bytes 8388608
  14.6 3.1 %slice-start.5 = ((s8[7340032]{0:T(1024)(128)(4,1)}), s8[3145728]{0:T(1024)(128)(4,1)S(1)}, s32[]{:S(2)}) async-start(s8[7340032]{0:T(1024)(128)(4,1)} %bitcast.13), calls=%async_computation.5 | async-start | bytes 6291456
  14.8 8.1 %collective-permute-start.10 = (bf16[64,1920]{1,0:T(8,128)(2,1)S(1)}, bf16[64,1920]{1,0:T(8,128)(2,1)S(1)}, u32[]{:S(2)}, u32[]{:S(2)}) collective-permute-start(bf16[64,1920]{1,0:T(8,128)(2,1)S(1)} %joined_far.1.refs_4_), channel_id=1, source_target_pairs={{0,2},{1,3},{2,0},{3,1},{4,6},{5,7},{6,4},{7,5},{8,10},{9,11},{10,... | collective-permute-start | bytes 737288 | tf_op jit(solution)/shard_map/ppermute | solution.py:27
  18.6 1.6 %collective-permute-start.7 = (bf16[2,64,1024]{2,1,0:T(8,128)(2,1)S(1)}, bf16[2,64,1024]{2,1,0:T(8,128)(2,1)S(1)}, u32[]{:S(2)}, u32[]{:S(2)}) collective-permute-start(bf16[2,64,1024]{2,1,0:T(8,128)(2,1)S(1)} %get-tuple-element.34.refs_2_), channel_id=1, source_target_pairs={{0,1},{1,0},{2,3},{3,2},{4,5},{5,4},{6,7},{7,6},{8,9},{9,8},{10,11... | collective-permute-start | bytes 786440 | tf_op jit(solution)/shard_map/ppermute | solution.py:27
  19.4 1.7 %collective-permute-start.9 = (bf16[64,1792]{1,0:T(8,128)(2,1)S(1)}, bf16[64,1792]{1,0:T(8,128)(2,1)S(1)}, u32[]{:S(2)}, u32[]{:S(2)}) collective-permute-start(bf16[64,1792]{1,0:T(8,128)(2,1)S(1)} %get-tuple-element.36), channel_id=1, source_target_pairs={{0,1},{1,0},{2,3},{3,2},{4,5},{5,4},{6,7},{7,6},{8,9},{9,8},{10,11... | collective-permute-start | bytes 688136 | tf_op jit(solution)/shard_map/ppermute | solution.py:27
  23.7 1.6 %collective-permute-start.11 = (bf16[2,64,1024]{2,1,0:T(8,128)(2,1)S(1)}, bf16[2,64,1024]{2,1,0:T(8,128)(2,1)S(1)}, u32[]{:S(2)}, u32[]{:S(2)}) collective-permute-start(bf16[2,64,1024]{2,1,0:T(8,128)(2,1)S(1)} %get-tuple-element.38.refs_2_), channel_id=1, source_target_pairs={{0,1},{1,0},{2,3},{3,2},{4,5},{5,4},{6,7},{7,6},{8,9},{9,8},{10,11... | collective-permute-start | bytes 786440 | tf_op jit(solution)/shard_map/ppermute | solution.py:27
  25.4 5.6 %collective-permute-start.14 = (bf16[2,32,1024]{2,1,0:T(8,128)(2,1)S(1)}, bf16[2,32,1024]{2,1,0:T(8,128)(2,1)S(1)}, u32[]{:S(2)}, u32[]{:S(2)}) collective-permute-start(bf16[2,32,1024]{2,1,0:T(8,128)(2,1)S(1)} %slice.17), channel_id=1, source_target_pairs={{0,4},{4,0},{8,12},{12,8},{1,5},{5,1},{9,13},{13,9},{2,6},{6,2},{1... | collective-permute-start | bytes 393224 | tf_op jit(solution)/shard_map/ppermute | solution.py:27
  27.2 5.6 %collective-permute-start.8 = (bf16[64,1024]{1,0:T(8,128)(2,1)S(1)}, bf16[64,1024]{1,0:T(8,128)(2,1)S(1)}, u32[]{:S(2)}, u32[]{:S(2)}) collective-permute-start(bf16[64,1024]{1,0:T(8,128)(2,1)S(1)} %slice_bitcast_fusion), channel_id=1, source_target_pairs={{0,2},{1,3},{2,0},{3,1},{4,6},{5,7},{6,4},{7,5},{8,10},{9,11},{10,... | collective-permute-start | bytes 393224 | tf_op jit(solution)/shard_map/ppermute | solution.py:27
  31.1 4.8 %collective-permute-start.15 = (bf16[32,1024]{1,0:T(8,128)(2,1)S(1)}, bf16[32,1024]{1,0:T(8,128)(2,1)S(1)}, u32[]{:S(2)}, u32[]{:S(2)}) collective-permute-start(bf16[32,1024]{1,0:T(8,128)(2,1)S(1)} %get-tuple-element.41), channel_id=1, source_target_pairs={{0,2},{1,3},{2,0},{3,1},{4,6},{5,7},{6,4},{7,5},{8,10},{9,11},{10,... | collective-permute-start | bytes 196616 | tf_op jit(solution)/shard_map/ppermute | solution.py:27
  32.8 7.0 %collective-permute-start.12 = (bf16[32,1024]{1,0:T(8,128)(2,1)S(1)}, bf16[32,1024]{1,0:T(8,128)(2,1)S(1)}, u32[]{:S(2)}, u32[]{:S(2)}) collective-permute-start(bf16[32,1024]{1,0:T(8,128)(2,1)S(1)} %get-tuple-element.39), channel_id=1, source_target_pairs={{0,16},{4,20},{8,24},{12,28},{16,0},{20,4},{24,8},{28,12},{1,17},{... | collective-permute-start | bytes 196616 | tf_op jit(solution)/shard_map/ppermute | solution.py:228
  34.3 5.9 %collective-permute-start.13 = (bf16[32,1024]{1,0:T(8,128)(2,1)S(1)}, bf16[32,1024]{1,0:T(8,128)(2,1)S(1)}, u32[]{:S(2)}, u32[]{:S(2)}) collective-permute-start(bf16[32,1024]{1,0:T(8,128)(2,1)S(1)} %get-tuple-element.40), channel_id=1, source_target_pairs={{0,20},{4,16},{8,28},{12,24},{16,4},{20,0},{24,12},{28,8},{1,21},{... | collective-permute-start | bytes 196616 | tf_op jit(solution)/shard_map/ppermute | solution.py:228
  35.9 6.1 %collective-permute-start.16 = (bf16[32,1024]{1,0:T(8,128)(2,1)S(1)}, bf16[32,1024]{1,0:T(8,128)(2,1)S(1)}, u32[]{:S(2)}, u32[]{:S(2)}) collective-permute-start(bf16[32,1024]{1,0:T(8,128)(2,1)S(1)} %sum_over_x.1), channel_id=1, source_target_pairs={{0,24},{4,28},{8,16},{12,20},{16,8},{20,12},{24,0},{28,4},{1,25},{... | collective-permute-start | bytes 196616 | tf_op jit(solution)/shard_map/ppermute | solution.py:228
